TPU v7x, 32 devices: a whole 2x2x4 slice. The times are simulated.
32 devices in a mesh: seq: 16 (over z, y, x), head: 2 (over core).
Axes of the slice: x: 2, y: 2, z: 4, core: 2. Of those that a mesh axis runs over, the one named last changes fastest.
Arguments:
- events: bfloat16 [4096, 1024], P('seq'), may hold values from -6 to 6
- w_uvqk: bfloat16 [1024, 4, 1024], P('seq', None, 'head'), may hold values from -0.1875 to 0.1875
- w_out: bfloat16 [1024, 1024], P('head', 'seq'), may hold values from -0.1875 to 0.1875
- time_bias: bfloat16 [8, 128], P('head'), may hold values from -4 to 4
- stamps: int32 [4096], P('seq'), may hold values from 0 to 127, as said below
Outputs:
- mixed: bfloat16 [4096, 1024], P('seq', 'head')
Inputs may be any that keep to these rules, and one draw needn't show every extreme that they name: stamps never fall along the events; the first is 0 and the last is 127.
All inputs are finite; a program needn't handle non-finite values.
Results may differ from a plain program's by a relative error of at most 0.0075.
Values may be sent and summed in bfloat16 or wider, within the bound.
No kernel may reach another device: no remote copies, remote signals or barrier semaphores. Data moves between devices by JAX's collectives and lax.ppermute only.
A program may use at most 128 MiB of HBM per device.

v0:
```python
import math

import jax
import jax.numpy as jnp
from jax import lax
from jax.sharding import PartitionSpec as P

EPSILON = 1e-05


def layer_norm(inputs):
    centre = inputs - jnp.mean(inputs, axis=-1, keepdims=True)
    spread = jnp.mean(centre * centre, axis=-1, keepdims=True)
    return centre * lax.rsqrt(spread + EPSILON)


def bucket_matrix(time_bias):
    buckets = time_bias.shape[1]
    levels = jnp.arange(buckets, dtype=jnp.int32)
    pattern = (levels[:, None, None] - levels[None, :, None] == levels[None, None, :]).astype(
        jnp.bfloat16
    )
    return jnp.einsum("hd,abd->hab", time_bias, pattern, preferred_element_type=jnp.float32).astype(
        jnp.bfloat16
    )


def query_side(queries, query_stamps, matrix, head_count):
    buckets = matrix.shape[1]
    levels = jnp.arange(buckets, dtype=jnp.int32)
    onehot = (query_stamps[:, None] == levels[None, :]).astype(jnp.bfloat16)
    stamp_bias = jnp.einsum(
        "ra,hab->hrb", onehot, matrix, preferred_element_type=jnp.float32
    ).astype(jnp.bfloat16)
    return (queries.reshape(queries.shape[0], head_count, -1), stamp_bias)


def attend_piece(
    total, query_heads, stamp_bias, query_start, keys, values, key_stamps, key_start, scale
):
    query_count, head_count, head_size = query_heads.shape
    key_count = keys.shape[0]
    buckets = stamp_bias.shape[2]
    key_heads = keys.reshape(key_count, head_count, head_size)
    value_heads = values.reshape(key_count, head_count, head_size)
    levels = jnp.arange(buckets, dtype=jnp.int32)
    key_onehot = (key_stamps[:, None] == levels[None, :]).astype(jnp.bfloat16)
    scores = (
        jnp.einsum("rhd,khd->hrk", query_heads, key_heads, preferred_element_type=jnp.float32)
        * scale
    )
    scores = scores + jnp.einsum(
        "hrb,kb->hrk", stamp_bias, key_onehot, preferred_element_type=jnp.float32
    )
    query_pos = query_start + jnp.arange(query_count, dtype=jnp.int32)
    key_pos = key_start + jnp.arange(key_count, dtype=jnp.int32)
    allowed = key_pos[None, :] <= query_pos[:, None]
    weights = jnp.where(allowed[None], jax.nn.silu(scores), 0.0).astype(jnp.bfloat16)
    update = jnp.einsum("hrk,khd->rhd", weights, value_heads, preferred_element_type=jnp.float32)
    return total + update.reshape(total.shape)


def fold_blocks(total, query_heads, stamp_bias, query_start, piece, shard_rows, scale):
    keys, values, key_stamps = piece
    key_count = keys.shape[0]
    step = math.gcd(key_count, max(512, shard_rows))
    last = query_start + query_heads.shape[0] - 1

    def visit(turn, carried):
        offset = turn * step

        def work(inner):
            return attend_piece(
                inner,
                query_heads,
                stamp_bias,
                query_start,
                lax.dynamic_slice_in_dim(keys, offset, step, 0),
                lax.dynamic_slice_in_dim(values, offset, step, 0),
                lax.dynamic_slice_in_dim(key_stamps, offset, step, 0),
                offset,
                scale,
            )

        def keep_total(inner):
            return inner

        return lax.cond(offset <= last, work, keep_total, carried)

    return lax.fori_loop(0, key_count // step, visit, total)


def per_device(events, w_uvqk, w_out, time_bias, stamps):
    shard_rows = events.shape[0]
    inputs = events.astype(jnp.float32)
    normed = layer_norm(inputs).astype(jnp.bfloat16)
    local_width = w_uvqk.shape[2]
    head_count = time_bias.shape[0]
    head_size = local_width // head_count
    scale = 1.0 / math.sqrt(head_size)
    projected = jnp.einsum(
        "td,dcf->tcf",
        normed,
        lax.all_gather(w_uvqk, "seq", axis=0, tiled=True),
        preferred_element_type=jnp.float32,
    )
    activated = jax.nn.silu(projected).astype(jnp.bfloat16)
    gate_u = activated[:, 0]
    values = activated[:, 1]
    queries = activated[:, 2]
    keys = activated[:, 3]
    matrix = bucket_matrix(time_bias)
    device = lax.axis_index("seq")
    own_start = device * shard_rows
    own_heads, own_bias = query_side(queries, stamps, matrix, head_count)
    attended = fold_blocks(
        jnp.zeros((shard_rows, local_width), jnp.float32),
        own_heads,
        own_bias,
        own_start,
        (
            lax.all_gather(keys, "seq", axis=0, tiled=True),
            lax.all_gather(values, "seq", axis=0, tiled=True),
            lax.all_gather(stamps, "seq", axis=0, tiled=True),
        ),
        shard_rows,
        scale,
    ).astype(jnp.bfloat16)
    attended_f = attended.astype(jnp.float32)
    full_width = local_width * lax.axis_size("head")
    middle = lax.psum(jnp.sum(attended_f, axis=-1), "head") / full_width
    centre = attended_f - middle[:, None]
    spread = lax.psum(jnp.sum(centre * centre, axis=-1), "head") / full_width
    normed_out = centre * lax.rsqrt(spread + EPSILON)[:, None]
    gated = (normed_out * gate_u.astype(jnp.float32)).astype(jnp.bfloat16)
    share = inputs.shape[1] // lax.axis_size("head")
    gated_full = lax.all_gather(gated, "head", axis=1, tiled=True)
    rows_full = lax.all_gather(w_out, "head", axis=0, tiled=True)
    whole = jnp.dot(
        gated_full,
        lax.all_gather(rows_full, "seq", axis=1, tiled=True),
        preferred_element_type=jnp.float32,
    )
    summed = lax.dynamic_slice_in_dim(whole, lax.axis_index("head") * share, share, 1)
    residual = lax.dynamic_slice_in_dim(inputs, lax.axis_index("head") * share, share, 1)
    return (residual + summed).astype(jnp.bfloat16)


def solution(mesh):
    placed = (P("seq", None), P("seq", None, "head"), P("head", "seq"), P("head", None), P("seq"))
    return jax.shard_map(
        per_device, mesh=mesh, in_specs=placed, out_specs=P("seq", "head"), check_vma=False
    )
```

profile of v0, /device:TPU:0, one launch (start us, length us, event | category | flops | bytes accessed | tf_op | source)
XLA Modules:
  0.0 318.3 jit_solution(1630814035086973915)
XLA Ops:
  6.5 0.0 copy-start
  6.5 0.0 all-gather.8.cloned.1.call-start
  6.5 1.7 copy.22
  8.2 0.0 all-gather.8.cloned.1.call-update
  8.3 0.0 all-gather.12.cloned.1.call-start
  8.3 1.2 convert_reduce_fusion
  9.5 1.3 multiply_reduce_fusion
  10.9 77.9 %all-gather.8.cloned.1.call-done = bf16[1024,4,512]{2,0,1:T(8,128)(2,1)} async-done(((bf16[64,4,512]{2,0,1:T(8,128)(2,1)}), bf16[1024,4,512]{2,0,1:T(8,128)(2,1)}) %all-gather.8.cloned.1.call-update) | async-done | bytes 4194320 | tf_op jit(solution)/shard_map/all_gather | solution.py:104
  88.8 3.8 %multiply_convert_fusion = bf16[256,4,512]{2,0,1:T(8,128)(2,1)S(1)} fusion(bf16[1024,4,512]{2,0,1:T(8,128)(2,1)} %all-gather.8.cloned.1.call-done, bf16[256,1024]{1,0:T(8,128)(2,1)} %param.9, f32[256]{0:T(256)S(1)} %add_rsqrt_fusion.1, f32[256]{0:T(256)S(1)} %broadcast_multiply_fusion.1), kind=kOutput, calls=%fused_computation.22 | convolution fusion | flops 1077411840 | bytes 5769216 | tf_op jit(solution)/shard_map/td,dcf->tcf/dot_general | solution.py:101
  92.6 0.0 copy-start.3
  92.6 1.0 copy-done.3
  93.6 0.0 copy-start.4
  93.6 0.0 copy-start.1
  93.6 0.8 fusion.32
  94.4 0.0 all-gather.12.cloned.1.call-update
  94.5 0.0 all-gather.14.cloned.1.call-start
  94.5 0.7 all-gather.14.cloned.1.call-update
  95.2 0.0 copy-start.5
  95.2 0.0 all-gather.10.cloned.1.call-start
  95.3 0.0 copy-done.4
  95.3 2.0 all_gather.26
  97.3 0.0 all-gather.10.cloned.1.call-update
  97.3 0.0 copy-done.1
  97.3 1.1 convert_element_type.52
  98.5 0.0 copy-done
  98.5 3.7 %fusion.17 = bf16[4,128,128]{2,0,1:T(4,128)(2,1)S(1)} fusion(s32[128,128]{1,0:T(8,128)S(1)} %iota_subtract_fusion, bf16[4,128]{1,0:T(4,128)(2,1)S(1)} %copy-done), kind=kOutput, calls=%fused_computation.26 | convolution fusion | flops 18939904 | bytes 197632 | tf_op jit(solution)/shard_map/hd,abd->hab/dot_general | solution.py:23
  102.1 0.0 copy-done.5
  102.2 0.3 fusion.15
  102.5 0.8 copy.27
  103.3 40.8 %all-gather.2 = s32[16,1,256]{2,1,0:T(1,128)} all-gather(s32[1,1,256]{2,1,0:T(1,128)S(1)} %bitcast.57), channel_id=1, replica_groups=mesh['seq'=16,'head'=2] {'seq'}, dimensions={0}, use_global_device_ids=true | all-gather | bytes 17408 | tf_op jit(solution)/shard_map/all_gather | solution.py:124
  144.1 0.1 reshape_squeeze.3
  144.2 24.9 %all-gather.12.cloned.1.call-done = bf16[4096,1,512]{2,0,1:T(8,128)(2,1)} async-done(((bf16[256,1,512]{2,0,1:T(8,128)(2,1)}), bf16[4096,1,512]{2,0,1:T(8,128)(2,1)}) %all-gather.12.cloned.1.call-update) | async-done | bytes 4194320 | tf_op jit(solution)/shard_map/all_gather | solution.py:123
  169.2 6.4 %copy.24 = bf16[4096,512]{0,1:T(8,128)(2,1)} copy(bf16[4096,512]{1,0:T(8,128)(2,1)} %bitcast.55) | data formatting | bytes 8388608 | tf_op jit(solution)/shard_map/while | solution.py:90
  175.6 71.1 %all-gather.14.cloned.1.call-done = bf16[4096,1,512]{2,0,1:T(8,128)(2,1)} async-done(((bf16[256,1,512]{2,0,1:T(8,128)(2,1)}), bf16[4096,1,512]{2,0,1:T(8,128)(2,1)}) %all-gather.14.cloned.1.call-update) | async-done | bytes 4194320 | tf_op jit(solution)/shard_map/all_gather | solution.py:122
  246.7 6.4 %copy.25 = bf16[4096,512]{0,1:T(8,128)(2,1)} copy(bf16[4096,512]{1,0:T(8,128)(2,1)} %bitcast.56) | data formatting | bytes 8388608 | tf_op jit(solution)/shard_map/while | solution.py:90
  253.1 7.1 %while.16 = (s32[]{:T(128)}, f32[256,512]{0,1:T(8,128)S(1)}, s32[]{:T(128)}, bf16[4096,512]{0,1:T(8,128)(2,1)}, s32[]{:T(128)}, /*index=5*/bf16[4096,512]{0,1:T(...) while((s32[]{:T(128)}, f32[256,512]{0,1:T(8,128)S(1)}, ...), condition=%wide.region_5.6_spmd, body=%wide.region_2.5_spmd.sunk | while | flops 407175936 | bytes 10236161 | solution.py:90
  253.1 6.7 %conditional.2 = (f32[256,512]{0,1:T(8,128)S(1)}) conditional(s32[]{:T(128)} %convert_element_type.104, f32[256,512]{0,1:T(8,128)S(1)} %get-tuple-element.309, (s32[]{:T(128)}, bf16[4096,512]{0,1:T(8,128)(2,1)}, s32[]{:T(128)}, bf16[4096,512]{0,1:T(8,128)(2,1)}, bf16[256,4,128]{2,0,1:T(8,128)(2,1)S(1)}, /*index=5*/s32[4096]{0:T(1024)}, ...), branch_computations={%region_3.3_spmd, %region_4.4_spmd} | conditional | flops 407175936 | bytes 10235962 | solution.py:88
  253.1 1.3 constant_dynamic-slice_fusion
  254.4 0.5 fusion.33
  254.9 0.8 dynamic_slice.12
  255.6 0.1 broadcast_compare_fusion
  255.8 2.9 fusion
  258.7 1.2 bitcast_add_fusion.1
  260.1 0.1 copy.28
  260.3 0.1 convert_reduce_fusion.1
  260.4 2.5 psum.14
  262.9 0.2 fusion.20
  263.1 2.5 psum.15
  265.6 1.2 fusion.22
  266.7 0.0 copy-start.2
  266.7 2.3 all_gather.25
  269.0 39.6 %all-gather.10.cloned.1.call-done = bf16[1024,1024]{0,1:T(8,128)(2,1)} async-done(((bf16[1024,64]{0,1:T(8,128)(2,1)}), bf16[1024,1024]{0,1:T(8,128)(2,1)}) %all-gather.10.cloned.1.call-update) | async-done | bytes 2097168 | tf_op jit(solution)/shard_map/all_gather | solution.py:141
  308.6 2.3 fusion.34
  311.0 0.0 copy-done.2
  311.0 0.8 add_convert_fusion
  (16 shorter events, 0.2 us)
Async XLA Ops:
  6.5 91.9 %copy-start = (bf16[4,128]{1,0:T(4,128)(2,1)S(1)}, bf16[4,128]{1,0:T(4,128)(2,1)}, u32[]{:S(2)}) copy-start(bf16[4,128]{1,0:T(4,128)(2,1)} %param.12) | copy-start | bytes 3076
  6.5 82.3 %all-gather.8.cloned.1.call-start = ((), (), s32[]{:S(2)}) async-start(), calls=%async_computation | async-start | bytes 4456448 | tf_op jit(solution)/shard_map/all_gather | solution.py:104
  8.3 160.9 %all-gather.12.cloned.1.call-start = ((), (), s32[]{:S(2)}) async-start(), calls=%async_computation.2 | async-start | bytes 4456448 | tf_op jit(solution)/shard_map/all_gather | solution.py:123
  92.6 1.0 copy-start.3
  93.6 1.7 copy-start.4
  93.6 3.7 %copy-start.1 = (bf16[256,1024]{1,0:T(8,128)(2,1)S(1)}, bf16[256,1024]{1,0:T(8,128)(2,1)}, u32[]{:S(2)}) copy-start(bf16[256,1024]{1,0:T(8,128)(2,1)} %param.9) | copy-start | bytes 1572868
  94.5 152.2 %all-gather.14.cloned.1.call-start = ((), (), s32[]{:S(2)}) async-start(), calls=%async_computation.3 | async-start | bytes 4456448 | tf_op jit(solution)/shard_map/all_gather | solution.py:122
  95.2 7.0 %copy-start.5 = (s32[256]{0:T(256)S(1)}, s32[256]{0:T(256)}, u32[]{:S(2)}) copy-start(s32[256]{0:T(256)} %param.13) | copy-start | bytes 3076
  95.2 213.4 %all-gather.10.cloned.1.call-start = ((), (), s32[]{:S(2)}) async-start(), calls=%async_computation.1 | async-start | bytes 2228224 | tf_op jit(solution)/shard_map/all_gather | solution.py:141
  266.7 44.2 %copy-start.2 = (f32[256,1024]{1,0:T(8,128)S(1)}, f32[256,1024]{1,0:T(8,128)}, u32[]{:S(2)}) copy-start(f32[256,1024]{1,0:T(8,128)} %convert_element_type.52) | copy-start | bytes 3145732
Sparse Core Ops, SparseCore 0:
  10.1 78.6 all-gather.7
  94.6 74.5 all-gather.11
  171.9 74.6 all-gather.13
  249.3 59.2 all-gather.9
where the time goes:
time: 325 us; the launch traced here: 318 us
  waiting for transfers between devices  214 us (66%)
  blocking collectives  50.1 us (15%)
  local copies, waits for them, and re-layouts  19.5 us (6%)
  matrix products  13.5 us (4%)
  between operations  13.3 us (4%)
  other arithmetic  7.23 us (2%)
    all_gather x1, waiting for transfers between devices, per_device(): lax.all_gather(w_uvqk, 'seq', axis=0, tiled=True)  77.9 us
    all_gather x1, waiting for transfers between devices, per_device(): lax.all_gather(keys, 'seq', axis=0, tiled=True)  71.1 us
    all_gather x1, blocking collectives, per_device(): lax.all_gather(stamps, 'seq', axis=0, tiled=True)  40.8 us
    all_gather x1, waiting for transfers between devices, per_device(): lax.all_gather(rows_full, 'seq', axis=1, tiled=True)  39.6 us
    all_gather x1, waiting for transfers between devices, per_device(): lax.all_gather(values, 'seq', axis=0, tiled=True)  24.9 us
    while x5, local copies, waits for them, and re-layouts, fold_blocks(): return lax.fori_loop(0, key_count // step, visit, total)  13.8 us
  transfers between devices with their start and end apart: 4, of which 4 were waited for; matrix products, arithmetic and copies ran while one was open for 9% of the time, Pallas kernels for 0%

commit v1 on v0

v1 whole, which is shorter than its diff:
```python
import functools
import math

import jax
import jax.numpy as jnp
from jax import lax
from jax.experimental import pallas as pl
from jax.experimental.pallas import tpu as pltpu
from jax.sharding import PartitionSpec as P

EPSILON = 1e-05
PAD = 16
VMEM_LIMIT = 50 * 1024 * 1024
NT = (((1,), (1,)), ((), ()))


def half_silu(t):
    return t * (1.0 + jnp.tanh(t))


def normalise(x):
    centre = x - jnp.mean(x, axis=-1, keepdims=True)
    spread = jnp.mean(centre * centre, axis=-1, keepdims=True)
    return centre * lax.rsqrt(spread + EPSILON)


def onehot_rows(stamp_row, buckets):
    count = stamp_row.shape[1]
    level = lax.broadcasted_iota(jnp.int32, (buckets, count), 0).astype(jnp.float32)
    return jnp.where(level == stamp_row, 1.0, 0.0).T


def vmem(count):
    return [pl.BlockSpec(memory_space=pltpu.VMEM)] * count


def projection_kernel(lead, lines, ids, events, *refs):
    arrived = refs[: lead - 1]
    other, bias_row, own_msg = refs[lead - 1 : lead + 2]
    marks = refs[lead + 2 : 2 * lead + 1]
    weights = refs[2 * lead + 1 : 2 * lead + 1 + lines]
    kv_ref, q_ref, u_ref, wbuf, xbuf = refs[2 * lead + 1 + lines :]
    a, i, c = ids[0], ids[1], ids[2]
    rows, _ = events.shape
    half = rows // 2
    size = u_ref.shape[1]
    buckets = bias_row.shape[1]
    chunk = wbuf.shape[0] // (lead * lines)
    for j in range(lines):
        for k in range(lead):
            place = ((a ^ k) * lines + (i ^ j)) * chunk
            wbuf[pl.ds(pl.multiple_of(place, chunk), chunk), :] = weights[j][
                k * chunk : (k + 1) * chunk, :
            ]
    table = jnp.broadcast_to(bias_row[...], (buckets, buckets))
    table = pltpu.roll(table, 0, 1, stride=1, stride_axis=0).astype(jnp.bfloat16)
    scale = 0.5 / math.sqrt(size)
    stamp_rows = lax.broadcasted_iota(jnp.int32, (PAD, rows), 0)
    stamp_tile = jnp.zeros((PAD, rows), jnp.float32)
    for k in range(lead):
        if k == 0:
            x = events[...].astype(jnp.float32)
            mark = own_msg[chunk : chunk + PAD, :rows]
        else:
            xbuf[pl.ds(pl.multiple_of(c * half, half), half), :] = arrived[k - 1][...]
            xbuf[pl.ds(pl.multiple_of((1 - c) * half, half), half), :] = other[
                (k - 1) * half : k * half, :
            ]
            x = xbuf[...].astype(jnp.float32)
            mark = marks[k - 1][chunk : chunk + PAD, :rows]
        mark = mark.astype(jnp.float32)[0:1, :]
        normed = normalise(x).astype(jnp.bfloat16)
        product = jnp.dot(normed, wbuf[...], preferred_element_type=jnp.float32)
        active = half_silu(0.5 * product)
        base = pl.ds(pl.multiple_of((a ^ k) * rows, rows), rows)
        u_ref[base, :] = active[:, :size].astype(jnp.bfloat16)
        kv_ref[base, size : 2 * size] = active[:, size : 2 * size].astype(jnp.bfloat16)
        q_ref[base, :size] = (active[:, 2 * size : 3 * size] * scale).astype(jnp.bfloat16)
        kv_ref[base, :size] = active[:, 3 * size :].astype(jnp.bfloat16)
        chosen = onehot_rows(mark, buckets).astype(jnp.bfloat16)
        q_ref[base, size:] = jnp.dot(
            chosen, table, preferred_element_type=jnp.float32
        ).astype(jnp.bfloat16)
        stamp_tile = jnp.where(stamp_rows == (a ^ k), mark, stamp_tile)
    kv_ref[lead * rows :, :] = stamp_tile.astype(jnp.bfloat16)


def attention_kernel(lead, j, last, ids, q_ref, kv_ref, *refs):
    refs = list(refs)
    before = refs.pop(0) if j > 0 else None
    u_ref = refs.pop(0) if last else None
    outs, (kaug, total) = refs[:-2], refs[-2:]
    a, i = ids[0], ids[1]
    size = q_ref.shape[1] // 2
    rows = q_ref.shape[0] // lead
    buckets = q_ref.shape[1] - size
    kaug[:, :size] = kv_ref[: lead * rows, :size]
    marks = kv_ref[lead * rows :, :].astype(jnp.float32)
    for p in range(lead):
        kaug[p * rows : (p + 1) * rows, size:] = onehot_rows(marks[p : p + 1, :], buckets).astype(
            jnp.bfloat16
        )

    def visit(extra):
        for p in range(lead):
            block = slice(p * rows, (p + 1) * rows)
            count = (p + extra) * rows
            old = before[block, :] if before is not None else None
            if count == 0:
                total[block, :] = old if old is not None else jnp.zeros((rows, size), jnp.float32)
                continue
            t = lax.dot_general(
                q_ref[block, :], kaug[:count, :], NT, preferred_element_type=jnp.float32
            )
            weight = half_silu(t)
            if j == 0:
                row = lax.broadcasted_iota(jnp.int32, (rows, count), 0) + p * rows
                column = lax.broadcasted_iota(jnp.int32, (rows, count), 1)
                weight = jnp.where(column <= row, weight, 0.0)
            update = jnp.dot(
                weight.astype(jnp.bfloat16),
                kv_ref[:count, size:],
                preferred_element_type=jnp.float32,
            )
            total[block, :] = update if old is None else old + update

    if j == 0:
        visit(1)
    else:
        pl.when((i ^ j) < i)(lambda: visit(1))
        pl.when((i ^ j) > i)(lambda: visit(0))
    if last:
        for k in range(lead):
            base = pl.ds(pl.multiple_of((a ^ k) * rows, rows), rows)
            outs[k][:, :size] = total[base, :].astype(jnp.bfloat16)
            outs[k][:, size:] = u_ref[base, :]
    else:
        outs[0][...] = total[...]


def output_kernel(lead, lines, ids, events, kept, given, *refs):
    own = refs[:lead]
    other = refs[lead : 2 * lead]
    out_ref, gated, wbuf = refs[2 * lead :]
    a, i, c = ids[0], ids[1], ids[2]
    rows, share = out_ref.shape
    size = own[0].shape[1] // 2
    full = 2 * lead * size
    chunk = kept.shape[0] // (2 * lines)
    for k in range(2):
        for j in range(lines):
            place = (((a ^ k) & 1) * lines + (i ^ j)) * chunk
            source = slice((k * lines + j) * chunk, (k * lines + j + 1) * chunk)
            to = pl.ds(pl.multiple_of(place, chunk), chunk)
            wbuf[0, to, :] = kept[source, :]
            wbuf[1, to, :] = given[source, :]
    parts = [ref[:, :size].astype(jnp.float32) for ref in (*own, *other)]
    middle = functools.reduce(jnp.add, [jnp.sum(x, -1, keepdims=True) for x in parts]) / full
    parts = [x - middle for x in parts]
    spread = functools.reduce(jnp.add, [jnp.sum(x * x, -1, keepdims=True) for x in parts]) / full
    inverse = lax.rsqrt(spread + EPSILON)
    for side, group in enumerate((own, other)):
        for k in range(lead):
            value = parts[side * lead + k] * inverse * group[k][:, size:].astype(jnp.float32)
            place = pl.ds(pl.multiple_of((a ^ k) * size, size), size)
            gated[side, :, place] = value.astype(jnp.bfloat16)
    total = lax.dot_general(gated[0], wbuf[0], NT, preferred_element_type=jnp.float32)
    total += lax.dot_general(gated[1], wbuf[1], NT, preferred_element_type=jnp.float32)
    residual = events[:, pl.ds(pl.multiple_of(c * share, share), share)].astype(jnp.float32)
    out_ref[...] = (residual + total).astype(jnp.bfloat16)


def call(kernel, ins, outs, scratch, flops, transcendentals=0):
    size = sum(math.prod(x.shape) * x.dtype.itemsize for x in [*ins, *outs])
    return pl.pallas_call(
        kernel,
        out_shape=outs,
        in_specs=[pl.BlockSpec(memory_space=pltpu.SMEM)] + vmem(len(ins) - 1),
        out_specs=vmem(len(outs)),
        scratch_shapes=scratch,
        compiler_params=pltpu.CompilerParams(vmem_limit_bytes=VMEM_LIMIT),
        cost_estimate=pl.CostEstimate(
            flops=flops, bytes_accessed=size, transcendentals=transcendentals
        ),
    )(*ins)


def per_device(events, w_uvqk, w_out, time_bias, stamps):
    bf16, f32 = jnp.bfloat16, jnp.float32
    devices = lax.axis_size("seq")
    rows, width = events.shape
    lead = time_bias.shape[0]
    lines = devices // lead
    chunk = w_uvqk.shape[0]
    size = w_uvqk.shape[2] // lead
    share = width // lax.axis_size("head")
    half = rows // 2
    place, c = lax.axis_index("seq"), lax.axis_index("head")
    a, i = place // lines, place % lines
    ids = jnp.stack([a, i, c]).astype(jnp.int32)

    def exchange(x, flip):
        return lax.ppermute(x, "seq", [(t, t ^ flip) for t in range(devices)])

    def swap(x):
        return lax.ppermute(x, "head", [(0, 1), (1, 0)])

    def shape(*dims, dtype=bf16):
        return jax.ShapeDtypeStruct(dims, dtype)

    by_head = w_uvqk.reshape(chunk, 4, lead, size).transpose(2, 0, 1, 3).reshape(lead, chunk, -1)
    stamp_rows = jnp.pad(stamps.astype(bf16)[None, :], ((0, PAD - 1), (0, 4 * size - rows)))
    sent = [
        jnp.concatenate([lax.dynamic_index_in_dim(by_head, a ^ k, 0, False), stamp_rows])
        for k in range(lead)
    ]
    got = [exchange(sent[k], k * lines) for k in range(1, lead)]
    own_half = lax.dynamic_slice_in_dim(events, c * half, half, 0)
    arrived = [exchange(own_half, k * lines) for k in range(1, lead)]
    w_out_t = w_out.T
    stack = jnp.concatenate([x[:chunk] for x in [sent[0], *got]] + [w_out_t])
    stacks = [stack] + [exchange(stack, j) for j in range(1, lines)]
    other = swap(jnp.concatenate(arrived))
    bias_row = lax.dynamic_index_in_dim(time_bias, a, 0, True).astype(f32) * 0.5
    bias_row = jnp.roll(bias_row[:, ::-1], 1, axis=1)

    span = lead * rows
    kv, queries, gate = call(
        functools.partial(projection_kernel, lead, lines),
        [ids, events, *arrived, other, bias_row, sent[0], *got, *stacks],
        [shape(span + PAD, 2 * size), shape(span, size + bias_row.shape[1]), shape(span, size)],
        [pltpu.VMEM((width, 4 * size), bf16), pltpu.VMEM((rows, width), bf16)],
        2 * span * width * 4 * size,
        span * 4 * size,
    )
    kvs = [kv] + [exchange(kv, j) for j in range(1, lines)]

    columns = jnp.concatenate([x[lead * chunk :] for x in stacks])
    shares = [columns] + [exchange(columns, k * lines) for k in range(1, lead)]
    low, high = jnp.concatenate(shares[: lead // 2]), jnp.concatenate(shares[lead // 2 :])
    mine = (a // (lead // 2)) == c
    kept = jnp.where(mine, low, high)
    given = swap(jnp.where(mine, high, low))

    total = None
    for j in range(lines):
        last = j == lines - 1
        ins = [ids, queries, kvs[j]] + ([total] if j else []) + ([gate] if last else [])
        outs = [shape(rows, 2 * size)] * lead if last else [shape(span, size, dtype=f32)]
        result = call(
            functools.partial(attention_kernel, lead, j, last),
            ins,
            outs,
            [pltpu.VMEM((span, queries.shape[1]), bf16), pltpu.VMEM((span, size), f32)],
            span * span * 3 * size,
            span * span // 2,
        )
        total = result[0]
    own = [result[0]] + [exchange(result[k], k * lines) for k in range(1, lead)]
    across = [swap(x) for x in own]
    return call(
        functools.partial(output_kernel, lead, lines),
        [ids, events, kept, given, *own, *across],
        [shape(rows, share)],
        [
            pltpu.VMEM((2, rows, lead * size), bf16),
            pltpu.VMEM((2, share, lead * size), bf16),
        ],
        2 * rows * width * share,
    )[0]


def solution(mesh):
    placed = (P("seq", None), P("seq", None, "head"), P("head", "seq"), P("head", None), P("seq"))
    return jax.shard_map(
        per_device, mesh=mesh, in_specs=placed, out_specs=P("seq", "head"), check_vma=False
    )
```

time: 325 us -> 118 us (0.36); the launches traced: 318 us -> 118 us
  waiting for transfers between devices: 214 us -> 68.4 us
  blocking collectives: 50.1 us -> 0 us
  starting transfers between devices: 0.12 us -> 27.5 us
  local copies, waits for them, and re-layouts: 19.5 us -> 5.58 us
  matrix products: 13.5 us -> 0 us
  Pallas kernels: 0 us -> 13.2 us
  between operations: 13.3 us -> 0.3 us
  other arithmetic: 7.23 us -> 2.58 us
    all_gather x4 -> x0, waiting for transfers between devices: 214 us -> none  [the longest x1 77.9 us: per_device(): lax.all_gather(w_uvqk, 'seq', axis=0, tiled=True)]
    ppermute x0 -> x24, waiting for transfers between devices: none -> 68.4 us  [the longest x18 67 us: exchange(): return lax.ppermute(x, 'seq', [(t, t ^ flip) for t in range(devices)])]
    all_gather x3 -> x0, blocking collectives: 45.1 us -> none  [the longest x1 40.8 us: per_device(): lax.all_gather(stamps, 'seq', axis=0, tiled=True)]
    ppermute x0 -> x24, starting transfers between devices: none -> 27.5 us  [the longest x18 26.9 us: exchange(): return lax.ppermute(x, 'seq', [(t, t ^ flip) for t in range(devices)])]
    while x5 -> x0, local copies, waits for them, and re-layouts: 13.8 us -> none  [fold_blocks(): return lax.fori_loop(0, key_count // step, visit, total)]
    dot_general x6 -> x0, matrix products: 13.5 us -> none  [the longest x1 3.77 us: per_device(): jnp.einsum('td,dcf->tcf', normed, lax.all_gather(w_uvqk, 'seq', axis=0, t...]
    pallas_call x0 -> x6, Pallas kernels: none -> 13.2 us  [call(): pl.pallas_call(kernel, out_shape=outs, in_specs=[pl.BlockSpec(memory_spac...]
    psum x2 -> x0, blocking collectives: 4.94 us -> none  [the longest x1 2.47 us: per_device(): middle = lax.psum(jnp.sum(attended_f, axis=-1), 'head') / full_width]
  transfers between devices with their start and end apart: 4 -> 24, of which waited for: 4 -> 9; matrix products, arithmetic and copies ran while one was open for 9% -> 5% of each run, Pallas kernels for 0% -> 9%
where the time goes in v1:
time: 118 us
  waiting for transfers between devices  68.4 us (58%)
  starting transfers between devices  27.5 us (23%)
  Pallas kernels  13.2 us (11%)
  local copies, waits for them, and re-layouts  5.58 us (5%)
  other arithmetic  2.58 us (2%)
    ppermute x18, waiting for transfers between devices, exchange(): return lax.ppermute(x, 'seq', [(t, t ^ flip) for t in range(devices)])  67 us
    ppermute x18, starting transfers between devices, exchange(): return lax.ppermute(x, 'seq', [(t, t ^ flip) for t in range(devices)])  26.9 us
    pallas_call x6, Pallas kernels, call(): pl.pallas_call(kernel, out_shape=outs, in_specs=[pl.BlockSpec(memory_spac...  13.2 us
  transfers between devices with their start and end apart: 24, of which 9 were waited for; matrix products, arithmetic and copies ran while one was open for 5% of the time, Pallas kernels for 9%

profile of v1, /device:TPU:0, one launch (start us, length us, event | category | flops | bytes accessed | tf_op | source)
XLA Modules:
  0.0 117.5 jit_solution(9150407568572234370)
XLA Ops:
  0.0 1.1 reshape.6
  1.1 0.1 copy.6
  1.2 0.0 copy-start
  1.2 0.1 reshape.7
  1.4 0.0 copy-start.2
  1.4 0.0 copy-start.4
  1.5 3.1 %collective-permute-start = (bf16[80,512]{1,0:T(8,128)(2,1)S(1)}, bf16[80,512]{1,0:T(8,128)(2,1)S(1)}, u32[]{:S(2)}, u32[]{:S(2)}) collective-permute-start(bf16[80,512]{1,0:T(8,128)(2,1)S(1)} %get-tuple-element.35), channel_id=1, source_target_pairs={{0,8},{2,10},{4,12},{6,14},{8,0},{10,2},{12,4},{14,6},{16,24},{18,... | collective-permute-start | bytes 245768 | tf_op jit(solution)/shard_map/ppermute | solution.py:203
  4.6 0.7 constant_dynamic-slice_fusion.1
  5.3 0.7 collective-permute-start.10
  6.0 2.6 %collective-permute-start.11 = (bf16[128,1024]{1,0:T(8,128)(2,1)}, bf16[128,1024]{1,0:T(8,128)(2,1)S(1)}, u32[]{:S(2)}, u32[]{:S(2)}) collective-permute-start(bf16[128,1024]{1,0:T(8,128)(2,1)} %constant_dynamic-slice_fusion.1), channel_id=1, source_target_pairs={{0,16},{2,18},{4,20},{6,22},{8,24},{10,26},{12,28},{14,30},{16,0},... | collective-permute-start | bytes 786440 | tf_op jit(solution)/shard_map/ppermute | solution.py:203
  8.6 1.1 collective-permute-start.12
  9.7 1.7 %collective-permute-start.1 = (bf16[80,512]{1,0:T(8,128)(2,1)S(1)}, bf16[80,512]{1,0:T(8,128)(2,1)S(1)}, u32[]{:S(2)}, u32[]{:S(2)}) collective-permute-start(bf16[80,512]{1,0:T(8,128)(2,1)S(1)} %get-tuple-element.36), channel_id=1, source_target_pairs={{0,16},{2,18},{4,20},{6,22},{8,24},{10,26},{12,28},{14,30},{16,0},... | collective-permute-start | bytes 245768 | tf_op jit(solution)/shard_map/ppermute | solution.py:203
  11.4 0.0 collective-permute-done.refs_6_
  11.4 1.0 collective-permute-start.2
  12.4 25.5 %collective-permute-done.1.refs_7_ = bf16[80,512]{1,0:T(8,128)(2,1)S(1)} collective-permute-done((bf16[80,512]{1,0:T(8,128)(2,1)S(1)}, bf16[80,512]{1,0:T(8,128)(2,1)S(1)}, u32[]{:S(2)}, u32[]{:S(2)}) %collective-permute-start.1) | collective-permute-done | bytes 81952 | tf_op jit(solution)/shard_map/ppermute | solution.py:203
  38.0 1.6 %collective-permute-start.3 = (bf16[320,512]{1,0:T(8,128)(2,1)S(1)}, bf16[320,512]{1,0:T(8,128)(2,1)S(1)}, u32[]{:S(2)}, u32[]{:S(2)}) collective-permute-start(bf16[320,512]{1,0:T(8,128)(2,1)S(1)} %get-tuple-element.32.refs_9_), channel_id=1, source_target_pairs={{0,2},{2,0},{4,6},{6,4},{8,10},{10,8},{12,14},{14,12},{16,18},{18,... | collective-permute-start | bytes 983048 | tf_op jit(solution)/shard_map/ppermute | solution.py:203
  39.5 0.1 reverse.3
  39.6 1.5 %collective-permute-start.4 = (bf16[320,512]{1,0:T(8,128)(2,1)S(1)}, bf16[320,512]{1,0:T(8,128)(2,1)S(1)}, u32[]{:S(2)}, u32[]{:S(2)}) collective-permute-start(bf16[320,512]{1,0:T(8,128)(2,1)S(1)} %get-tuple-element.32.refs_9_), channel_id=1, source_target_pairs={{0,4},{2,6},{4,0},{6,2},{8,12},{10,14},{12,8},{14,10},{16,20},{18,... | collective-permute-start | bytes 983048 | tf_op jit(solution)/shard_map/ppermute | solution.py:203
  41.1 0.0 collective-permute-done.10.refs_0_
  41.1 0.5 collective-permute-start.5
  41.6 0.0 collective-permute-done.11.refs_1_
  41.6 0.0 collective-permute-done.12.refs_2_
  41.6 1.0 pad_maximum_fusion
  42.6 0.0 collective-permute-start.13
  42.6 6.1 %collective-permute-done.3.refs_10_ = bf16[320,512]{1,0:T(8,128)(2,1)S(1)} collective-permute-done((bf16[320,512]{1,0:T(8,128)(2,1)S(1)}, bf16[320,512]{1,0:T(8,128)(2,1)S(1)}, u32[]{:S(2)}, u32[]{:S(2)}) %collective-permute-start.3) | collective-permute-done | bytes 327712 | tf_op jit(solution)/shard_map/ppermute | solution.py:203
  48.7 4.8 %collective-permute-done.4.refs_11_ = bf16[320,512]{1,0:T(8,128)(2,1)S(1)} collective-permute-done((bf16[320,512]{1,0:T(8,128)(2,1)S(1)}, bf16[320,512]{1,0:T(8,128)(2,1)S(1)}, u32[]{:S(2)}, u32[]{:S(2)}) %collective-permute-start.4) | collective-permute-done | bytes 327712 | tf_op jit(solution)/shard_map/ppermute | solution.py:203
  53.5 0.0 collective-permute-done.5.refs_12_
  53.6 0.7 pad_maximum_fusion.1
  54.3 3.8 %collective-permute-start.7 = (bf16[256,512]{1,0:T(8,128)(2,1)}, bf16[256,512]{1,0:T(8,128)(2,1)}, u32[]{:S(2)}, u32[]{:S(2)}) collective-permute-start(bf16[256,512]{1,0:T(8,128)(2,1)} %pad_maximum_fusion.1), channel_id=1, source_target_pairs={{0,16},{2,18},{4,20},{6,22},{8,24},{10,26},{12,28},{14,30},{16,0},... | collective-permute-start | bytes 786440 | tf_op jit(solution)/shard_map/ppermute | solution.py:203
  58.1 0.6 slice.32
  58.7 0.6 pad_maximum_fusion.2.refs_4_
  59.3 0.1 pad_add_fusion.ids
  59.4 1.5 %collective-permute-start.8 = (bf16[256,512]{1,0:T(8,128)(2,1)}, bf16[256,512]{1,0:T(8,128)(2,1)S(1)}, u32[]{:S(2)}, u32[]{:S(2)}) collective-permute-start(bf16[256,512]{1,0:T(8,128)(2,1)} %pad_maximum_fusion.1), channel_id=1, source_target_pairs={{0,24},{2,26},{4,28},{6,30},{8,16},{10,18},{12,20},{14,22},{16,8},... | collective-permute-start | bytes 786440 | tf_op jit(solution)/shard_map/ppermute | solution.py:203
  60.9 13.2 %collective-permute-done.7 = bf16[256,512]{1,0:T(8,128)(2,1)} collective-permute-done((bf16[256,512]{1,0:T(8,128)(2,1)}, bf16[256,512]{1,0:T(8,128)(2,1)}, u32[]{:S(2)}, u32[]{:S(2)}) %collective-permute-start.7) | collective-permute-done | bytes 262176 | tf_op jit(solution)/shard_map/ppermute | solution.py:203
  74.1 1.0 constant_dynamic-update-slice_fusion.8
  75.1 1.0 constant_dynamic-update-slice_fusion.2
  76.0 0.0 collective-permute-done.13.refs_3_
  76.0 4.0 %shard_map.55 = (bf16[1040,256]{1,0:T(8,128)(2,1)}, bf16[1024,256]{1,0:T(8,128)(2,1)S(1)}, bf16[1024,128]{1,0:T(8,128)(2,1)S(1)}) custom-call(s32[3]{0:T(128)S(1)} %pad_add_fusion.ids, bf16[256,1024]{1,0:T(8,128)(2,1)S(1)} %copy-done, bf16[128,1024]{1,0:T(8,128)(2,1)S(1)} %collective-permute-done.10.refs_0_, ...), custom_call_target="tpu_custom_call" | custom-call | flops 1073741824 | bytes 5054988 | tf_op jit(solution)/shard_map/pallas_call | solution.py:175
  80.1 0.8 collective-permute-start.16
  80.9 1.3 %collective-permute-start.15 = (bf16[1040,256]{1,0:T(8,128)(2,1)}, bf16[1040,256]{1,0:T(8,128)(2,1)S(1)}, u32[]{:S(2)}, u32[]{:S(2)}) collective-permute-start(bf16[1040,256]{1,0:T(8,128)(2,1)} %get-tuple-element.13.kv_ref), channel_id=1, source_target_pairs={{0,4},{2,6},{4,0},{6,2},{8,12},{10,14},{12,8},{14,10},{16,20},{18,... | collective-permute-start | bytes 1597448 | tf_op jit(solution)/shard_map/ppermute | solution.py:203
  82.2 1.4 %collective-permute-start.14 = (bf16[1040,256]{1,0:T(8,128)(2,1)}, bf16[1040,256]{1,0:T(8,128)(2,1)S(1)}, u32[]{:S(2)}, u32[]{:S(2)}) collective-permute-start(bf16[1040,256]{1,0:T(8,128)(2,1)} %get-tuple-element.13.kv_ref), channel_id=1, source_target_pairs={{0,6},{2,4},{4,2},{6,0},{8,14},{10,12},{12,10},{14,8},{16,22},{18,... | collective-permute-start | bytes 1597448 | tf_op jit(solution)/shard_map/ppermute | solution.py:203
  83.6 0.0 collective-permute-done.8
  83.6 0.1 broadcast_select_fusion
  83.8 0.1 collective-permute-start.9
  83.8 0.8 copy-done.1
  84.7 1.8 %shard_map.56.refs_0_ = f32[1024,128]{1,0:T(8,128)S(1)} custom-call(s32[3]{0:T(128)S(1)} %pad_add_fusion.ids, bf16[1024,256]{1,0:T(8,128)(2,1)S(1)} %get-tuple-element.12.q_ref, bf16[1040,256]{1,0:T(8,128)(2,1)S(1)} %copy-done.1), custom_call_target="tpu_custom_call" | custom-call | flops 402653184 | bytes 1581068 | tf_op jit(solution)/shard_map/pallas_call | solution.py:175
  86.4 8.5 %collective-permute-done.16.kv_ref = bf16[1040,256]{1,0:T(8,128)(2,1)S(1)} collective-permute-done((bf16[1040,256]{1,0:T(8,128)(2,1)}, bf16[1040,256]{1,0:T(8,128)(2,1)S(1)}, u32[]{:S(2)}, u32[]{:S(2)}) %collective-permute-start.16) | collective-permute-done | bytes 532512 | tf_op jit(solution)/shard_map/ppermute | solution.py:203
  94.9 1.6 %shard_map.57.refs_0_ = f32[1024,128]{1,0:T(8,128)S(1)} custom-call(s32[3]{0:T(128)S(1)} %pad_add_fusion.ids, bf16[1024,256]{1,0:T(8,128)(2,1)S(1)} %get-tuple-element.12.q_ref, bf16[1040,256]{1,0:T(8,128)(2,1)S(1)} %collective-permute-done.16.kv_ref, f32[1024,128]{1,0:T(8,128)S(1)} %shard_map.56.refs_0_), custom_call_target="tpu_custom_call" | custom-call | flops 402653184 | bytes 2105356 | tf_op jit(solution)/shard_map/pallas_call | solution.py:175
  96.5 4.9 %collective-permute-done.15.kv_ref = bf16[1040,256]{1,0:T(8,128)(2,1)S(1)} collective-permute-done((bf16[1040,256]{1,0:T(8,128)(2,1)}, bf16[1040,256]{1,0:T(8,128)(2,1)S(1)}, u32[]{:S(2)}, u32[]{:S(2)}) %collective-permute-start.15) | collective-permute-done | bytes 532512 | tf_op jit(solution)/shard_map/ppermute | solution.py:203
  101.5 1.6 %shard_map.58.refs_0_ = f32[1024,128]{1,0:T(8,128)S(1)} custom-call(s32[3]{0:T(128)S(1)} %pad_add_fusion.ids, bf16[1024,256]{1,0:T(8,128)(2,1)S(1)} %get-tuple-element.12.q_ref, bf16[1040,256]{1,0:T(8,128)(2,1)S(1)} %collective-permute-done.15.kv_ref, f32[1024,128]{1,0:T(8,128)S(1)} %shard_map.57.refs_0_), custom_call_target="tpu_custom_call" | custom-call | flops 402653184 | bytes 2105356 | tf_op jit(solution)/shard_map/pallas_call | solution.py:175
  103.1 0.0 collective-permute-done.14.kv_ref
  103.1 1.6 %shard_map.59 = (bf16[256,256]{1,0:T(8,128)(2,1)S(1)}, bf16[256,256]{1,0:T(8,128)(2,1)S(1)}, bf16[256,256]{1,0:T(8,128)(2,1)S(1)}, bf16[256,256]{1,0:T(8,128)(2,1)S(1)}) custom-call(s32[3]{0:T(128)S(1)} %pad_add_fusion.ids, bf16[1024,256]{1,0:T(8,128)(2,1)S(1)} %get-tuple-element.12.q_ref, bf16[1040,256]{1,0:T(8,128)(2,1)S(1)} %collective-permute-done.14.kv_ref, ...), custom_call_target="tpu_custom_call" | custom-call | flops 402653184 | bytes 2367500 | tf_op jit(solution)/shard_map/pallas_call | solution.py:175
  104.7 0.1 collective-permute-start.17
  104.8 0.1 collective-permute-start.18
  104.9 4.3 %collective-permute-start.19 = (bf16[256,256]{1,0:T(8,128)(2,1)S(1)}, bf16[256,256]{1,0:T(8,128)(2,1)S(1)}, u32[]{:S(2)}, u32[]{:S(2)}) collective-permute-start(bf16[256,256]{1,0:T(8,128)(2,1)S(1)} %get-tuple-element.18), channel_id=1, source_target_pairs={{0,24},{2,26},{4,28},{6,30},{8,16},{10,18},{12,20},{14,22},{16,8},... | collective-permute-start | bytes 393224 | tf_op jit(solution)/shard_map/ppermute | solution.py:203
  109.2 0.0 collective-permute-start.20
  109.2 2.0 %collective-permute-done.17.refs_1_ = bf16[256,256]{1,0:T(8,128)(2,1)S(1)} collective-permute-done((bf16[256,256]{1,0:T(8,128)(2,1)S(1)}, bf16[256,256]{1,0:T(8,128)(2,1)S(1)}, u32[]{:S(2)}, u32[]{:S(2)}) %collective-permute-start.17) | collective-permute-done | bytes 131104 | tf_op jit(solution)/shard_map/ppermute | solution.py:203
  111.2 0.5 collective-permute-start.22
  111.7 2.0 %collective-permute-done.19.refs_3_ = bf16[256,256]{1,0:T(8,128)(2,1)S(1)} collective-permute-done((bf16[256,256]{1,0:T(8,128)(2,1)S(1)}, bf16[256,256]{1,0:T(8,128)(2,1)S(1)}, u32[]{:S(2)}, u32[]{:S(2)}) %collective-permute-start.19) | collective-permute-done | bytes 131104 | tf_op jit(solution)/shard_map/ppermute | solution.py:203
  113.7 0.0 collective-permute-done.9.given
  113.7 0.0 collective-permute-done.20.refs_4_
  113.7 0.0 collective-permute-done.21.refs_5_
  113.7 1.3 %collective-permute-done.23.refs_7_ = bf16[256,256]{1,0:T(8,128)(2,1)S(1)} collective-permute-done((bf16[256,256]{1,0:T(8,128)(2,1)S(1)}, bf16[256,256]{1,0:T(8,128)(2,1)S(1)}, u32[]{:S(2)}, u32[]{:S(2)}) %collective-permute-start.23) | collective-permute-done | bytes 131104 | tf_op jit(solution)/shard_map/ppermute | solution.py:206
  115.0 2.5 %shard_map.60 = bf16[256,512]{1,0:T(8,128)(2,1)} custom-call(s32[3]{0:T(128)S(1)} %pad_add_fusion.ids, bf16[256,1024]{1,0:T(8,128)(2,1)S(1)} %copy-done, bf16[512,512]{1,0:T(8,128)(2,1)S(1)} %get-tuple-element.22.kept, bf16[512,512]{1,0:T(8,128)(2,1)S(1)} %collective-permute-done.9.given, bf16[256,256]{1,0:T(8,128)(2,1)S(1)} %get-tuple-element.15.refs_0_, ...), custom_call_target="tpu_custom_call" | custom-call | flops 268435456 | bytes 2883596 | tf_op jit(solution)/shard_map/pallas_call | solution.py:175
  (28 shorter events, 0.2 us)
Async XLA Ops:
  0.0 1.3 %copy-start.3 = (s32[256]{0:T(256)S(1)}, s32[256]{0:T(256)}, u32[]{:S(2)}) copy-start(s32[256]{0:T(256)} %param.9) | copy-start | bytes 3076
  1.2 3.4 %copy-start = (bf16[256,1024]{1,0:T(8,128)(2,1)S(1)}, bf16[256,1024]{1,0:T(8,128)(2,1)}, u32[]{:S(2)}) copy-start(bf16[256,1024]{1,0:T(8,128)(2,1)} %events.3) | copy-start | bytes 1572868
  1.4 36.5 %copy-start.2 = (bf16[512,64]{0,1:T(8,128)(2,1)S(1)}, bf16[512,64]{0,1:T(8,128)(2,1)}, u32[]{:S(2)}) copy-start(bf16[512,64]{0,1:T(8,128)(2,1)} %param.7) | copy-start | bytes 196612
  1.4 38.1 %copy-start.4 = (bf16[4,128]{1,0:T(4,128)(2,1)S(1)}, bf16[4,128]{1,0:T(4,128)(2,1)}, u32[]{:S(2)}) copy-start(bf16[4,128]{1,0:T(4,128)(2,1)} %param.8) | copy-start | bytes 3076
  1.5 9.9 %collective-permute-start = (bf16[80,512]{1,0:T(8,128)(2,1)S(1)}, bf16[80,512]{1,0:T(8,128)(2,1)S(1)}, u32[]{:S(2)}, u32[]{:S(2)}) collective-permute-start(bf16[80,512]{1,0:T(8,128)(2,1)S(1)} %get-tuple-element.35), channel_id=1, source_target_pairs={{0,8},{2,10},{4,12},{6,14},{8,0},{10,2},{12,4},{14,6},{16,24},{18,... | collective-permute-start | bytes 245768 | tf_op jit(solution)/shard_map/ppermute | solution.py:203
  5.3 35.9 %collective-permute-start.10 = (bf16[128,1024]{1,0:T(8,128)(2,1)}, bf16[128,1024]{1,0:T(8,128)(2,1)S(1)}, u32[]{:S(2)}, u32[]{:S(2)}) collective-permute-start(bf16[128,1024]{1,0:T(8,128)(2,1)} %constant_dynamic-slice_fusion.1), channel_id=1, source_target_pairs={{0,8},{2,10},{4,12},{6,14},{8,0},{10,2},{12,4},{14,6},{16,24},{18,... | collective-permute-start | bytes 786440 | tf_op jit(solution)/shard_map/ppermute | solution.py:203
  6.0 35.7 %collective-permute-start.11 = (bf16[128,1024]{1,0:T(8,128)(2,1)}, bf16[128,1024]{1,0:T(8,128)(2,1)S(1)}, u32[]{:S(2)}, u32[]{:S(2)}) collective-permute-start(bf16[128,1024]{1,0:T(8,128)(2,1)} %constant_dynamic-slice_fusion.1), channel_id=1, source_target_pairs={{0,16},{2,18},{4,20},{6,22},{8,24},{10,26},{12,28},{14,30},{16,0},... | collective-permute-start | bytes 786440 | tf_op jit(solution)/shard_map/ppermute | solution.py:203
  8.6 33.1 %collective-permute-start.12 = (bf16[128,1024]{1,0:T(8,128)(2,1)}, bf16[128,1024]{1,0:T(8,128)(2,1)S(1)}, u32[]{:S(2)}, u32[]{:S(2)}) collective-permute-start(bf16[128,1024]{1,0:T(8,128)(2,1)} %constant_dynamic-slice_fusion.1), channel_id=1, source_target_pairs={{0,24},{2,26},{4,28},{6,30},{8,16},{10,18},{12,20},{14,22},{16,8},... | collective-permute-start | bytes 786440 | tf_op jit(solution)/shard_map/ppermute | solution.py:203
  9.7 28.2 %collective-permute-start.1 = (bf16[80,512]{1,0:T(8,128)(2,1)S(1)}, bf16[80,512]{1,0:T(8,128)(2,1)S(1)}, u32[]{:S(2)}, u32[]{:S(2)}) collective-permute-start(bf16[80,512]{1,0:T(8,128)(2,1)S(1)} %get-tuple-element.36), channel_id=1, source_target_pairs={{0,16},{2,18},{4,20},{6,22},{8,24},{10,26},{12,28},{14,30},{16,0},... | collective-permute-start | bytes 245768 | tf_op jit(solution)/shard_map/ppermute | solution.py:203
  11.4 26.6 %collective-permute-start.2 = (bf16[80,512]{1,0:T(8,128)(2,1)S(1)}, bf16[80,512]{1,0:T(8,128)(2,1)S(1)}, u32[]{:S(2)}, u32[]{:S(2)}) collective-permute-start(bf16[80,512]{1,0:T(8,128)(2,1)S(1)} %get-tuple-element.37), channel_id=1, source_target_pairs={{0,24},{2,26},{4,28},{6,30},{8,16},{10,18},{12,20},{14,22},{16,8},... | collective-permute-start | bytes 245768 | tf_op jit(solution)/shard_map/ppermute | solution.py:203
  38.0 10.7 %collective-permute-start.3 = (bf16[320,512]{1,0:T(8,128)(2,1)S(1)}, bf16[320,512]{1,0:T(8,128)(2,1)S(1)}, u32[]{:S(2)}, u32[]{:S(2)}) collective-permute-start(bf16[320,512]{1,0:T(8,128)(2,1)S(1)} %get-tuple-element.32.refs_9_), channel_id=1, source_target_pairs={{0,2},{2,0},{4,6},{6,4},{8,10},{10,8},{12,14},{14,12},{16,18},{18,... | collective-permute-start | bytes 983048 | tf_op jit(solution)/shard_map/ppermute | solution.py:203
  39.6 13.9 %collective-permute-start.4 = (bf16[320,512]{1,0:T(8,128)(2,1)S(1)}, bf16[320,512]{1,0:T(8,128)(2,1)S(1)}, u32[]{:S(2)}, u32[]{:S(2)}) collective-permute-start(bf16[320,512]{1,0:T(8,128)(2,1)S(1)} %get-tuple-element.32.refs_9_), channel_id=1, source_target_pairs={{0,4},{2,6},{4,0},{6,2},{8,12},{10,14},{12,8},{14,10},{16,20},{18,... | collective-permute-start | bytes 983048 | tf_op jit(solution)/shard_map/ppermute | solution.py:203
  41.1 12.4 %collective-permute-start.5 = (bf16[320,512]{1,0:T(8,128)(2,1)S(1)}, bf16[320,512]{1,0:T(8,128)(2,1)S(1)}, u32[]{:S(2)}, u32[]{:S(2)}) collective-permute-start(bf16[320,512]{1,0:T(8,128)(2,1)S(1)} %get-tuple-element.32.refs_9_), channel_id=1, source_target_pairs={{0,6},{2,4},{4,2},{6,0},{8,14},{10,12},{12,10},{14,8},{16,22},{18,... | collective-permute-start | bytes 983048 | tf_op jit(solution)/shard_map/ppermute | solution.py:203
  42.6 33.4 %collective-permute-start.13 = (bf16[384,1024]{1,0:T(8,128)(2,1)}, bf16[384,1024]{1,0:T(8,128)(2,1)}, u32[]{:S(2)}, u32[]{:S(2)}) collective-permute-start(bf16[384,1024]{1,0:T(8,128)(2,1)} %pad_maximum_fusion), channel_id=1, source_target_pairs={{0,1},{1,0},{2,3},{3,2},{4,5},{5,4},{6,7},{7,6},{8,9},{9,8},{10,11... | collective-permute-start | bytes 2359304 | tf_op jit(solution)/shard_map/ppermute | solution.py:206
  54.3 19.8 %collective-permute-start.7 = (bf16[256,512]{1,0:T(8,128)(2,1)}, bf16[256,512]{1,0:T(8,128)(2,1)}, u32[]{:S(2)}, u32[]{:S(2)}) collective-permute-start(bf16[256,512]{1,0:T(8,128)(2,1)} %pad_maximum_fusion.1), channel_id=1, source_target_pairs={{0,16},{2,18},{4,20},{6,22},{8,24},{10,26},{12,28},{14,30},{16,0},... | collective-permute-start | bytes 786440 | tf_op jit(solution)/shard_map/ppermute | solution.py:203
  58.7 16.4 %collective-permute-start.6 = (bf16[256,512]{1,0:T(8,128)(2,1)}, bf16[256,512]{1,0:T(8,128)(2,1)}, u32[]{:S(2)}, u32[]{:S(2)}) collective-permute-start(bf16[256,512]{1,0:T(8,128)(2,1)} %pad_maximum_fusion.1), channel_id=1, source_target_pairs={{0,8},{2,10},{4,12},{6,14},{8,0},{10,2},{12,4},{14,6},{16,24},{18,... | collective-permute-start | bytes 786440 | tf_op jit(solution)/shard_map/ppermute | solution.py:203
  59.4 24.2 %collective-permute-start.8 = (bf16[256,512]{1,0:T(8,128)(2,1)}, bf16[256,512]{1,0:T(8,128)(2,1)S(1)}, u32[]{:S(2)}, u32[]{:S(2)}) collective-permute-start(bf16[256,512]{1,0:T(8,128)(2,1)} %pad_maximum_fusion.1), channel_id=1, source_target_pairs={{0,24},{2,26},{4,28},{6,30},{8,16},{10,18},{12,20},{14,22},{16,8},... | collective-permute-start | bytes 786440 | tf_op jit(solution)/shard_map/ppermute | solution.py:203
  80.1 14.8 %collective-permute-start.16 = (bf16[1040,256]{1,0:T(8,128)(2,1)}, bf16[1040,256]{1,0:T(8,128)(2,1)S(1)}, u32[]{:S(2)}, u32[]{:S(2)}) collective-permute-start(bf16[1040,256]{1,0:T(8,128)(2,1)} %get-tuple-element.13.kv_ref), channel_id=1, source_target_pairs={{0,2},{2,0},{4,6},{6,4},{8,10},{10,8},{12,14},{14,12},{16,18},{18,... | collective-permute-start | bytes 1597448 | tf_op jit(solution)/shard_map/ppermute | solution.py:203
  80.9 20.6 %collective-permute-start.15 = (bf16[1040,256]{1,0:T(8,128)(2,1)}, bf16[1040,256]{1,0:T(8,128)(2,1)S(1)}, u32[]{:S(2)}, u32[]{:S(2)}) collective-permute-start(bf16[1040,256]{1,0:T(8,128)(2,1)} %get-tuple-element.13.kv_ref), channel_id=1, source_target_pairs={{0,4},{2,6},{4,0},{6,2},{8,12},{10,14},{12,8},{14,10},{16,20},{18,... | collective-permute-start | bytes 1597448 | tf_op jit(solution)/shard_map/ppermute | solution.py:203
  82.2 20.9 %collective-permute-start.14 = (bf16[1040,256]{1,0:T(8,128)(2,1)}, bf16[1040,256]{1,0:T(8,128)(2,1)S(1)}, u32[]{:S(2)}, u32[]{:S(2)}) collective-permute-start(bf16[1040,256]{1,0:T(8,128)(2,1)} %get-tuple-element.13.kv_ref), channel_id=1, source_target_pairs={{0,6},{2,4},{4,2},{6,0},{8,14},{10,12},{12,10},{14,8},{16,22},{18,... | collective-permute-start | bytes 1597448 | tf_op jit(solution)/shard_map/ppermute | solution.py:203
  83.6 1.1 copy-start.1
  83.8 29.9 %collective-permute-start.9 = (bf16[512,512]{1,0:T(8,128)(2,1)S(1)}, bf16[512,512]{1,0:T(8,128)(2,1)S(1)}, u32[]{:S(2)}, u32[]{:S(2)}) collective-permute-start(bf16[512,512]{1,0:T(8,128)(2,1)S(1)} %get-tuple-element.21), channel_id=1, source_target_pairs={{0,1},{1,0},{2,3},{3,2},{4,5},{5,4},{6,7},{7,6},{8,9},{9,8},{10,11... | collective-permute-start | bytes 1572872 | tf_op jit(solution)/shard_map/ppermute | solution.py:206
  104.7 6.4 %collective-permute-start.17 = (bf16[256,256]{1,0:T(8,128)(2,1)S(1)}, bf16[256,256]{1,0:T(8,128)(2,1)S(1)}, u32[]{:S(2)}, u32[]{:S(2)}) collective-permute-start(bf16[256,256]{1,0:T(8,128)(2,1)S(1)} %get-tuple-element.16), channel_id=1, source_target_pairs={{0,8},{2,10},{4,12},{6,14},{8,0},{10,2},{12,4},{14,6},{16,24},{18,... | collective-permute-start | bytes 393224 | tf_op jit(solution)/shard_map/ppermute | solution.py:203
  104.8 6.4 %collective-permute-start.18 = (bf16[256,256]{1,0:T(8,128)(2,1)S(1)}, bf16[256,256]{1,0:T(8,128)(2,1)S(1)}, u32[]{:S(2)}, u32[]{:S(2)}) collective-permute-start(bf16[256,256]{1,0:T(8,128)(2,1)S(1)} %get-tuple-element.17), channel_id=1, source_target_pairs={{0,16},{2,18},{4,20},{6,22},{8,24},{10,26},{12,28},{14,30},{16,0},... | collective-permute-start | bytes 393224 | tf_op jit(solution)/shard_map/ppermute | solution.py:203
  104.9 8.7 %collective-permute-start.19 = (bf16[256,256]{1,0:T(8,128)(2,1)S(1)}, bf16[256,256]{1,0:T(8,128)(2,1)S(1)}, u32[]{:S(2)}, u32[]{:S(2)}) collective-permute-start(bf16[256,256]{1,0:T(8,128)(2,1)S(1)} %get-tuple-element.18), channel_id=1, source_target_pairs={{0,24},{2,26},{4,28},{6,30},{8,16},{10,18},{12,20},{14,22},{16,8},... | collective-permute-start | bytes 393224 | tf_op jit(solution)/shard_map/ppermute | solution.py:203
  109.2 4.5 %collective-permute-start.20 = (bf16[256,256]{1,0:T(8,128)(2,1)S(1)}, bf16[256,256]{1,0:T(8,128)(2,1)S(1)}, u32[]{:S(2)}, u32[]{:S(2)}) collective-permute-start(bf16[256,256]{1,0:T(8,128)(2,1)S(1)} %get-tuple-element.15.refs_0_), channel_id=1, source_target_pairs={{0,1},{1,0},{2,3},{3,2},{4,5},{5,4},{6,7},{7,6},{8,9},{9,8},{10,11... | collective-permute-start | bytes 393224 | tf_op jit(solution)/shard_map/ppermute | solution.py:206
  111.2 2.5 %collective-permute-start.21 = (bf16[256,256]{1,0:T(8,128)(2,1)S(1)}, bf16[256,256]{1,0:T(8,128)(2,1)S(1)}, u32[]{:S(2)}, u32[]{:S(2)}) collective-permute-start(bf16[256,256]{1,0:T(8,128)(2,1)S(1)} %collective-permute-done.17.refs_1_), channel_id=1, source_target_pairs={{0,1},{1,0},{2,3},{3,2},{4,5},{5,4},{6,7},{7,6},{8,9},{9,8},{10,11... | collective-permute-start | bytes 393224 | tf_op jit(solution)/shard_map/ppermute | solution.py:206
  111.2 2.5 %collective-permute-start.22 = (bf16[256,256]{1,0:T(8,128)(2,1)S(1)}, bf16[256,256]{1,0:T(8,128)(2,1)S(1)}, u32[]{:S(2)}, u32[]{:S(2)}) collective-permute-start(bf16[256,256]{1,0:T(8,128)(2,1)S(1)} %collective-permute-done.18.refs_2_), channel_id=1, source_target_pairs={{0,1},{1,0},{2,3},{3,2},{4,5},{5,4},{6,7},{7,6},{8,9},{9,8},{10,11... | collective-permute-start | bytes 393224 | tf_op jit(solution)/shard_map/ppermute | solution.py:206
  113.7 1.3 %collective-permute-start.23 = (bf16[256,256]{1,0:T(8,128)(2,1)S(1)}, bf16[256,256]{1,0:T(8,128)(2,1)S(1)}, u32[]{:S(2)}, u32[]{:S(2)}) collective-permute-start(bf16[256,256]{1,0:T(8,128)(2,1)S(1)} %collective-permute-done.19.refs_3_), channel_id=1, source_target_pairs={{0,1},{1,0},{2,3},{3,2},{4,5},{5,4},{6,7},{7,6},{8,9},{9,8},{10,11... | collective-permute-start | bytes 393224 | tf_op jit(solution)/shard_map/ppermute | solution.py:206

commit v2 on v1

--- a/solution.py
+++ b/solution.py
@@ -39,11 +39,12 @@
     other, bias_row, own_msg = refs[lead - 1 : lead + 2]
     marks = refs[lead + 2 : 2 * lead + 1]
     weights = refs[2 * lead + 1 : 2 * lead + 1 + lines]
-    kv_ref, q_ref, u_ref, wbuf, xbuf = refs[2 * lead + 1 + lines :]
+    kv_ref, q_ref, *u_refs = refs[2 * lead + 1 + lines : -2]
+    wbuf, xbuf = refs[-2:]
     a, i, c = ids[0], ids[1], ids[2]
     rows, _ = events.shape
     half = rows // 2
-    size = u_ref.shape[1]
+    size = u_refs[0].shape[1]
     buckets = bias_row.shape[1]
     chunk = wbuf.shape[0] // (lead * lines)
     for j in range(lines):
@@ -73,7 +74,7 @@
         product = jnp.dot(normed, wbuf[...], preferred_element_type=jnp.float32)
         active = half_silu(0.5 * product)
         base = pl.ds(pl.multiple_of((a ^ k) * rows, rows), rows)
-        u_ref[base, :] = active[:, :size].astype(jnp.bfloat16)
+        u_refs[k][...] = active[:, :size].astype(jnp.bfloat16)
         kv_ref[base, size : 2 * size] = active[:, size : 2 * size].astype(jnp.bfloat16)
         q_ref[base, :size] = (active[:, 2 * size : 3 * size] * scale).astype(jnp.bfloat16)
         kv_ref[base, :size] = active[:, 3 * size :].astype(jnp.bfloat16)
@@ -88,7 +89,7 @@
 def attention_kernel(lead, j, last, ids, q_ref, kv_ref, *refs):
     refs = list(refs)
     before = refs.pop(0) if j > 0 else None
-    u_ref = refs.pop(0) if last else None
+    gates, refs = (refs[:lead], refs[lead:]) if last else ([], refs)
     outs, (kaug, total) = refs[:-2], refs[-2:]
     a, i = ids[0], ids[1]
     size = q_ref.shape[1] // 2
@@ -133,7 +134,7 @@
         for k in range(lead):
             base = pl.ds(pl.multiple_of((a ^ k) * rows, rows), rows)
             outs[k][:, :size] = total[base, :].astype(jnp.bfloat16)
-            outs[k][:, size:] = u_ref[base, :]
+            outs[k][:, size:] = gates[k][...]
     else:
         outs[0][...] = total[...]
 
@@ -172,7 +173,7 @@
 
 def call(kernel, ins, outs, scratch, flops, transcendentals=0):
     size = sum(math.prod(x.shape) * x.dtype.itemsize for x in [*ins, *outs])
-    return pl.pallas_call(
+    return list(pl.pallas_call(
         kernel,
         out_shape=outs,
         in_specs=[pl.BlockSpec(memory_space=pltpu.SMEM)] + vmem(len(ins) - 1),
@@ -182,7 +183,7 @@
         cost_estimate=pl.CostEstimate(
             flops=flops, bytes_accessed=size, transcendentals=transcendentals
         ),
-    )(*ins)
+    )(*ins))
 
 
 def per_device(events, w_uvqk, w_out, time_bias, stamps):
@@ -202,6 +203,13 @@
     def exchange(x, flip):
         return lax.ppermute(x, "seq", [(t, t ^ flip) for t in range(devices)])
 
+    def spread(x):
+        held = [x]
+        for k in range(1, lead):
+            low = k & -k
+            held.append(exchange(held[k ^ low], low * lines))
+        return held
+
     def swap(x):
         return lax.ppermute(x, "head", [(0, 1), (1, 0)])
 
@@ -216,46 +224,52 @@
     ]
     got = [exchange(sent[k], k * lines) for k in range(1, lead)]
     own_half = lax.dynamic_slice_in_dim(events, c * half, half, 0)
-    arrived = [exchange(own_half, k * lines) for k in range(1, lead)]
+    own_half, got[0] = lax.optimization_barrier((own_half, got[0]))
+    arrived = spread(own_half)[1:]
     w_out_t = w_out.T
     stack = jnp.concatenate([x[:chunk] for x in [sent[0], *got]] + [w_out_t])
     stacks = [stack] + [exchange(stack, j) for j in range(1, lines)]
+    held = lax.optimization_barrier((*arrived, *stacks[1:]))
+    arrived, stacks[1:] = list(held[: lead - 1]), held[lead - 1 :]
     other = swap(jnp.concatenate(arrived))
     bias_row = lax.dynamic_index_in_dim(time_bias, a, 0, True).astype(f32) * 0.5
     bias_row = jnp.roll(bias_row[:, ::-1], 1, axis=1)
 
     span = lead * rows
-    kv, queries, gate = call(
+    kv, queries, *gates = call(
         functools.partial(projection_kernel, lead, lines),
         [ids, events, *arrived, other, bias_row, sent[0], *got, *stacks],
-        [shape(span + PAD, 2 * size), shape(span, size + bias_row.shape[1]), shape(span, size)],
+        [shape(span + PAD, 2 * size), shape(span, size + bias_row.shape[1])]
+        + [shape(rows, size)] * lead,
         [pltpu.VMEM((width, 4 * size), bf16), pltpu.VMEM((rows, width), bf16)],
         2 * span * width * 4 * size,
         span * 4 * size,
     )
-    kvs = [kv] + [exchange(kv, j) for j in range(1, lines)]
-
-    columns = jnp.concatenate([x[lead * chunk :] for x in stacks])
-    shares = [columns] + [exchange(columns, k * lines) for k in range(1, lead)]
-    low, high = jnp.concatenate(shares[: lead // 2]), jnp.concatenate(shares[lead // 2 :])
-    mine = (a // (lead // 2)) == c
-    kept = jnp.where(mine, low, high)
-    given = swap(jnp.where(mine, high, low))
-
-    total = None
-    for j in range(lines):
+
+    def attend(j, total):
         last = j == lines - 1
-        ins = [ids, queries, kvs[j]] + ([total] if j else []) + ([gate] if last else [])
         outs = [shape(rows, 2 * size)] * lead if last else [shape(span, size, dtype=f32)]
-        result = call(
+        return call(
             functools.partial(attention_kernel, lead, j, last),
-            ins,
+            [ids, queries, kvs[j]] + ([total] if j else []) + (gates if last else []),
             outs,
             [pltpu.VMEM((span, queries.shape[1]), bf16), pltpu.VMEM((span, size), f32)],
             span * span * 3 * size,
             span * span // 2,
         )
-        total = result[0]
+
+    columns = jnp.concatenate([x[lead * chunk :] for x in stacks])
+    columns, kv = lax.optimization_barrier((columns, kv))
+    kvs = [kv] + [exchange(kv, j) for j in range(1, lines)]
+    shares = spread(columns)
+    low, high = jnp.concatenate(shares[: lead // 2]), jnp.concatenate(shares[lead // 2 :])
+    mine = (a // (lead // 2)) == c
+    kept = jnp.where(mine, low, high)
+    given = swap(jnp.where(mine, high, low))
+
+    result = [None]
+    for j in range(lines):
+        result = attend(j, result[0])
     own = [result[0]] + [exchange(result[k], k * lines) for k in range(1, lead)]
     across = [swap(x) for x in own]
     return call(

time: 118 us -> 94.3 us (0.80)
  waiting for transfers between devices: 68.4 us -> 46.4 us
    ppermute x18, waiting for transfers between devices: 67 us -> 45 us  [exchange(): return lax.ppermute(x, 'seq', [(t, t ^ flip) for t in range(devices)])]
    unnamed x15 -> x20, local copies, waits for them, and re-layouts: 1.85 us -> 2.9 us
  transfers between devices with their start and end apart: 24 -> 24, of which waited for: 9 -> 12; matrix products, arithmetic and copies ran while one was open for 5% -> 4% of each run, Pallas kernels for 9% -> 7%
where the time goes in v2:
time: 94.3 us; the launch traced here: 94 us
  waiting for transfers between devices  46.4 us (49%)
  starting transfers between devices  26.5 us (28%)
  Pallas kernels  13.2 us (14%)
  local copies, waits for them, and re-layouts  4.97 us (5%)
  other arithmetic  2.56 us (3%)
    ppermute x18, waiting for transfers between devices, exchange(): return lax.ppermute(x, 'seq', [(t, t ^ flip) for t in range(devices)])  45 us
    ppermute x18, starting transfers between devices, exchange(): return lax.ppermute(x, 'seq', [(t, t ^ flip) for t in range(devices)])  26 us
    pallas_call x6, Pallas kernels, call(): pl.pallas_call(kernel, out_shape=outs, in_specs=[pl.BlockSpec(memory_spac...  13.2 us
    unnamed x20, local copies, waits for them, and re-layouts  2.9 us
  transfers between devices with their start and end apart: 24, of which 12 were waited for; matrix products, arithmetic and copies ran while one was open for 4% of the time, Pallas kernels for 7%

profile of v2, /device:TPU:0, one launch (start us, length us, event | category | flops | bytes accessed | tf_op | source)
XLA Modules:
  0.0 94.0 jit_solution(12799981485810719100)
XLA Ops:
  0.0 1.1 %reshape.6 = bf16[64,4,4,128]{3,2,1,0:T(4,128)(2,1)S(1)} reshape(bf16[64,4,512]{2,1,0:T(4,128)(2,1)} %param.6) | data formatting | bytes 524288 | tf_op jit(solution)/shard_map/reshape | solution.py:219
  1.1 0.1 copy.6
  1.2 0.0 copy-start
  1.2 0.1 reshape.7
  1.4 0.0 copy-start.4
  1.5 3.1 %collective-permute-start = (bf16[80,512]{1,0:T(8,128)(2,1)S(1)}, bf16[80,512]{1,0:T(8,128)(2,1)S(1)}, u32[]{:S(2)}, u32[]{:S(2)}) collective-permute-start(bf16[80,512]{1,0:T(8,128)(2,1)S(1)} %get-tuple-element.53), channel_id=1, source_target_pairs={{0,8},{2,10},{4,12},{6,14},{8,0},{10,2},{12,4},{14,6},{16,24},{18,... | collective-permute-start | bytes 245768 | tf_op jit(solution)/shard_map/ppermute | solution.py:204
  4.5 2.6 %collective-permute-start.4 = (bf16[80,512]{1,0:T(8,128)(2,1)S(1)}, bf16[80,512]{1,0:T(8,128)(2,1)S(1)}, u32[]{:S(2)}, u32[]{:S(2)}) collective-permute-start(bf16[80,512]{1,0:T(8,128)(2,1)S(1)} %get-tuple-element.54), channel_id=1, source_target_pairs={{0,16},{2,18},{4,20},{6,22},{8,24},{10,26},{12,28},{14,30},{16,0},... | collective-permute-start | bytes 245768 | tf_op jit(solution)/shard_map/ppermute | solution.py:204
  7.1 0.0 collective-permute-start.5
  7.2 0.0 collective-permute-done.refs_6_
  7.2 3.4 %collective-permute-start.2 = (bf16[128,1024]{1,0:T(8,128)(2,1)S(1)}, bf16[128,1024]{1,0:T(8,128)(2,1)S(1)}, u32[]{:S(2)}, u32[]{:S(2)}) collective-permute-start(bf16[128,1024]{1,0:T(8,128)(2,1)S(1)} %constant_dynamic-slice_fusion.1), channel_id=1, source_target_pairs={{0,16},{2,18},{4,20},{6,22},{8,24},{10,26},{12,28},{14,30},{16,0},... | collective-permute-start | bytes 786440 | tf_op jit(solution)/shard_map/ppermute | solution.py:204
  10.6 8.8 %collective-permute-done.4.refs_7_ = bf16[80,512]{1,0:T(8,128)(2,1)S(1)} collective-permute-done((bf16[80,512]{1,0:T(8,128)(2,1)S(1)}, bf16[80,512]{1,0:T(8,128)(2,1)S(1)}, u32[]{:S(2)}, u32[]{:S(2)}) %collective-permute-start.4) | collective-permute-done | bytes 81952 | tf_op jit(solution)/shard_map/ppermute | solution.py:204
  19.5 0.0 collective-permute-done.5.refs_8_
  19.5 0.0 copy-start.6
  19.5 1.6 %collective-permute-start.6 = (bf16[320,512]{1,0:T(8,128)(2,1)S(1)}, bf16[320,512]{1,0:T(8,128)(2,1)S(1)}, u32[]{:S(2)}, u32[]{:S(2)}) collective-permute-start(bf16[320,512]{1,0:T(8,128)(2,1)S(1)} %constant_dynamic-update-slice_fusion.refs_9_), channel_id=1, source_target_pairs={{0,2},{2,0},{4,6},{6,4},{8,10},{10,8},{12,14},{14,12},{16,18},{18,... | collective-permute-start | bytes 983048 | tf_op jit(solution)/shard_map/ppermute | solution.py:204
  21.1 1.5 %collective-permute-start.7 = (bf16[320,512]{1,0:T(8,128)(2,1)S(1)}, bf16[320,512]{1,0:T(8,128)(2,1)S(1)}, u32[]{:S(2)}, u32[]{:S(2)}) collective-permute-start(bf16[320,512]{1,0:T(8,128)(2,1)S(1)} %constant_dynamic-update-slice_fusion.refs_9_), channel_id=1, source_target_pairs={{0,4},{2,6},{4,0},{6,2},{8,12},{10,14},{12,8},{14,10},{16,20},{18,... | collective-permute-start | bytes 983048 | tf_op jit(solution)/shard_map/ppermute | solution.py:204
  22.6 0.5 collective-permute-start.8
  23.1 2.3 %collective-permute-start.1 = (bf16[128,1024]{1,0:T(8,128)(2,1)S(1)}, bf16[128,1024]{1,0:T(8,128)(2,1)S(1)}, u32[]{:S(2)}, u32[]{:S(2)}) collective-permute-start(bf16[128,1024]{1,0:T(8,128)(2,1)S(1)} %constant_dynamic-slice_fusion.1), channel_id=1, source_target_pairs={{0,8},{2,10},{4,12},{6,14},{8,0},{10,2},{12,4},{14,6},{16,24},{18,... | collective-permute-start | bytes 786440 | tf_op jit(solution)/shard_map/ppermute | solution.py:204
  25.4 0.6 collective-permute-done.2.refs_1_
  26.0 0.0 collective-permute-start.3
  26.0 6.6 %collective-permute-done.1.refs_0_ = bf16[128,1024]{1,0:T(8,128)(2,1)S(1)} collective-permute-done((bf16[128,1024]{1,0:T(8,128)(2,1)S(1)}, bf16[128,1024]{1,0:T(8,128)(2,1)S(1)}, u32[]{:S(2)}, u32[]{:S(2)}) %collective-permute-start.1) | collective-permute-done | bytes 262176 | tf_op jit(solution)/shard_map/ppermute | solution.py:204
  32.6 0.0 collective-permute-done.6.refs_10_
  32.6 0.0 collective-permute-done.7.refs_11_
  32.6 0.0 collective-permute-done.8.refs_12_
  32.6 4.5 %collective-permute-done.3.refs_2_ = bf16[128,1024]{1,0:T(8,128)(2,1)S(1)} collective-permute-done((bf16[128,1024]{1,0:T(8,128)(2,1)S(1)}, bf16[128,1024]{1,0:T(8,128)(2,1)S(1)}, u32[]{:S(2)}, u32[]{:S(2)}) %collective-permute-start.3) | collective-permute-done | bytes 262176 | tf_op jit(solution)/shard_map/ppermute | solution.py:204
  37.1 0.9 %pad_maximum_fusion = bf16[384,1024]{1,0:T(8,128)(2,1)} fusion(bf16[128,1024]{1,0:T(8,128)(2,1)S(1)} %collective-permute-done.3.refs_2_, bf16[128,1024]{1,0:T(8,128)(2,1)S(1)} %collective-permute-done.2.refs_1_, bf16[128,1024]{1,0:T(8,128)(2,1)S(1)} %collective-permute-done.1.refs_0_), kind=kLoop, calls=%fused_computation | loop fusion | flops 2359296 | bytes 1572864 | tf_op jit(solution)/shard_map/concatenate | solution.py:234
  38.0 0.1 reverse.3
  38.1 0.6 slice.32
  38.8 0.7 pad_maximum_fusion.2.refs_4_
  39.5 0.1 pad_add_fusion.ids
  39.6 0.7 pad_maximum_fusion.1
  40.3 0.4 collective-permute-done.9.refs_3_
  40.7 1.0 %copy-done.3 = bf16[320,512]{1,0:T(8,128)(2,1)S(1)} copy-done((bf16[320,512]{1,0:T(8,128)(2,1)S(1)}, bf16[320,512]{1,0:T(8,128)(2,1)}, u32[]{:S(2)}) %copy-start.3) | copy-done | bytes 327704
  41.6 4.1 %shard_map.55 = (bf16[1040,256]{1,0:T(8,128)(2,1)}, bf16[1024,256]{1,0:T(8,128)(2,1)S(1)}, bf16[256,128]{1,0:T(8,128)(2,1)S(1)}, bf16[256,128]{1,0:T(8,128)(2,1)...) custom-call(s32[3]{0:T(128)S(1)} %pad_add_fusion.ids, bf16[256,1024]{1,0:T(8,128)(2,1)S(1)} %copy-done, ...), custom_call_target="tpu_custom_call" | custom-call | flops 1073741824 | bytes 5054988 | tf_op jit(solution)/shard_map/pallas_call | solution.py:176
  45.7 1.4 %collective-permute-start.11 = (bf16[256,512]{1,0:T(8,128)(2,1)}, bf16[256,512]{1,0:T(8,128)(2,1)S(1)}, u32[]{:S(2)}, u32[]{:S(2)}) collective-permute-start(bf16[256,512]{1,0:T(8,128)(2,1)} %pad_maximum_fusion.1), channel_id=1, source_target_pairs={{0,16},{2,18},{4,20},{6,22},{8,24},{10,26},{12,28},{14,30},{16,0},... | collective-permute-start | bytes 786440 | tf_op jit(solution)/shard_map/ppermute | solution.py:204
  47.1 1.6 %collective-permute-start.10 = (bf16[256,512]{1,0:T(8,128)(2,1)}, bf16[256,512]{1,0:T(8,128)(2,1)S(1)}, u32[]{:S(2)}, u32[]{:S(2)}) collective-permute-start(bf16[256,512]{1,0:T(8,128)(2,1)} %pad_maximum_fusion.1), channel_id=1, source_target_pairs={{0,8},{2,10},{4,12},{6,14},{8,0},{10,2},{12,4},{14,6},{16,24},{18,... | collective-permute-start | bytes 786440 | tf_op jit(solution)/shard_map/ppermute | solution.py:204
  48.7 1.5 %collective-permute-start.16 = (bf16[1040,256]{1,0:T(8,128)(2,1)}, bf16[1040,256]{1,0:T(8,128)(2,1)S(1)}, u32[]{:S(2)}, u32[]{:S(2)}) collective-permute-start(bf16[1040,256]{1,0:T(8,128)(2,1)} %get-tuple-element.36.kv_ref), channel_id=1, source_target_pairs={{0,2},{2,0},{4,6},{6,4},{8,10},{10,8},{12,14},{14,12},{16,18},{18,... | collective-permute-start | bytes 1597448 | tf_op jit(solution)/shard_map/ppermute | solution.py:204
  50.2 1.5 %collective-permute-start.15 = (bf16[1040,256]{1,0:T(8,128)(2,1)}, bf16[1040,256]{1,0:T(8,128)(2,1)S(1)}, u32[]{:S(2)}, u32[]{:S(2)}) collective-permute-start(bf16[1040,256]{1,0:T(8,128)(2,1)} %get-tuple-element.36.kv_ref), channel_id=1, source_target_pairs={{0,4},{2,6},{4,0},{6,2},{8,12},{10,14},{12,8},{14,10},{16,20},{18,... | collective-permute-start | bytes 1597448 | tf_op jit(solution)/shard_map/ppermute | solution.py:204
  51.7 0.5 collective-permute-start.14
  52.2 8.7 %collective-permute-done.11 = bf16[256,512]{1,0:T(8,128)(2,1)S(1)} collective-permute-done((bf16[256,512]{1,0:T(8,128)(2,1)}, bf16[256,512]{1,0:T(8,128)(2,1)S(1)}, u32[]{:S(2)}, u32[]{:S(2)}) %collective-permute-start.11) | collective-permute-done | bytes 262176 | tf_op jit(solution)/shard_map/ppermute | solution.py:204
  60.9 1.0 %constant_dynamic-update-slice_fusion.3 = bf16[512,512]{1,0:T(8,128)(2,1)S(1)} fusion(bf16[256,512]{1,0:T(8,128)(2,1)} %pad_maximum_fusion.1), kind=kLoop, calls=%fused_computation.20 | loop fusion | bytes 524288
  61.9 0.0 collective-permute-done.10
  61.9 7.1 %collective-permute-done.12 = bf16[256,512]{1,0:T(8,128)(2,1)S(1)} collective-permute-done((bf16[256,512]{1,0:T(8,128)(2,1)S(1)}, bf16[256,512]{1,0:T(8,128)(2,1)S(1)}, u32[]{:S(2)}, u32[]{:S(2)}) %collective-permute-start.12) | collective-permute-done | bytes 262176 | tf_op jit(solution)/shard_map/ppermute | solution.py:204
  69.0 0.1 broadcast_select_fusion
  69.1 0.1 collective-permute-start.13
  69.2 0.9 copy-done.1
  70.1 1.8 %shard_map.56.refs_0_ = f32[1024,128]{1,0:T(8,128)S(1)} custom-call(s32[3]{0:T(128)S(1)} %pad_add_fusion.ids, bf16[1024,256]{1,0:T(8,128)(2,1)S(1)} %get-tuple-element.35.q_ref, bf16[1040,256]{1,0:T(8,128)(2,1)S(1)} %copy-done.1), custom_call_target="tpu_custom_call" | custom-call | flops 402653184 | bytes 1581068 | tf_op jit(solution)/shard_map/pallas_call | solution.py:176
  71.9 1.6 %shard_map.57.refs_0_ = f32[1024,128]{1,0:T(8,128)S(1)} custom-call(s32[3]{0:T(128)S(1)} %pad_add_fusion.ids, bf16[1024,256]{1,0:T(8,128)(2,1)S(1)} %get-tuple-element.35.q_ref, bf16[1040,256]{1,0:T(8,128)(2,1)S(1)} %collective-permute-done.16.kv_ref, f32[1024,128]{1,0:T(8,128)S(1)} %shard_map.56.refs_0_), custom_call_target="tpu_custom_call" | custom-call | flops 402653184 | bytes 2105356 | tf_op jit(solution)/shard_map/pallas_call | solution.py:176
  73.5 1.7 %collective-permute-done.15.kv_ref = bf16[1040,256]{1,0:T(8,128)(2,1)S(1)} collective-permute-done((bf16[1040,256]{1,0:T(8,128)(2,1)}, bf16[1040,256]{1,0:T(8,128)(2,1)S(1)}, u32[]{:S(2)}, u32[]{:S(2)}) %collective-permute-start.15) | collective-permute-done | bytes 532512 | tf_op jit(solution)/shard_map/ppermute | solution.py:204
  75.2 1.6 %shard_map.58.refs_0_ = f32[1024,128]{1,0:T(8,128)S(1)} custom-call(s32[3]{0:T(128)S(1)} %pad_add_fusion.ids, bf16[1024,256]{1,0:T(8,128)(2,1)S(1)} %get-tuple-element.35.q_ref, bf16[1040,256]{1,0:T(8,128)(2,1)S(1)} %collective-permute-done.15.kv_ref, f32[1024,128]{1,0:T(8,128)S(1)} %shard_map.57.refs_0_), custom_call_target="tpu_custom_call" | custom-call | flops 402653184 | bytes 2105356 | tf_op jit(solution)/shard_map/pallas_call | solution.py:176
  76.8 1.7 %shard_map.59 = (bf16[256,256]{1,0:T(8,128)(2,1)S(1)}, bf16[256,256]{1,0:T(8,128)(2,1)S(1)}, bf16[256,256]{1,0:T(8,128)(2,1)S(1)}, bf16[256,256]{1,0:T(8,128)(2,1)S(1)}) custom-call(s32[3]{0:T(128)S(1)} %pad_add_fusion.ids, bf16[1024,256]{1,0:T(8,128)(2,1)S(1)} %get-tuple-element.35.q_ref, bf16[1040,256]{1,0:T(8,128)(2,1)S(1)} %collective-permute-done.14.kv_ref, ...), custom_call_target="tpu_custom_call" | custom-call | flops 402653184 | bytes 2367500 | tf_op jit(solution)/shard_map/pallas_call | solution.py:176
  78.4 0.3 collective-permute-start.17
  78.8 1.6 %collective-permute-start.18 = (bf16[256,256]{1,0:T(8,128)(2,1)S(1)}, bf16[256,256]{1,0:T(8,128)(2,1)S(1)}, u32[]{:S(2)}, u32[]{:S(2)}) collective-permute-start(bf16[256,256]{1,0:T(8,128)(2,1)S(1)} %get-tuple-element.43), channel_id=1, source_target_pairs={{0,16},{2,18},{4,20},{6,22},{8,24},{10,26},{12,28},{14,30},{16,0},... | collective-permute-start | bytes 393224 | tf_op jit(solution)/shard_map/ppermute | solution.py:204
  80.4 2.5 %collective-permute-start.19 = (bf16[256,256]{1,0:T(8,128)(2,1)S(1)}, bf16[256,256]{1,0:T(8,128)(2,1)S(1)}, u32[]{:S(2)}, u32[]{:S(2)}) collective-permute-start(bf16[256,256]{1,0:T(8,128)(2,1)S(1)} %get-tuple-element.44), channel_id=1, source_target_pairs={{0,24},{2,26},{4,28},{6,30},{8,16},{10,18},{12,20},{14,22},{16,8},... | collective-permute-start | bytes 393224 | tf_op jit(solution)/shard_map/ppermute | solution.py:204
  82.9 0.0 collective-permute-start.20
  82.9 0.6 collective-permute-done.17.refs_1_
  83.5 6.4 %collective-permute-done.18.refs_2_ = bf16[256,256]{1,0:T(8,128)(2,1)S(1)} collective-permute-done((bf16[256,256]{1,0:T(8,128)(2,1)S(1)}, bf16[256,256]{1,0:T(8,128)(2,1)S(1)}, u32[]{:S(2)}, u32[]{:S(2)}) %collective-permute-start.18) | collective-permute-done | bytes 131104 | tf_op jit(solution)/shard_map/ppermute | solution.py:204
  89.9 0.0 collective-permute-done.19.refs_3_
  89.9 0.5 collective-permute-start.23
  90.4 0.0 collective-permute-done.20.refs_4_
  90.4 0.0 collective-permute-done.21.refs_5_
  90.4 0.8 collective-permute-done.22.refs_6_
  91.3 0.2 collective-permute-done.23.refs_7_
  91.5 0.0 collective-permute-done.13.given
  91.5 2.5 %shard_map.60 = bf16[256,512]{1,0:T(8,128)(2,1)} custom-call(s32[3]{0:T(128)S(1)} %pad_add_fusion.ids, bf16[256,1024]{1,0:T(8,128)(2,1)S(1)} %copy-done, bf16[512,512]{1,0:T(8,128)(2,1)S(1)} %get-tuple-element.48.kept, bf16[512,512]{1,0:T(8,128)(2,1)S(1)} %collective-permute-done.13.given, bf16[256,256]{1,0:T(8,128)(2,1)S(1)} %get-tuple-element.41.refs_0_, ...), custom_call_target="tpu_custom_call" | custom-call | flops 268435456 | bytes 2883596 | tf_op jit(solution)/shard_map/pallas_call | solution.py:176
  (33 shorter events, 0.2 us)
Async XLA Ops:
  0.0 1.3 %copy-start.5 = (s32[256]{0:T(256)S(1)}, s32[256]{0:T(256)}, u32[]{:S(2)}) copy-start(s32[256]{0:T(256)} %param.9) | copy-start | bytes 3076
  1.2 6.0 %copy-start = (bf16[256,1024]{1,0:T(8,128)(2,1)S(1)}, bf16[256,1024]{1,0:T(8,128)(2,1)}, u32[]{:S(2)}) copy-start(bf16[256,1024]{1,0:T(8,128)(2,1)} %events.3) | copy-start | bytes 1572868
  1.4 18.1 %copy-start.4 = (bf16[512,64]{0,1:T(8,128)(2,1)S(1)}, bf16[512,64]{0,1:T(8,128)(2,1)}, u32[]{:S(2)}) copy-start(bf16[512,64]{0,1:T(8,128)(2,1)} %param.7) | copy-start | bytes 196612
  1.5 5.7 %collective-permute-start = (bf16[80,512]{1,0:T(8,128)(2,1)S(1)}, bf16[80,512]{1,0:T(8,128)(2,1)S(1)}, u32[]{:S(2)}, u32[]{:S(2)}) collective-permute-start(bf16[80,512]{1,0:T(8,128)(2,1)S(1)} %get-tuple-element.53), channel_id=1, source_target_pairs={{0,8},{2,10},{4,12},{6,14},{8,0},{10,2},{12,4},{14,6},{16,24},{18,... | collective-permute-start | bytes 245768 | tf_op jit(solution)/shard_map/ppermute | solution.py:204
  4.5 14.9 %collective-permute-start.4 = (bf16[80,512]{1,0:T(8,128)(2,1)S(1)}, bf16[80,512]{1,0:T(8,128)(2,1)S(1)}, u32[]{:S(2)}, u32[]{:S(2)}) collective-permute-start(bf16[80,512]{1,0:T(8,128)(2,1)S(1)} %get-tuple-element.54), channel_id=1, source_target_pairs={{0,16},{2,18},{4,20},{6,22},{8,24},{10,26},{12,28},{14,30},{16,0},... | collective-permute-start | bytes 245768 | tf_op jit(solution)/shard_map/ppermute | solution.py:204
  7.1 12.3 %collective-permute-start.5 = (bf16[80,512]{1,0:T(8,128)(2,1)S(1)}, bf16[80,512]{1,0:T(8,128)(2,1)S(1)}, u32[]{:S(2)}, u32[]{:S(2)}) collective-permute-start(bf16[80,512]{1,0:T(8,128)(2,1)S(1)} %get-tuple-element.55), channel_id=1, source_target_pairs={{0,24},{2,26},{4,28},{6,30},{8,16},{10,18},{12,20},{14,22},{16,8},... | collective-permute-start | bytes 245768 | tf_op jit(solution)/shard_map/ppermute | solution.py:204
  7.2 18.8 %collective-permute-start.2 = (bf16[128,1024]{1,0:T(8,128)(2,1)S(1)}, bf16[128,1024]{1,0:T(8,128)(2,1)S(1)}, u32[]{:S(2)}, u32[]{:S(2)}) collective-permute-start(bf16[128,1024]{1,0:T(8,128)(2,1)S(1)} %constant_dynamic-slice_fusion.1), channel_id=1, source_target_pairs={{0,16},{2,18},{4,20},{6,22},{8,24},{10,26},{12,28},{14,30},{16,0},... | collective-permute-start | bytes 786440 | tf_op jit(solution)/shard_map/ppermute | solution.py:204
  19.5 18.5 %copy-start.6 = (bf16[4,128]{1,0:T(4,128)(2,1)S(1)}, bf16[4,128]{1,0:T(4,128)(2,1)}, u32[]{:S(2)}) copy-start(bf16[4,128]{1,0:T(4,128)(2,1)} %param.8) | copy-start | bytes 3076
  19.5 13.1 %collective-permute-start.6 = (bf16[320,512]{1,0:T(8,128)(2,1)S(1)}, bf16[320,512]{1,0:T(8,128)(2,1)S(1)}, u32[]{:S(2)}, u32[]{:S(2)}) collective-permute-start(bf16[320,512]{1,0:T(8,128)(2,1)S(1)} %constant_dynamic-update-slice_fusion.refs_9_), channel_id=1, source_target_pairs={{0,2},{2,0},{4,6},{6,4},{8,10},{10,8},{12,14},{14,12},{16,18},{18,... | collective-permute-start | bytes 983048 | tf_op jit(solution)/shard_map/ppermute | solution.py:204
  21.1 11.5 %collective-permute-start.7 = (bf16[320,512]{1,0:T(8,128)(2,1)S(1)}, bf16[320,512]{1,0:T(8,128)(2,1)S(1)}, u32[]{:S(2)}, u32[]{:S(2)}) collective-permute-start(bf16[320,512]{1,0:T(8,128)(2,1)S(1)} %constant_dynamic-update-slice_fusion.refs_9_), channel_id=1, source_target_pairs={{0,4},{2,6},{4,0},{6,2},{8,12},{10,14},{12,8},{14,10},{16,20},{18,... | collective-permute-start | bytes 983048 | tf_op jit(solution)/shard_map/ppermute | solution.py:204
  22.6 10.0 %collective-permute-start.8 = (bf16[320,512]{1,0:T(8,128)(2,1)S(1)}, bf16[320,512]{1,0:T(8,128)(2,1)S(1)}, u32[]{:S(2)}, u32[]{:S(2)}) collective-permute-start(bf16[320,512]{1,0:T(8,128)(2,1)S(1)} %constant_dynamic-update-slice_fusion.refs_9_), channel_id=1, source_target_pairs={{0,6},{2,4},{4,2},{6,0},{8,14},{10,12},{12,10},{14,8},{16,22},{18,... | collective-permute-start | bytes 983048 | tf_op jit(solution)/shard_map/ppermute | solution.py:204
  23.1 9.5 %collective-permute-start.1 = (bf16[128,1024]{1,0:T(8,128)(2,1)S(1)}, bf16[128,1024]{1,0:T(8,128)(2,1)S(1)}, u32[]{:S(2)}, u32[]{:S(2)}) collective-permute-start(bf16[128,1024]{1,0:T(8,128)(2,1)S(1)} %constant_dynamic-slice_fusion.1), channel_id=1, source_target_pairs={{0,8},{2,10},{4,12},{6,14},{8,0},{10,2},{12,4},{14,6},{16,24},{18,... | collective-permute-start | bytes 786440 | tf_op jit(solution)/shard_map/ppermute | solution.py:204
  26.0 11.1 %collective-permute-start.3 = (bf16[128,1024]{1,0:T(8,128)(2,1)S(1)}, bf16[128,1024]{1,0:T(8,128)(2,1)S(1)}, u32[]{:S(2)}, u32[]{:S(2)}) collective-permute-start(bf16[128,1024]{1,0:T(8,128)(2,1)S(1)} %collective-permute-done.2.refs_1_), channel_id=1, source_target_pairs={{0,8},{2,10},{4,12},{6,14},{8,0},{10,2},{12,4},{14,6},{16,24},{18,... | collective-permute-start | bytes 786440 | tf_op jit(solution)/shard_map/ppermute | solution.py:204
  32.6 7.0 %copy-start.2 = (bf16[320,512]{1,0:T(8,128)(2,1)}, bf16[320,512]{1,0:T(8,128)(2,1)S(1)}, u32[]{:S(2)}) copy-start(bf16[320,512]{1,0:T(8,128)(2,1)S(1)} %collective-permute-done.8.refs_12_) | copy-start | bytes 983044
  38.0 2.6 %collective-permute-start.9 = (bf16[384,1024]{1,0:T(8,128)(2,1)}, bf16[384,1024]{1,0:T(8,128)(2,1)}, u32[]{:S(2)}, u32[]{:S(2)}) collective-permute-start(bf16[384,1024]{1,0:T(8,128)(2,1)} %pad_maximum_fusion), channel_id=1, source_target_pairs={{0,1},{1,0},{2,3},{3,2},{4,5},{5,4},{6,7},{7,6},{8,9},{9,8},{10,11... | collective-permute-start | bytes 2359304 | tf_op jit(solution)/shard_map/ppermute | solution.py:214
  40.7 1.0 %copy-start.3 = (bf16[320,512]{1,0:T(8,128)(2,1)S(1)}, bf16[320,512]{1,0:T(8,128)(2,1)}, u32[]{:S(2)}) copy-start(bf16[320,512]{1,0:T(8,128)(2,1)} %copy-done.2) | copy-start | bytes 983044
  45.7 15.2 %collective-permute-start.11 = (bf16[256,512]{1,0:T(8,128)(2,1)}, bf16[256,512]{1,0:T(8,128)(2,1)S(1)}, u32[]{:S(2)}, u32[]{:S(2)}) collective-permute-start(bf16[256,512]{1,0:T(8,128)(2,1)} %pad_maximum_fusion.1), channel_id=1, source_target_pairs={{0,16},{2,18},{4,20},{6,22},{8,24},{10,26},{12,28},{14,30},{16,0},... | collective-permute-start | bytes 786440 | tf_op jit(solution)/shard_map/ppermute | solution.py:204
  47.1 14.8 %collective-permute-start.10 = (bf16[256,512]{1,0:T(8,128)(2,1)}, bf16[256,512]{1,0:T(8,128)(2,1)S(1)}, u32[]{:S(2)}, u32[]{:S(2)}) collective-permute-start(bf16[256,512]{1,0:T(8,128)(2,1)} %pad_maximum_fusion.1), channel_id=1, source_target_pairs={{0,8},{2,10},{4,12},{6,14},{8,0},{10,2},{12,4},{14,6},{16,24},{18,... | collective-permute-start | bytes 786440 | tf_op jit(solution)/shard_map/ppermute | solution.py:204
  48.7 23.1 %collective-permute-start.16 = (bf16[1040,256]{1,0:T(8,128)(2,1)}, bf16[1040,256]{1,0:T(8,128)(2,1)S(1)}, u32[]{:S(2)}, u32[]{:S(2)}) collective-permute-start(bf16[1040,256]{1,0:T(8,128)(2,1)} %get-tuple-element.36.kv_ref), channel_id=1, source_target_pairs={{0,2},{2,0},{4,6},{6,4},{8,10},{10,8},{12,14},{14,12},{16,18},{18,... | collective-permute-start | bytes 1597448 | tf_op jit(solution)/shard_map/ppermute | solution.py:204
  50.2 24.9 %collective-permute-start.15 = (bf16[1040,256]{1,0:T(8,128)(2,1)}, bf16[1040,256]{1,0:T(8,128)(2,1)S(1)}, u32[]{:S(2)}, u32[]{:S(2)}) collective-permute-start(bf16[1040,256]{1,0:T(8,128)(2,1)} %get-tuple-element.36.kv_ref), channel_id=1, source_target_pairs={{0,4},{2,6},{4,0},{6,2},{8,12},{10,14},{12,8},{14,10},{16,20},{18,... | collective-permute-start | bytes 1597448 | tf_op jit(solution)/shard_map/ppermute | solution.py:204
  51.7 25.0 %collective-permute-start.14 = (bf16[1040,256]{1,0:T(8,128)(2,1)}, bf16[1040,256]{1,0:T(8,128)(2,1)S(1)}, u32[]{:S(2)}, u32[]{:S(2)}) collective-permute-start(bf16[1040,256]{1,0:T(8,128)(2,1)} %get-tuple-element.36.kv_ref), channel_id=1, source_target_pairs={{0,6},{2,4},{4,2},{6,0},{8,14},{10,12},{12,10},{14,8},{16,22},{18,... | collective-permute-start | bytes 1597448 | tf_op jit(solution)/shard_map/ppermute | solution.py:204
  60.9 8.1 %collective-permute-start.12 = (bf16[256,512]{1,0:T(8,128)(2,1)S(1)}, bf16[256,512]{1,0:T(8,128)(2,1)S(1)}, u32[]{:S(2)}, u32[]{:S(2)}) collective-permute-start(bf16[256,512]{1,0:T(8,128)(2,1)S(1)} %collective-permute-done.11), channel_id=1, source_target_pairs={{0,8},{2,10},{4,12},{6,14},{8,0},{10,2},{12,4},{14,6},{16,24},{18,... | collective-permute-start | bytes 786440 | tf_op jit(solution)/shard_map/ppermute | solution.py:204
  69.0 1.0 %copy-start.1 = (bf16[1040,256]{1,0:T(8,128)(2,1)S(1)}, bf16[1040,256]{1,0:T(8,128)(2,1)}, u32[]{:S(2)}) copy-start(bf16[1040,256]{1,0:T(8,128)(2,1)} %get-tuple-element.36.kv_ref) | copy-start | bytes 1597444
  69.1 22.3 %collective-permute-start.13 = (bf16[512,512]{1,0:T(8,128)(2,1)S(1)}, bf16[512,512]{1,0:T(8,128)(2,1)S(1)}, u32[]{:S(2)}, u32[]{:S(2)}) collective-permute-start(bf16[512,512]{1,0:T(8,128)(2,1)S(1)} %get-tuple-element.47), channel_id=1, source_target_pairs={{0,1},{1,0},{2,3},{3,2},{4,5},{5,4},{6,7},{7,6},{8,9},{9,8},{10,11... | collective-permute-start | bytes 1572872 | tf_op jit(solution)/shard_map/ppermute | solution.py:214
  78.4 5.1 %collective-permute-start.17 = (bf16[256,256]{1,0:T(8,128)(2,1)S(1)}, bf16[256,256]{1,0:T(8,128)(2,1)S(1)}, u32[]{:S(2)}, u32[]{:S(2)}) collective-permute-start(bf16[256,256]{1,0:T(8,128)(2,1)S(1)} %get-tuple-element.42), channel_id=1, source_target_pairs={{0,8},{2,10},{4,12},{6,14},{8,0},{10,2},{12,4},{14,6},{16,24},{18,... | collective-permute-start | bytes 393224 | tf_op jit(solution)/shard_map/ppermute | solution.py:204
  78.8 11.1 %collective-permute-start.18 = (bf16[256,256]{1,0:T(8,128)(2,1)S(1)}, bf16[256,256]{1,0:T(8,128)(2,1)S(1)}, u32[]{:S(2)}, u32[]{:S(2)}) collective-permute-start(bf16[256,256]{1,0:T(8,128)(2,1)S(1)} %get-tuple-element.43), channel_id=1, source_target_pairs={{0,16},{2,18},{4,20},{6,22},{8,24},{10,26},{12,28},{14,30},{16,0},... | collective-permute-start | bytes 393224 | tf_op jit(solution)/shard_map/ppermute | solution.py:204
  80.4 9.5 %collective-permute-start.19 = (bf16[256,256]{1,0:T(8,128)(2,1)S(1)}, bf16[256,256]{1,0:T(8,128)(2,1)S(1)}, u32[]{:S(2)}, u32[]{:S(2)}) collective-permute-start(bf16[256,256]{1,0:T(8,128)(2,1)S(1)} %get-tuple-element.44), channel_id=1, source_target_pairs={{0,24},{2,26},{4,28},{6,30},{8,16},{10,18},{12,20},{14,22},{16,8},... | collective-permute-start | bytes 393224 | tf_op jit(solution)/shard_map/ppermute | solution.py:204
  82.9 7.6 %collective-permute-start.20 = (bf16[256,256]{1,0:T(8,128)(2,1)S(1)}, bf16[256,256]{1,0:T(8,128)(2,1)S(1)}, u32[]{:S(2)}, u32[]{:S(2)}) collective-permute-start(bf16[256,256]{1,0:T(8,128)(2,1)S(1)} %get-tuple-element.41.refs_0_), channel_id=1, source_target_pairs={{0,1},{1,0},{2,3},{3,2},{4,5},{5,4},{6,7},{7,6},{8,9},{9,8},{10,11... | collective-permute-start | bytes 393224 | tf_op jit(solution)/shard_map/ppermute | solution.py:214
  83.5 6.9 %collective-permute-start.21 = (bf16[256,256]{1,0:T(8,128)(2,1)S(1)}, bf16[256,256]{1,0:T(8,128)(2,1)S(1)}, u32[]{:S(2)}, u32[]{:S(2)}) collective-permute-start(bf16[256,256]{1,0:T(8,128)(2,1)S(1)} %collective-permute-done.17.refs_1_), channel_id=1, source_target_pairs={{0,1},{1,0},{2,3},{3,2},{4,5},{5,4},{6,7},{7,6},{8,9},{9,8},{10,11... | collective-permute-start | bytes 393224 | tf_op jit(solution)/shard_map/ppermute | solution.py:214
  89.9 1.3 %collective-permute-start.22 = (bf16[256,256]{1,0:T(8,128)(2,1)S(1)}, bf16[256,256]{1,0:T(8,128)(2,1)S(1)}, u32[]{:S(2)}, u32[]{:S(2)}) collective-permute-start(bf16[256,256]{1,0:T(8,128)(2,1)S(1)} %collective-permute-done.18.refs_2_), channel_id=1, source_target_pairs={{0,1},{1,0},{2,3},{3,2},{4,5},{5,4},{6,7},{7,6},{8,9},{9,8},{10,11... | collective-permute-start | bytes 393224 | tf_op jit(solution)/shard_map/ppermute | solution.py:214
  89.9 1.5 %collective-permute-start.23 = (bf16[256,256]{1,0:T(8,128)(2,1)S(1)}, bf16[256,256]{1,0:T(8,128)(2,1)S(1)}, u32[]{:S(2)}, u32[]{:S(2)}) collective-permute-start(bf16[256,256]{1,0:T(8,128)(2,1)S(1)} %collective-permute-done.19.refs_3_), channel_id=1, source_target_pairs={{0,1},{1,0},{2,3},{3,2},{4,5},{5,4},{6,7},{7,6},{8,9},{9,8},{10,11... | collective-permute-start | bytes 393224 | tf_op jit(solution)/shard_map/ppermute | solution.py:214

commit v3 on v2

v3 whole, which is shorter than its diff:
```python
import functools
import math

import jax
import jax.numpy as jnp
from jax import lax
from jax.experimental import pallas as pl
from jax.experimental.pallas import tpu as pltpu
from jax.sharding import PartitionSpec as P

EPSILON = 1e-05
PAD = 16
VMEM_LIMIT = 50 * 1024 * 1024
NT = (((1,), (1,)), ((), ()))


def half_silu(t):
    return t * (1.0 + jnp.tanh(t))


def normalise(x):
    centre = x - jnp.mean(x, axis=-1, keepdims=True)
    spread = jnp.mean(centre * centre, axis=-1, keepdims=True)
    return centre * lax.rsqrt(spread + EPSILON)


def onehot_rows(stamp_row, buckets):
    count = stamp_row.shape[1]
    level = lax.broadcasted_iota(jnp.int32, (buckets, count), 0).astype(jnp.float32)
    return jnp.where(level == stamp_row, 1.0, 0.0).T


def vmem(count):
    return [pl.BlockSpec(memory_space=pltpu.VMEM)] * count


def norm_kernel(ids, events, normed_ref, half_ref):
    half = half_ref.shape[0]
    normed_ref[...] = normalise(events[...].astype(jnp.float32)).astype(jnp.bfloat16)
    half_ref[...] = normed_ref[pl.ds(pl.multiple_of(ids[2] * half, half), half), :]


def gather_weights(lead, lines, a, i, weights, wbuf, slices):
    size = wbuf.shape[1] // len(slices)
    chunk = wbuf.shape[0] // (lead * lines)
    for j in range(lines):
        for k in range(lead):
            place = ((a ^ k) * lines + (i ^ j)) * chunk
            to = pl.ds(pl.multiple_of(place, chunk), chunk)
            for n, part in enumerate(slices):
                wbuf[to, n * size : (n + 1) * size] = weights[j][
                    k * chunk : (k + 1) * chunk, part * size : (part + 1) * size
                ]


def keys_kernel(lead, lines, ids, normed, own_msg, *refs):
    arrived, refs = refs[: lead - 1], refs[lead - 1 :]
    others, refs = refs[: lead - 1], refs[lead - 1 :]
    marks, refs = refs[: lead - 1], refs[lead - 1 :]
    weights, (kv_ref, all_ref, columns_ref, wbuf) = refs[:lines], refs[lines:]
    a, i, c = ids[0], ids[1], ids[2]
    rows = normed.shape[0]
    half = rows // 2
    size = wbuf.shape[1] // 2
    chunk = wbuf.shape[0] // (lead * lines)
    gather_weights(lead, lines, a, i, weights, wbuf, (3, 1))
    for j in range(lines):
        columns_ref[j * chunk : (j + 1) * chunk, :] = weights[j][lead * chunk :, :]
    all_ref[pl.ds(pl.multiple_of(a * rows, rows), rows), :] = normed[...]
    for k in range(1, lead):
        for side, block in ((c, arrived[k - 1]), (1 - c, others[k - 1])):
            place = (a ^ k) * rows + side * half
            all_ref[pl.ds(pl.multiple_of(place, half), half), :] = block[...]
    for p in range(lead):
        block = slice(p * rows, (p + 1) * rows)
        product = jnp.dot(all_ref[block, :], wbuf[...], preferred_element_type=jnp.float32)
        kv_ref[block, :] = half_silu(0.5 * product).astype(jnp.bfloat16)
    stamp_rows = lax.broadcasted_iota(jnp.int32, (PAD, rows), 0)
    stamp_tile = jnp.zeros((PAD, rows), jnp.float32)
    for k, ref in enumerate((own_msg, *marks)):
        mark = ref[chunk : chunk + PAD, :rows].astype(jnp.float32)[0:1, :]
        stamp_tile = jnp.where(stamp_rows == (a ^ k), mark, stamp_tile)
    kv_ref[lead * rows :, :] = stamp_tile.astype(jnp.bfloat16)


def queries_kernel(lead, lines, ids, normed_all, time_bias, kv_ref, *refs):
    weights, (q_ref, *gate_refs, wbuf, ubuf) = refs[:lines], refs[lines:]
    a, i = ids[0], ids[1]
    size = wbuf.shape[1] // 2
    buckets = time_bias.shape[1]
    chunk = wbuf.shape[0] // (lead * lines)
    rows = normed_all.shape[0] // lead
    gather_weights(lead, lines, a, i, weights, wbuf, (2, 0))
    bias = time_bias[...].astype(jnp.float32) * 0.5
    picked = lax.broadcasted_iota(jnp.int32, bias.shape, 0) == a
    bias = jnp.sum(jnp.where(picked, bias, 0.0), axis=0, keepdims=True)
    table = jnp.broadcast_to(bias, (buckets, buckets))
    table = pltpu.roll(table, 0, 1, stride=1, stride_axis=0).astype(jnp.bfloat16)
    marks = kv_ref[lead * rows :, :].astype(jnp.float32)
    scale = 0.5 / math.sqrt(size)
    for p in range(lead):
        block = slice(p * rows, (p + 1) * rows)
        product = jnp.dot(normed_all[block, :], wbuf[...], preferred_element_type=jnp.float32)
        active = half_silu(0.5 * product)
        q_ref[block, :size] = (active[:, :size] * scale).astype(jnp.bfloat16)
        ubuf[block, :] = active[:, size:].astype(jnp.bfloat16)
        chosen = onehot_rows(marks[p : p + 1, :], buckets).astype(jnp.bfloat16)
        q_ref[block, size:] = lax.dot_general(
            chosen, table, NT, preferred_element_type=jnp.float32
        ).astype(jnp.bfloat16)
    for k in range(lead):
        gate_refs[k][...] = ubuf[pl.ds(pl.multiple_of((a ^ k) * rows, rows), rows), :]


def attention_kernel(lead, j, last, pieces, ids, q_ref, *refs):
    refs = list(refs)
    kv_refs, refs = refs[:pieces], refs[pieces:]
    before = refs.pop(0) if j > 0 else None
    gates, refs = (refs[:lead], refs[lead:]) if last else ([], refs)
    outs, (kaug, values, total) = refs[:-3], refs[-3:]
    a, i = ids[0], ids[1]
    size = q_ref.shape[1] // 2
    rows = q_ref.shape[0] // lead
    buckets = q_ref.shape[1] - size
    span = lead * rows // pieces
    for n, ref in enumerate(kv_refs):
        kaug[n * span : (n + 1) * span, :size] = ref[:span, :size]
        if pieces > 1:
            values[n * span : (n + 1) * span, :] = ref[:span, size:]
    marks = kv_refs[-1][span:, :].astype(jnp.float32)
    for p in range(lead):
        kaug[p * rows : (p + 1) * rows, size:] = onehot_rows(marks[p : p + 1, :], buckets).astype(
            jnp.bfloat16
        )

    def visit(extra):
        for p in range(lead):
            block = slice(p * rows, (p + 1) * rows)
            count = (p + extra) * rows
            old = before[block, :] if before is not None else None
            if count == 0:
                total[block, :] = old if old is not None else jnp.zeros((rows, size), jnp.float32)
                continue
            t = lax.dot_general(
                q_ref[block, :], kaug[:count, :], NT, preferred_element_type=jnp.float32
            )
            weight = half_silu(t)
            if j == 0:
                row = lax.broadcasted_iota(jnp.int32, (rows, count), 0) + p * rows
                column = lax.broadcasted_iota(jnp.int32, (rows, count), 1)
                weight = jnp.where(column <= row, weight, 0.0)
            update = jnp.dot(
                weight.astype(jnp.bfloat16),
                values[:count, :] if pieces > 1 else kv_refs[0][:count, size:],
                preferred_element_type=jnp.float32,
            )
            total[block, :] = update if old is None else old + update

    if j == 0:
        visit(1)
    else:
        pl.when((i ^ j) < i)(lambda: visit(1))
        pl.when((i ^ j) > i)(lambda: visit(0))
    if last:
        for k in range(lead):
            base = pl.ds(pl.multiple_of((a ^ k) * rows, rows), rows)
            outs[k][:, :size] = total[base, :].astype(jnp.bfloat16)
            outs[k][:, size:] = gates[k][...]
    else:
        outs[0][...] = total[...]


def parcel_kernel(lead, ids, *refs):
    columns, (kept_ref, give_ref) = refs[:lead], refs[lead:]
    height = columns[0].shape[0]

    def place(low_ref, high_ref):
        for n in range(lead // 2):
            low_ref[n * height : (n + 1) * height, :] = columns[n][...]
            high_ref[n * height : (n + 1) * height, :] = columns[lead // 2 + n][...]

    mine = ids[0] // (lead // 2) == ids[2]
    pl.when(mine)(lambda: place(kept_ref, give_ref))
    pl.when(jnp.logical_not(mine))(lambda: place(give_ref, kept_ref))


def output_kernel(lead, lines, ids, events, kept, given, *refs):
    own, refs = refs[:lead], refs[lead:]
    other, refs = refs[:lead], refs[lead:]
    out_ref, gated, wbuf = refs
    a, i, c = ids[0], ids[1], ids[2]
    rows, share = out_ref.shape
    size = own[0].shape[1] // 2
    full = 2 * lead * size
    chunk = kept.shape[0] // (2 * lines)
    for k in range(2):
        for j in range(lines):
            place = (((a ^ k) & 1) * lines + (i ^ j)) * chunk
            source = slice((k * lines + j) * chunk, (k * lines + j + 1) * chunk)
            to = pl.ds(pl.multiple_of(place, chunk), chunk)
            wbuf[0, to, :] = kept[source, :]
            wbuf[1, to, :] = given[source, :]
    parts = [ref[:, :size].astype(jnp.float32) for ref in (*own, *other)]
    middle = functools.reduce(jnp.add, [jnp.sum(x, -1, keepdims=True) for x in parts]) / full
    parts = [x - middle for x in parts]
    spread = functools.reduce(jnp.add, [jnp.sum(x * x, -1, keepdims=True) for x in parts]) / full
    inverse = lax.rsqrt(spread + EPSILON)
    for side, group in enumerate((own, other)):
        for k in range(lead):
            value = parts[side * lead + k] * inverse * group[k][:, size:].astype(jnp.float32)
            place = pl.ds(pl.multiple_of((a ^ k) * size, size), size)
            gated[side, :, place] = value.astype(jnp.bfloat16)
    total = lax.dot_general(gated[0], wbuf[0], NT, preferred_element_type=jnp.float32)
    total += lax.dot_general(gated[1], wbuf[1], NT, preferred_element_type=jnp.float32)
    residual = events[:, pl.ds(pl.multiple_of(c * share, share), share)].astype(jnp.float32)
    out_ref[...] = (residual + total).astype(jnp.bfloat16)


def call(kernel, ins, outs, scratch):
    return list(pl.pallas_call(
        kernel,
        out_shape=outs,
        in_specs=[pl.BlockSpec(memory_space=pltpu.SMEM)] + vmem(len(ins) - 1),
        out_specs=vmem(len(outs)),
        scratch_shapes=scratch,
        compiler_params=pltpu.CompilerParams(vmem_limit_bytes=VMEM_LIMIT),
        cost_estimate=pl.CostEstimate(flops=1, bytes_accessed=1, transcendentals=0),
    )(*ins))


def per_device(events, w_uvqk, w_out, time_bias, stamps):
    bf16, f32 = jnp.bfloat16, jnp.float32
    devices = lax.axis_size("seq")
    rows, width = events.shape
    lead = time_bias.shape[0]
    lines = devices // lead
    chunk = w_uvqk.shape[0]
    size = w_uvqk.shape[2] // lead
    share = width // lax.axis_size("head")
    half = rows // 2
    place, c = lax.axis_index("seq"), lax.axis_index("head")
    a, i = place // lines, place % lines
    ids = jnp.stack([a, i, c]).astype(jnp.int32)

    def exchange(x, flip):
        return lax.ppermute(x, "seq", [(t, t ^ flip) for t in range(devices)])

    def swap(x):
        return lax.ppermute(x, "head", [(0, 1), (1, 0)])

    def shape(*dims, dtype=bf16):
        return jax.ShapeDtypeStruct(dims, dtype)

    by_head = w_uvqk.reshape(chunk, 4, lead, size).transpose(2, 0, 1, 3).reshape(lead, chunk, -1)
    stamp_rows = jnp.pad(stamps.astype(bf16)[None, :], ((0, PAD - 1), (0, 4 * size - rows)))
    sent = [
        jnp.concatenate([lax.dynamic_index_in_dim(by_head, a ^ k, 0, False), stamp_rows])
        for k in range(lead)
    ]
    got = [exchange(sent[k], k * lines) for k in range(1, lead)]
    normed, own_half = call(
        norm_kernel,
        [ids, events],
        [shape(rows, width), shape(half, width)],
        [],
    )
    own_half, got[0] = lax.optimization_barrier((own_half, got[0]))
    near, far = exchange(own_half, lines), exchange(own_half, 2 * lines)
    near, relayed = lax.optimization_barrier((near, far))
    arrived = [near, far, exchange(relayed, lines)]
    stack = jnp.concatenate([x[:chunk] for x in [sent[0], *got]] + [w_out.T])
    stacks = [stack] + [exchange(stack, j) for j in range(1, lines)]
    others = [swap(x) for x in arrived[:-1]]
    *stacks[1:], last_half = lax.optimization_barrier((*stacks[1:], arrived[-1]))
    arrived[-1] = last_half
    others.append(swap(last_half))

    span = lead * rows
    kv, normed_all, columns = call(
        functools.partial(keys_kernel, lead, lines),
        [ids, normed, sent[0], *arrived, *others, *got, *stacks],
        [shape(span + PAD, 2 * size), shape(span, width), shape(lines * chunk, w_out.shape[0])],
        [pltpu.VMEM((width, 2 * size), bf16)],
    )
    direct = [exchange(kv, j) for j in ((1, 2) if lines == 4 else range(1, lines))]
    near, far = exchange(columns, lines), exchange(columns, 2 * lines)
    queries, *gates = call(
        functools.partial(queries_kernel, lead, lines),
        [ids, normed_all, time_bias, kv, *stacks],
        [shape(span, size + time_bias.shape[1])] + [shape(rows, size)] * lead,
        [pltpu.VMEM((width, 2 * size), bf16), pltpu.VMEM((span, size), bf16)],
    )

    def attend(j, total):
        last = j == lines - 1
        outs = [shape(rows, 2 * size)] * lead if last else [shape(span, size, dtype=f32)]
        return call(
            functools.partial(attention_kernel, lead, j, last, len(kvs[j])),
            [ids, queries, *kvs[j]] + ([total] if j else []) + (gates if last else []),
            outs,
            [
                pltpu.VMEM((span, queries.shape[1]), bf16),
                pltpu.VMEM((span, size), bf16),
                pltpu.VMEM((span, size), f32),
            ],
        )

    kvs = [[kv]] + [[x] for x in direct]
    result = attend(0, None)
    *direct, far, near, result[0] = lax.optimization_barrier((*direct, far, near, result[0]))
    kvs = [[kv]] + [[x] for x in direct]
    if lines == 4:
        part = span // 2
        kvs.append([exchange(direct[1][:part], 1), exchange(direct[0][part:], 2)])
    relayed = exchange(far, lines)
    for j in range(1, lines):
        result = attend(j, result[0])
    relayed, result[0] = lax.optimization_barrier((relayed, result[0]))
    own = [result[0]] + [exchange(result[k], k * lines) for k in range(1, lead)]
    across = [swap(x) for x in own]
    parcel = shape(2 * lines * chunk, w_out.shape[0])
    kept, given = call(
        functools.partial(parcel_kernel, lead),
        [ids, columns, near, far, relayed],
        [parcel, parcel],
        [],
    )
    given = swap(given)
    return call(
        functools.partial(output_kernel, lead, lines),
        [ids, events, kept, given, *own, *across],
        [shape(rows, share)],
        [
            pltpu.VMEM((2, rows, lead * size), bf16),
            pltpu.VMEM((2, share, lead * size), bf16),
        ],
    )[0]


def solution(mesh):
    placed = (P("seq", None), P("seq", None, "head"), P("head", "seq"), P("head", None), P("seq"))
    return jax.shard_map(
        per_device, mesh=mesh, in_specs=placed, out_specs=P("seq", "head"), check_vma=False
    )
```

time: 94.3 us -> 82 us (0.87)
  waiting for transfers between devices: 46.4 us -> 39.6 us
  starting transfers between devices: 26.5 us -> 23.1 us
  local copies, waits for them, and re-layouts: 4.97 us -> 2.42 us
  Pallas kernels: 13.2 us -> 15.6 us
  other arithmetic: 2.56 us -> 0.84 us
    ppermute x18 -> x19, waiting for transfers between devices: 45 us -> 37 us  [exchange(): return lax.ppermute(x, 'seq', [(t, t ^ flip) for t in range(devices)])]
    ppermute x18 -> x19, starting transfers between devices: 26 us -> 22.1 us  [exchange(): return lax.ppermute(x, 'seq', [(t, t ^ flip) for t in range(devices)])]
    pallas_call x6 -> x9, Pallas kernels: 13.2 us -> 15.6 us  [call(): pl.pallas_call(kernel, out_shape=outs, in_specs=[pl.BlockSpec(memory_spac...]
    concatenate x3 -> x0, other arithmetic: 2.37 us -> none  [the longest x1 0.94 us: per_device(): other = swap(jnp.concatenate(arrived))]
    unnamed x20 -> x14, local copies, waits for them, and re-layouts: 2.9 us -> 1.09 us
    ppermute x6 -> x8, waiting for transfers between devices: 1.38 us -> 2.55 us  [swap(): return lax.ppermute(x, 'head', [(0, 1), (1, 0)])]
  transfers between devices with their start and end apart: 24 -> 27, of which waited for: 12 -> 14; matrix products, arithmetic and copies ran while one was open for 4% -> 0% of each run, Pallas kernels for 7% -> 12%
where the time goes in v3:
time: 82 us; the launch traced here: 81.8 us
  waiting for transfers between devices  39.6 us (48%)
  starting transfers between devices  23.1 us (28%)
  Pallas kernels  15.6 us (19%)
  local copies, waits for them, and re-layouts  2.42 us (3%)
  other arithmetic  0.84 us (1%)
    ppermute x19, waiting for transfers between devices, exchange(): return lax.ppermute(x, 'seq', [(t, t ^ flip) for t in range(devices)])  37 us
    ppermute x19, starting transfers between devices, exchange(): return lax.ppermute(x, 'seq', [(t, t ^ flip) for t in range(devices)])  22.1 us
    pallas_call x9, Pallas kernels, call(): pl.pallas_call(kernel, out_shape=outs, in_specs=[pl.BlockSpec(memory_spac...  15.6 us
    ppermute x8, waiting for transfers between devices, swap(): return lax.ppermute(x, 'head', [(0, 1), (1, 0)])  2.55 us
  transfers between devices with their start and end apart: 27, of which 14 were waited for; matrix products, arithmetic and copies ran while one was open for 0% of the time, Pallas kernels for 12%

profile of v3, /device:TPU:0, one launch (start us, length us, event | category | flops | bytes accessed | tf_op | source)
XLA Modules:
  0.0 81.8 jit_solution(8067570875296269135)
XLA Ops:
  0.0 0.7 convert_element_type.5
  0.8 1.1 %reshape.6 = bf16[64,4,4,128]{3,2,1,0:T(4,128)(2,1)S(1)} reshape(bf16[64,4,512]{2,1,0:T(4,128)(2,1)} %param.6) | data formatting | bytes 524288 | tf_op jit(solution)/shard_map/reshape | solution.py:254
  1.8 0.1 copy.6
  1.9 0.1 reshape.7
  2.1 5.1 %collective-permute-start.4 = (bf16[80,512]{1,0:T(8,128)(2,1)S(1)}, bf16[80,512]{1,0:T(8,128)(2,1)S(1)}, u32[]{:S(2)}, u32[]{:S(2)}) collective-permute-start(bf16[80,512]{1,0:T(8,128)(2,1)S(1)} %get-tuple-element.72), channel_id=1, source_target_pairs={{0,24},{2,26},{4,28},{6,30},{8,16},{10,18},{12,20},{14,22},{16,8},... | collective-permute-start | bytes 245768 | tf_op jit(solution)/shard_map/ppermute | solution.py:246
  7.3 0.0 collective-permute-start
  7.3 0.6 collective-permute-start.3
  7.9 0.1 pad_add_fusion.ids
  8.0 0.9 %shard_map.55 = (bf16[256,1024]{1,0:T(8,128)(2,1)S(1)}, bf16[128,1024]{1,0:T(8,128)(2,1)S(1)}) custom-call(s32[3]{0:T(128)S(1)} %pad_add_fusion.ids, bf16[256,1024]{1,0:T(8,128)(2,1)S(1)} %copy-done.2), custom_call_target="tpu_custom_call" | custom-call | flops 1 | bytes 1 | tf_op jit(solution)/shard_map/pallas_call | solution.py:220
  8.9 4.6 %collective-permute-done.refs_6_ = bf16[80,512]{1,0:T(8,128)(2,1)S(1)} collective-permute-done((bf16[80,512]{1,0:T(8,128)(2,1)S(1)}, bf16[80,512]{1,0:T(8,128)(2,1)S(1)}, u32[]{:S(2)}, u32[]{:S(2)}) %collective-permute-start) | collective-permute-done | bytes 81952 | tf_op jit(solution)/shard_map/ppermute | solution.py:246
  13.5 0.0 collective-permute-start.2
  13.5 1.3 %collective-permute-start.1 = (bf16[128,1024]{1,0:T(8,128)(2,1)S(1)}, bf16[128,1024]{1,0:T(8,128)(2,1)S(1)}, u32[]{:S(2)}, u32[]{:S(2)}) collective-permute-start(bf16[128,1024]{1,0:T(8,128)(2,1)S(1)} %get-tuple-element.38), channel_id=1, source_target_pairs={{0,8},{2,10},{4,12},{6,14},{8,0},{10,2},{12,4},{14,6},{16,24},{18,... | collective-permute-start | bytes 786440 | tf_op jit(solution)/shard_map/ppermute | solution.py:246
  14.8 0.0 collective-permute-done.3.refs_7_
  14.8 0.0 collective-permute-done.4.refs_8_
  14.9 2.8 %collective-permute-start.7 = (bf16[320,512]{1,0:T(8,128)(2,1)S(1)}, bf16[320,512]{1,0:T(8,128)(2,1)S(1)}, u32[]{:S(2)}, u32[]{:S(2)}) collective-permute-start(bf16[320,512]{1,0:T(8,128)(2,1)S(1)} %bitcast_dynamic-update-slice_fusion.refs_9_.refs_0_), channel_id=1, source_target_pairs={{0,6},{2,4},{4,2},{6,0},{8,14},{10,12},{12,10},{14,8},{16,22},{18,... | collective-permute-start | bytes 983048 | tf_op jit(solution)/shard_map/ppermute | solution.py:246
  17.7 0.5 collective-permute-start.6
  18.2 0.2 collective-permute-start.5
  18.4 7.6 %collective-permute-done.2.refs_1_ = bf16[128,1024]{1,0:T(8,128)(2,1)S(1)} collective-permute-done((bf16[128,1024]{1,0:T(8,128)(2,1)S(1)}, bf16[128,1024]{1,0:T(8,128)(2,1)S(1)}, u32[]{:S(2)}, u32[]{:S(2)}) %collective-permute-start.2) | collective-permute-done | bytes 262176 | tf_op jit(solution)/shard_map/ppermute | solution.py:246
  26.0 0.0 collective-permute-done.1.refs_0_
  26.0 0.2 collective-permute-start.8
  26.2 0.0 collective-permute-start.9
  26.2 0.1 collective-permute-done.7.refs_12_.refs_3_
  26.3 0.4 collective-permute-start.10
  26.7 3.0 %collective-permute-done.6.refs_11_.refs_2_ = bf16[320,512]{1,0:T(8,128)(2,1)S(1)} collective-permute-done((bf16[320,512]{1,0:T(8,128)(2,1)S(1)}, bf16[320,512]{1,0:T(8,128)(2,1)S(1)}, u32[]{:S(2)}, u32[]{:S(2)}) %collective-permute-start.6) | collective-permute-done | bytes 327712 | tf_op jit(solution)/shard_map/ppermute | solution.py:246
  29.7 0.3 collective-permute-done.5.refs_10_.refs_1_
  30.0 4.0 %collective-permute-done.8.refs_2_ = bf16[128,1024]{1,0:T(8,128)(2,1)S(1)} collective-permute-done((bf16[128,1024]{1,0:T(8,128)(2,1)S(1)}, bf16[128,1024]{1,0:T(8,128)(2,1)S(1)}, u32[]{:S(2)}, u32[]{:S(2)}) %collective-permute-start.8) | collective-permute-done | bytes 262176 | tf_op jit(solution)/shard_map/ppermute | solution.py:246
  34.0 0.0 collective-permute-start.11
  34.0 0.0 collective-permute-done.10.refs_4_
  34.0 0.0 collective-permute-done.9.refs_3_
  34.0 1.5 %collective-permute-done.11.refs_5_ = bf16[128,1024]{1,0:T(8,128)(2,1)S(1)} collective-permute-done((bf16[128,1024]{1,0:T(8,128)(2,1)S(1)}, bf16[128,1024]{1,0:T(8,128)(2,1)S(1)}, u32[]{:S(2)}, u32[]{:S(2)}) %collective-permute-start.11) | collective-permute-done | bytes 262176 | tf_op jit(solution)/shard_map/ppermute | solution.py:249
  35.5 2.3 %shard_map.56 = (bf16[1040,256]{1,0:T(8,128)(2,1)}, bf16[1024,1024]{1,0:T(8,128)(2,1)}, bf16[256,512]{1,0:T(8,128)(2,1)S(1)}) custom-call(s32[3]{0:T(128)S(1)} %pad_add_fusion.ids, bf16[256,1024]{1,0:T(8,128)(2,1)S(1)} %get-tuple-element.36.normed, bf16[80,512]{1,0:T(8,128)(2,1)S(1)} %get-tuple-element.73.own_msg, ...), custom_call_target="tpu_custom_call" | custom-call | flops 1 | bytes 1 | tf_op jit(solution)/shard_map/pallas_call | solution.py:220
  37.9 1.4 %collective-permute-start.13 = (bf16[1040,256]{1,0:T(8,128)(2,1)}, bf16[1040,256]{1,0:T(8,128)(2,1)S(1)}, u32[]{:S(2)}, u32[]{:S(2)}) collective-permute-start(bf16[1040,256]{1,0:T(8,128)(2,1)} %get-tuple-element.47.kv_ref.refs_0_), channel_id=1, source_target_pairs={{0,4},{2,6},{4,0},{6,2},{8,12},{10,14},{12,8},{14,10},{16,20},{18,... | collective-permute-start | bytes 1597448 | tf_op jit(solution)/shard_map/ppermute | solution.py:246
  39.2 1.5 %collective-permute-start.12 = (bf16[1040,256]{1,0:T(8,128)(2,1)}, bf16[1040,256]{1,0:T(8,128)(2,1)S(1)}, u32[]{:S(2)}, u32[]{:S(2)}) collective-permute-start(bf16[1040,256]{1,0:T(8,128)(2,1)} %get-tuple-element.47.kv_ref.refs_0_), channel_id=1, source_target_pairs={{0,2},{2,0},{4,6},{6,4},{8,10},{10,8},{12,14},{14,12},{16,18},{18,... | collective-permute-start | bytes 1597448 | tf_op jit(solution)/shard_map/ppermute | solution.py:246
  40.7 0.3 collective-permute-start.15
  41.0 2.4 %collective-permute-start.14 = (bf16[256,512]{1,0:T(8,128)(2,1)S(1)}, bf16[256,512]{1,0:T(8,128)(2,1)S(1)}, u32[]{:S(2)}, u32[]{:S(2)}) collective-permute-start(bf16[256,512]{1,0:T(8,128)(2,1)S(1)} %get-tuple-element.46.refs_0_), channel_id=1, source_target_pairs={{0,16},{2,18},{4,20},{6,22},{8,24},{10,26},{12,28},{14,30},{16,0},... | collective-permute-start | bytes 786440 | tf_op jit(solution)/shard_map/ppermute | solution.py:246
  43.4 1.0 %copy-done = bf16[1040,256]{1,0:T(8,128)(2,1)S(1)} copy-done((bf16[1040,256]{1,0:T(8,128)(2,1)S(1)}, bf16[1040,256]{1,0:T(8,128)(2,1)}, u32[]{:S(2)}) %copy-start) | copy-done | bytes 532504
  44.5 2.6 %shard_map.57 = (bf16[1024,256]{1,0:T(8,128)(2,1)S(1)}, bf16[256,128]{1,0:T(8,128)(2,1)S(1)}, bf16[256,128]{1,0:T(8,128)(2,1)S(1)}, bf16[256,128]{1,0:T(8,128)(2,1)S(1)}, bf16[256,128]{1,0:T(8,128)(2,1)S(1)}) custom-call(s32[3]{0:T(128)S(1)} %pad_add_fusion.ids, bf16[1024,1024]{1,0:T(8,128)(2,1)} %get-tuple-element.48.normed_all, ...), custom_call_target="tpu_custom_call" | custom-call | flops 1 | bytes 1 | tf_op jit(solution)/shard_map/pallas_call | solution.py:220
  47.1 1.8 %shard_map.58.refs_1_ = f32[1024,128]{1,0:T(8,128)S(1)} custom-call(s32[3]{0:T(128)S(1)} %pad_add_fusion.ids, bf16[1024,256]{1,0:T(8,128)(2,1)S(1)} %get-tuple-element.49.q_ref, bf16[1040,256]{1,0:T(8,128)(2,1)S(1)} %copy-done.1), custom_call_target="tpu_custom_call" | custom-call | flops 1 | bytes 1 | tf_op jit(solution)/shard_map/pallas_call | solution.py:220
  48.9 4.8 %collective-permute-done.15.refs_1_ = bf16[256,512]{1,0:T(8,128)(2,1)S(1)} collective-permute-done((bf16[256,512]{1,0:T(8,128)(2,1)S(1)}, bf16[256,512]{1,0:T(8,128)(2,1)S(1)}, u32[]{:S(2)}, u32[]{:S(2)}) %collective-permute-start.15) | collective-permute-done | bytes 262176 | tf_op jit(solution)/shard_map/ppermute | solution.py:246
  53.7 1.4 %collective-permute-done.14.refs_2_ = bf16[256,512]{1,0:T(8,128)(2,1)S(1)} collective-permute-done((bf16[256,512]{1,0:T(8,128)(2,1)S(1)}, bf16[256,512]{1,0:T(8,128)(2,1)S(1)}, u32[]{:S(2)}, u32[]{:S(2)}) %collective-permute-start.14) | collective-permute-done | bytes 262176 | tf_op jit(solution)/shard_map/ppermute | solution.py:246
  55.1 0.0 collective-permute-done.13.refs_0_
  55.1 0.0 collective-permute-done.12.refs_0_
  55.1 0.6 collective-permute-start.18
  55.7 0.8 collective-permute-start.17
  56.5 0.0 collective-permute-start.16
  56.5 1.6 %shard_map.59.refs_1_ = f32[1024,128]{1,0:T(8,128)S(1)} custom-call(s32[3]{0:T(128)S(1)} %pad_add_fusion.ids, bf16[1024,256]{1,0:T(8,128)(2,1)S(1)} %get-tuple-element.49.q_ref, bf16[1040,256]{1,0:T(8,128)(2,1)S(1)} %collective-permute-done.12.refs_0_, f32[1024,128]{1,0:T(8,128)S(1)} %shard_map.58.refs_1_), custom_call_target="tpu_custom_call" | custom-call | flops 1 | bytes 1 | tf_op jit(solution)/shard_map/pallas_call | solution.py:220
  58.1 1.6 %shard_map.60.refs_2_ = f32[1024,128]{1,0:T(8,128)S(1)} custom-call(s32[3]{0:T(128)S(1)} %pad_add_fusion.ids, bf16[1024,256]{1,0:T(8,128)(2,1)S(1)} %get-tuple-element.49.q_ref, bf16[1040,256]{1,0:T(8,128)(2,1)S(1)} %collective-permute-done.13.refs_0_, f32[1024,128]{1,0:T(8,128)S(1)} %shard_map.59.refs_1_), custom_call_target="tpu_custom_call" | custom-call | flops 1 | bytes 1 | tf_op jit(solution)/shard_map/pallas_call | solution.py:220
  59.7 2.4 %collective-permute-done.17.refs_0_ = bf16[512,256]{1,0:T(8,128)(2,1)S(1)} collective-permute-done((bf16[512,256]{1,0:T(8,128)(2,1)S(1)}, bf16[512,256]{1,0:T(8,128)(2,1)S(1)}, u32[]{:S(2)}, u32[]{:S(2)}) %collective-permute-start.17) | collective-permute-done | bytes 262176 | tf_op jit(solution)/shard_map/ppermute | solution.py:246
  62.1 0.0 collective-permute-done.18.refs_1_
  62.1 1.7 %shard_map.61 = (bf16[256,256]{1,0:T(8,128)(2,1)S(1)}, bf16[256,256]{1,0:T(8,128)(2,1)S(1)}, bf16[256,256]{1,0:T(8,128)(2,1)S(1)}, bf16[256,256]{1,0:T(8,128)(2,1)S(1)}) custom-call(s32[3]{0:T(128)S(1)} %pad_add_fusion.ids, bf16[1024,256]{1,0:T(8,128)(2,1)S(1)} %get-tuple-element.49.q_ref, bf16[512,256]{1,0:T(8,128)(2,1)S(1)} %collective-permute-done.17.refs_0_, ...), custom_call_target="tpu_custom_call" | custom-call | flops 1 | bytes 1 | tf_op jit(solution)/shard_map/pallas_call | solution.py:220
  63.8 0.6 shard_map.62
  64.5 0.1 collective-permute-start.19
  64.5 0.3 collective-permute-start.20
  64.8 2.4 %collective-permute-start.21 = (bf16[256,256]{1,0:T(8,128)(2,1)S(1)}, bf16[256,256]{1,0:T(8,128)(2,1)S(1)}, u32[]{:S(2)}, u32[]{:S(2)}) collective-permute-start(bf16[256,256]{1,0:T(8,128)(2,1)S(1)} %get-tuple-element.65), channel_id=1, source_target_pairs={{0,16},{2,18},{4,20},{6,22},{8,24},{10,26},{12,28},{14,30},{16,0},... | collective-permute-start | bytes 393224 | tf_op jit(solution)/shard_map/ppermute | solution.py:246
  67.3 1.7 %collective-permute-start.22 = (bf16[256,256]{1,0:T(8,128)(2,1)S(1)}, bf16[256,256]{1,0:T(8,128)(2,1)S(1)}, u32[]{:S(2)}, u32[]{:S(2)}) collective-permute-start(bf16[256,256]{1,0:T(8,128)(2,1)S(1)} %get-tuple-element.66), channel_id=1, source_target_pairs={{0,24},{2,26},{4,28},{6,30},{8,16},{10,18},{12,20},{14,22},{16,8},... | collective-permute-start | bytes 393224 | tf_op jit(solution)/shard_map/ppermute | solution.py:246
  69.0 0.0 collective-permute-start.23
  69.0 3.7 %collective-permute-done.20.refs_1_ = bf16[256,256]{1,0:T(8,128)(2,1)S(1)} collective-permute-done((bf16[256,256]{1,0:T(8,128)(2,1)S(1)}, bf16[256,256]{1,0:T(8,128)(2,1)S(1)}, u32[]{:S(2)}, u32[]{:S(2)}) %collective-permute-start.20) | collective-permute-done | bytes 131104 | tf_op jit(solution)/shard_map/ppermute | solution.py:246
  72.6 5.1 %collective-permute-done.21.refs_2_ = bf16[256,256]{1,0:T(8,128)(2,1)S(1)} collective-permute-done((bf16[256,256]{1,0:T(8,128)(2,1)S(1)}, bf16[256,256]{1,0:T(8,128)(2,1)S(1)}, u32[]{:S(2)}, u32[]{:S(2)}) %collective-permute-start.21) | collective-permute-done | bytes 131104 | tf_op jit(solution)/shard_map/ppermute | solution.py:246
  77.8 0.5 collective-permute-start.26
  78.3 0.0 collective-permute-done.24.refs_5_
  78.3 0.8 %collective-permute-done.25.refs_6_ = bf16[256,256]{1,0:T(8,128)(2,1)S(1)} collective-permute-done((bf16[256,256]{1,0:T(8,128)(2,1)S(1)}, bf16[256,256]{1,0:T(8,128)(2,1)S(1)}, u32[]{:S(2)}, u32[]{:S(2)}) %collective-permute-start.25) | collective-permute-done | bytes 131104 | tf_op jit(solution)/shard_map/ppermute | solution.py:249
  79.1 0.2 collective-permute-done.26.refs_7_
  79.3 0.0 collective-permute-done.19.given
  79.3 2.5 %shard_map.63 = bf16[256,512]{1,0:T(8,128)(2,1)} custom-call(s32[3]{0:T(128)S(1)} %pad_add_fusion.ids, bf16[256,1024]{1,0:T(8,128)(2,1)S(1)} %copy-done.2, bf16[512,512]{1,0:T(8,128)(2,1)S(1)} %get-tuple-element.61.kept, bf16[512,512]{1,0:T(8,128)(2,1)S(1)} %collective-permute-done.19.given, bf16[256,256]{1,0:T(8,128)(2,1)S(1)} %get-tuple-element.63.refs_0_, ...), custom_call_target="tpu_custom_call" | custom-call | flops 1 | bytes 1 | tf_op jit(solution)/shard_map/pallas_call | solution.py:220
  (24 shorter events, 0.2 us)
Async XLA Ops:
  0.0 8.0 %copy-start.2 = (bf16[256,1024]{1,0:T(8,128)(2,1)S(1)}, bf16[256,1024]{1,0:T(8,128)(2,1)}, u32[]{:S(2)}) copy-start(bf16[256,1024]{1,0:T(8,128)(2,1)} %events.3) | copy-start | bytes 1572868
  0.0 14.8 %copy-start.4 = (bf16[512,64]{0,1:T(8,128)(2,1)S(1)}, bf16[512,64]{0,1:T(8,128)(2,1)}, u32[]{:S(2)}) copy-start(bf16[512,64]{0,1:T(8,128)(2,1)} %param.7) | copy-start | bytes 196612
  2.1 12.7 %collective-permute-start.4 = (bf16[80,512]{1,0:T(8,128)(2,1)S(1)}, bf16[80,512]{1,0:T(8,128)(2,1)S(1)}, u32[]{:S(2)}, u32[]{:S(2)}) collective-permute-start(bf16[80,512]{1,0:T(8,128)(2,1)S(1)} %get-tuple-element.72), channel_id=1, source_target_pairs={{0,24},{2,26},{4,28},{6,30},{8,16},{10,18},{12,20},{14,22},{16,8},... | collective-permute-start | bytes 245768 | tf_op jit(solution)/shard_map/ppermute | solution.py:246
  7.3 6.2 %collective-permute-start = (bf16[80,512]{1,0:T(8,128)(2,1)S(1)}, bf16[80,512]{1,0:T(8,128)(2,1)S(1)}, u32[]{:S(2)}, u32[]{:S(2)}) collective-permute-start(bf16[80,512]{1,0:T(8,128)(2,1)S(1)} %get-tuple-element.74), channel_id=1, source_target_pairs={{0,8},{2,10},{4,12},{6,14},{8,0},{10,2},{12,4},{14,6},{16,24},{18,... | collective-permute-start | bytes 245768 | tf_op jit(solution)/shard_map/ppermute | solution.py:246
  7.3 7.5 %collective-permute-start.3 = (bf16[80,512]{1,0:T(8,128)(2,1)S(1)}, bf16[80,512]{1,0:T(8,128)(2,1)S(1)}, u32[]{:S(2)}, u32[]{:S(2)}) collective-permute-start(bf16[80,512]{1,0:T(8,128)(2,1)S(1)} %get-tuple-element.75), channel_id=1, source_target_pairs={{0,16},{2,18},{4,20},{6,22},{8,24},{10,26},{12,28},{14,30},{16,0},... | collective-permute-start | bytes 245768 | tf_op jit(solution)/shard_map/ppermute | solution.py:246
  13.5 12.5 %collective-permute-start.2 = (bf16[128,1024]{1,0:T(8,128)(2,1)S(1)}, bf16[128,1024]{1,0:T(8,128)(2,1)S(1)}, u32[]{:S(2)}, u32[]{:S(2)}) collective-permute-start(bf16[128,1024]{1,0:T(8,128)(2,1)S(1)} %get-tuple-element.38), channel_id=1, source_target_pairs={{0,16},{2,18},{4,20},{6,22},{8,24},{10,26},{12,28},{14,30},{16,0},... | collective-permute-start | bytes 786440 | tf_op jit(solution)/shard_map/ppermute | solution.py:246
  13.5 12.5 %collective-permute-start.1 = (bf16[128,1024]{1,0:T(8,128)(2,1)S(1)}, bf16[128,1024]{1,0:T(8,128)(2,1)S(1)}, u32[]{:S(2)}, u32[]{:S(2)}) collective-permute-start(bf16[128,1024]{1,0:T(8,128)(2,1)S(1)} %get-tuple-element.38), channel_id=1, source_target_pairs={{0,8},{2,10},{4,12},{6,14},{8,0},{10,2},{12,4},{14,6},{16,24},{18,... | collective-permute-start | bytes 786440 | tf_op jit(solution)/shard_map/ppermute | solution.py:246
  14.8 28.6 %copy-start.3 = (bf16[4,128]{1,0:T(4,128)(2,1)S(1)}, bf16[4,128]{1,0:T(4,128)(2,1)}, u32[]{:S(2)}) copy-start(bf16[4,128]{1,0:T(4,128)(2,1)} %time_bias.1) | copy-start | bytes 3076
  14.9 11.4 %collective-permute-start.7 = (bf16[320,512]{1,0:T(8,128)(2,1)S(1)}, bf16[320,512]{1,0:T(8,128)(2,1)S(1)}, u32[]{:S(2)}, u32[]{:S(2)}) collective-permute-start(bf16[320,512]{1,0:T(8,128)(2,1)S(1)} %bitcast_dynamic-update-slice_fusion.refs_9_.refs_0_), channel_id=1, source_target_pairs={{0,6},{2,4},{4,2},{6,0},{8,14},{10,12},{12,10},{14,8},{16,22},{18,... | collective-permute-start | bytes 983048 | tf_op jit(solution)/shard_map/ppermute | solution.py:246
  17.7 12.1 %collective-permute-start.6 = (bf16[320,512]{1,0:T(8,128)(2,1)S(1)}, bf16[320,512]{1,0:T(8,128)(2,1)S(1)}, u32[]{:S(2)}, u32[]{:S(2)}) collective-permute-start(bf16[320,512]{1,0:T(8,128)(2,1)S(1)} %bitcast_dynamic-update-slice_fusion.refs_9_.refs_0_), channel_id=1, source_target_pairs={{0,4},{2,6},{4,0},{6,2},{8,12},{10,14},{12,8},{14,10},{16,20},{18,... | collective-permute-start | bytes 983048 | tf_op jit(solution)/shard_map/ppermute | solution.py:246
  18.2 11.9 %collective-permute-start.5 = (bf16[320,512]{1,0:T(8,128)(2,1)S(1)}, bf16[320,512]{1,0:T(8,128)(2,1)S(1)}, u32[]{:S(2)}, u32[]{:S(2)}) collective-permute-start(bf16[320,512]{1,0:T(8,128)(2,1)S(1)} %bitcast_dynamic-update-slice_fusion.refs_9_.refs_0_), channel_id=1, source_target_pairs={{0,2},{2,0},{4,6},{6,4},{8,10},{10,8},{12,14},{14,12},{16,18},{18,... | collective-permute-start | bytes 983048 | tf_op jit(solution)/shard_map/ppermute | solution.py:246
  26.0 8.0 %collective-permute-start.8 = (bf16[128,1024]{1,0:T(8,128)(2,1)S(1)}, bf16[128,1024]{1,0:T(8,128)(2,1)S(1)}, u32[]{:S(2)}, u32[]{:S(2)}) collective-permute-start(bf16[128,1024]{1,0:T(8,128)(2,1)S(1)} %collective-permute-done.2.refs_1_), channel_id=1, source_target_pairs={{0,8},{2,10},{4,12},{6,14},{8,0},{10,2},{12,4},{14,6},{16,24},{18,... | collective-permute-start | bytes 786440 | tf_op jit(solution)/shard_map/ppermute | solution.py:246
  26.2 7.8 %collective-permute-start.9 = (bf16[128,1024]{1,0:T(8,128)(2,1)S(1)}, bf16[128,1024]{1,0:T(8,128)(2,1)S(1)}, u32[]{:S(2)}, u32[]{:S(2)}) collective-permute-start(bf16[128,1024]{1,0:T(8,128)(2,1)S(1)} %collective-permute-done.1.refs_0_), channel_id=1, source_target_pairs={{0,1},{1,0},{2,3},{3,2},{4,5},{5,4},{6,7},{7,6},{8,9},{9,8},{10,11... | collective-permute-start | bytes 786440 | tf_op jit(solution)/shard_map/ppermute | solution.py:249
  26.3 7.7 %collective-permute-start.10 = (bf16[128,1024]{1,0:T(8,128)(2,1)S(1)}, bf16[128,1024]{1,0:T(8,128)(2,1)S(1)}, u32[]{:S(2)}, u32[]{:S(2)}) collective-permute-start(bf16[128,1024]{1,0:T(8,128)(2,1)S(1)} %collective-permute-done.2.refs_1_), channel_id=1, source_target_pairs={{0,1},{1,0},{2,3},{3,2},{4,5},{5,4},{6,7},{7,6},{8,9},{9,8},{10,11... | collective-permute-start | bytes 786440 | tf_op jit(solution)/shard_map/ppermute | solution.py:249
  34.0 1.5 %collective-permute-start.11 = (bf16[128,1024]{1,0:T(8,128)(2,1)S(1)}, bf16[128,1024]{1,0:T(8,128)(2,1)S(1)}, u32[]{:S(2)}, u32[]{:S(2)}) collective-permute-start(bf16[128,1024]{1,0:T(8,128)(2,1)S(1)} %collective-permute-done.8.refs_2_), channel_id=1, source_target_pairs={{0,1},{1,0},{2,3},{3,2},{4,5},{5,4},{6,7},{7,6},{8,9},{9,8},{10,11... | collective-permute-start | bytes 786440 | tf_op jit(solution)/shard_map/ppermute | solution.py:249
  37.9 17.2 %collective-permute-start.13 = (bf16[1040,256]{1,0:T(8,128)(2,1)}, bf16[1040,256]{1,0:T(8,128)(2,1)S(1)}, u32[]{:S(2)}, u32[]{:S(2)}) collective-permute-start(bf16[1040,256]{1,0:T(8,128)(2,1)} %get-tuple-element.47.kv_ref.refs_0_), channel_id=1, source_target_pairs={{0,4},{2,6},{4,0},{6,2},{8,12},{10,14},{12,8},{14,10},{16,20},{18,... | collective-permute-start | bytes 1597448 | tf_op jit(solution)/shard_map/ppermute | solution.py:246
  39.2 15.9 %collective-permute-start.12 = (bf16[1040,256]{1,0:T(8,128)(2,1)}, bf16[1040,256]{1,0:T(8,128)(2,1)S(1)}, u32[]{:S(2)}, u32[]{:S(2)}) collective-permute-start(bf16[1040,256]{1,0:T(8,128)(2,1)} %get-tuple-element.47.kv_ref.refs_0_), channel_id=1, source_target_pairs={{0,2},{2,0},{4,6},{6,4},{8,10},{10,8},{12,14},{14,12},{16,18},{18,... | collective-permute-start | bytes 1597448 | tf_op jit(solution)/shard_map/ppermute | solution.py:246
  40.7 12.9 %collective-permute-start.15 = (bf16[256,512]{1,0:T(8,128)(2,1)S(1)}, bf16[256,512]{1,0:T(8,128)(2,1)S(1)}, u32[]{:S(2)}, u32[]{:S(2)}) collective-permute-start(bf16[256,512]{1,0:T(8,128)(2,1)S(1)} %get-tuple-element.46.refs_0_), channel_id=1, source_target_pairs={{0,8},{2,10},{4,12},{6,14},{8,0},{10,2},{12,4},{14,6},{16,24},{18,... | collective-permute-start | bytes 786440 | tf_op jit(solution)/shard_map/ppermute | solution.py:246
  41.0 14.1 %collective-permute-start.14 = (bf16[256,512]{1,0:T(8,128)(2,1)S(1)}, bf16[256,512]{1,0:T(8,128)(2,1)S(1)}, u32[]{:S(2)}, u32[]{:S(2)}) collective-permute-start(bf16[256,512]{1,0:T(8,128)(2,1)S(1)} %get-tuple-element.46.refs_0_), channel_id=1, source_target_pairs={{0,16},{2,18},{4,20},{6,22},{8,24},{10,26},{12,28},{14,30},{16,0},... | collective-permute-start | bytes 786440 | tf_op jit(solution)/shard_map/ppermute | solution.py:246
  43.4 1.0 %copy-start = (bf16[1040,256]{1,0:T(8,128)(2,1)S(1)}, bf16[1040,256]{1,0:T(8,128)(2,1)}, u32[]{:S(2)}) copy-start(bf16[1040,256]{1,0:T(8,128)(2,1)} %get-tuple-element.47.kv_ref.refs_0_) | copy-start | bytes 1597444
  44.5 2.6 %copy-start.1 = (bf16[1040,256]{1,0:T(8,128)(2,1)S(1)}, bf16[1040,256]{1,0:T(8,128)(2,1)}, u32[]{:S(2)}) copy-start(bf16[1040,256]{1,0:T(8,128)(2,1)} %get-tuple-element.47.kv_ref.refs_0_) | copy-start | bytes 1597444
  55.1 7.0 %collective-permute-start.18 = (bf16[528,256]{1,0:T(8,128)(2,1)S(1)}, bf16[528,256]{1,0:T(8,128)(2,1)S(1)}, u32[]{:S(2)}, u32[]{:S(2)}) collective-permute-start(bf16[528,256]{1,0:T(8,128)(2,1)S(1)} %slice.19), channel_id=1, source_target_pairs={{0,4},{2,6},{4,0},{6,2},{8,12},{10,14},{12,8},{14,10},{16,20},{18,... | collective-permute-start | bytes 811016 | tf_op jit(solution)/shard_map/ppermute | solution.py:246
  55.7 6.4 %collective-permute-start.17 = (bf16[512,256]{1,0:T(8,128)(2,1)S(1)}, bf16[512,256]{1,0:T(8,128)(2,1)S(1)}, u32[]{:S(2)}, u32[]{:S(2)}) collective-permute-start(bf16[512,256]{1,0:T(8,128)(2,1)S(1)} %slice.18), channel_id=1, source_target_pairs={{0,2},{2,0},{4,6},{6,4},{8,10},{10,8},{12,14},{14,12},{16,18},{18,... | collective-permute-start | bytes 786440 | tf_op jit(solution)/shard_map/ppermute | solution.py:246
  56.5 7.3 %collective-permute-start.16 = (bf16[256,512]{1,0:T(8,128)(2,1)S(1)}, bf16[256,512]{1,0:T(8,128)(2,1)S(1)}, u32[]{:S(2)}, u32[]{:S(2)}) collective-permute-start(bf16[256,512]{1,0:T(8,128)(2,1)S(1)} %collective-permute-done.14.refs_2_), channel_id=1, source_target_pairs={{0,8},{2,10},{4,12},{6,14},{8,0},{10,2},{12,4},{14,6},{16,24},{18,... | collective-permute-start | bytes 786440 | tf_op jit(solution)/shard_map/ppermute | solution.py:246
  64.5 14.8 %collective-permute-start.19 = (bf16[512,512]{1,0:T(8,128)(2,1)S(1)}, bf16[512,512]{1,0:T(8,128)(2,1)S(1)}, u32[]{:S(2)}, u32[]{:S(2)}) collective-permute-start(bf16[512,512]{1,0:T(8,128)(2,1)S(1)} %get-tuple-element.62), channel_id=1, source_target_pairs={{0,1},{1,0},{2,3},{3,2},{4,5},{5,4},{6,7},{7,6},{8,9},{9,8},{10,11... | collective-permute-start | bytes 1572872 | tf_op jit(solution)/shard_map/ppermute | solution.py:249
  64.5 8.1 %collective-permute-start.20 = (bf16[256,256]{1,0:T(8,128)(2,1)S(1)}, bf16[256,256]{1,0:T(8,128)(2,1)S(1)}, u32[]{:S(2)}, u32[]{:S(2)}) collective-permute-start(bf16[256,256]{1,0:T(8,128)(2,1)S(1)} %get-tuple-element.64), channel_id=1, source_target_pairs={{0,8},{2,10},{4,12},{6,14},{8,0},{10,2},{12,4},{14,6},{16,24},{18,... | collective-permute-start | bytes 393224 | tf_op jit(solution)/shard_map/ppermute | solution.py:246
  64.8 12.9 %collective-permute-start.21 = (bf16[256,256]{1,0:T(8,128)(2,1)S(1)}, bf16[256,256]{1,0:T(8,128)(2,1)S(1)}, u32[]{:S(2)}, u32[]{:S(2)}) collective-permute-start(bf16[256,256]{1,0:T(8,128)(2,1)S(1)} %get-tuple-element.65), channel_id=1, source_target_pairs={{0,16},{2,18},{4,20},{6,22},{8,24},{10,26},{12,28},{14,30},{16,0},... | collective-permute-start | bytes 393224 | tf_op jit(solution)/shard_map/ppermute | solution.py:246
  67.3 10.5 %collective-permute-start.22 = (bf16[256,256]{1,0:T(8,128)(2,1)S(1)}, bf16[256,256]{1,0:T(8,128)(2,1)S(1)}, u32[]{:S(2)}, u32[]{:S(2)}) collective-permute-start(bf16[256,256]{1,0:T(8,128)(2,1)S(1)} %get-tuple-element.66), channel_id=1, source_target_pairs={{0,24},{2,26},{4,28},{6,30},{8,16},{10,18},{12,20},{14,22},{16,8},... | collective-permute-start | bytes 393224 | tf_op jit(solution)/shard_map/ppermute | solution.py:246
  69.0 9.3 %collective-permute-start.23 = (bf16[256,256]{1,0:T(8,128)(2,1)S(1)}, bf16[256,256]{1,0:T(8,128)(2,1)S(1)}, u32[]{:S(2)}, u32[]{:S(2)}) collective-permute-start(bf16[256,256]{1,0:T(8,128)(2,1)S(1)} %get-tuple-element.63.refs_0_), channel_id=1, source_target_pairs={{0,1},{1,0},{2,3},{3,2},{4,5},{5,4},{6,7},{7,6},{8,9},{9,8},{10,11... | collective-permute-start | bytes 393224 | tf_op jit(solution)/shard_map/ppermute | solution.py:249
  72.6 5.6 %collective-permute-start.24 = (bf16[256,256]{1,0:T(8,128)(2,1)S(1)}, bf16[256,256]{1,0:T(8,128)(2,1)S(1)}, u32[]{:S(2)}, u32[]{:S(2)}) collective-permute-start(bf16[256,256]{1,0:T(8,128)(2,1)S(1)} %collective-permute-done.20.refs_1_), channel_id=1, source_target_pairs={{0,1},{1,0},{2,3},{3,2},{4,5},{5,4},{6,7},{7,6},{8,9},{9,8},{10,11... | collective-permute-start | bytes 393224 | tf_op jit(solution)/shard_map/ppermute | solution.py:249
  77.7 1.3 %collective-permute-start.25 = (bf16[256,256]{1,0:T(8,128)(2,1)S(1)}, bf16[256,256]{1,0:T(8,128)(2,1)S(1)}, u32[]{:S(2)}, u32[]{:S(2)}) collective-permute-start(bf16[256,256]{1,0:T(8,128)(2,1)S(1)} %collective-permute-done.21.refs_2_), channel_id=1, source_target_pairs={{0,1},{1,0},{2,3},{3,2},{4,5},{5,4},{6,7},{7,6},{8,9},{9,8},{10,11... | collective-permute-start | bytes 393224 | tf_op jit(solution)/shard_map/ppermute | solution.py:249
  77.8 1.5 %collective-permute-start.26 = (bf16[256,256]{1,0:T(8,128)(2,1)S(1)}, bf16[256,256]{1,0:T(8,128)(2,1)S(1)}, u32[]{:S(2)}, u32[]{:S(2)}) collective-permute-start(bf16[256,256]{1,0:T(8,128)(2,1)S(1)} %collective-permute-done.22.refs_3_), channel_id=1, source_target_pairs={{0,1},{1,0},{2,3},{3,2},{4,5},{5,4},{6,7},{7,6},{8,9},{9,8},{10,11... | collective-permute-start | bytes 393224 | tf_op jit(solution)/shard_map/ppermute | solution.py:249

commit v4 on v3

--- a/solution.py
+++ b/solution.py
@@ -170,36 +170,34 @@
         outs[0][...] = total[...]
 
 
-def parcel_kernel(lead, ids, *refs):
+def parcel_kernel(lead, lines, ids, *refs):
     columns, (kept_ref, give_ref) = refs[:lead], refs[lead:]
-    height = columns[0].shape[0]
+    a, i, c = ids[0], ids[1], ids[2]
+    chunk = columns[0].shape[0] // lines
+    parts = lead // 2
 
     def place(low_ref, high_ref):
-        for n in range(lead // 2):
-            low_ref[n * height : (n + 1) * height, :] = columns[n][...]
-            high_ref[n * height : (n + 1) * height, :] = columns[lead // 2 + n][...]
-
-    mine = ids[0] // (lead // 2) == ids[2]
+        for n, ref in enumerate(columns):
+            target = low_ref if n < parts else high_ref
+            for j in range(lines):
+                to = (((a ^ n) % parts) * lines + (i ^ j)) * chunk
+                target[pl.ds(pl.multiple_of(to, chunk), chunk), :] = ref[
+                    j * chunk : (j + 1) * chunk, :
+                ]
+
+    mine = a // parts == c
     pl.when(mine)(lambda: place(kept_ref, give_ref))
     pl.when(jnp.logical_not(mine))(lambda: place(give_ref, kept_ref))
 
 
-def output_kernel(lead, lines, ids, events, kept, given, *refs):
+def output_kernel(lead, ids, events, kept, given, *refs):
     own, refs = refs[:lead], refs[lead:]
     other, refs = refs[:lead], refs[lead:]
-    out_ref, gated, wbuf = refs
-    a, i, c = ids[0], ids[1], ids[2]
+    out_ref, gated = refs
+    a, c = ids[0], ids[2]
     rows, share = out_ref.shape
     size = own[0].shape[1] // 2
     full = 2 * lead * size
-    chunk = kept.shape[0] // (2 * lines)
-    for k in range(2):
-        for j in range(lines):
-            place = (((a ^ k) & 1) * lines + (i ^ j)) * chunk
-            source = slice((k * lines + j) * chunk, (k * lines + j + 1) * chunk)
-            to = pl.ds(pl.multiple_of(place, chunk), chunk)
-            wbuf[0, to, :] = kept[source, :]
-            wbuf[1, to, :] = given[source, :]
     parts = [ref[:, :size].astype(jnp.float32) for ref in (*own, *other)]
     middle = functools.reduce(jnp.add, [jnp.sum(x, -1, keepdims=True) for x in parts]) / full
     parts = [x - middle for x in parts]
@@ -210,8 +208,8 @@
             value = parts[side * lead + k] * inverse * group[k][:, size:].astype(jnp.float32)
             place = pl.ds(pl.multiple_of((a ^ k) * size, size), size)
             gated[side, :, place] = value.astype(jnp.bfloat16)
-    total = lax.dot_general(gated[0], wbuf[0], NT, preferred_element_type=jnp.float32)
-    total += lax.dot_general(gated[1], wbuf[1], NT, preferred_element_type=jnp.float32)
+    total = lax.dot_general(gated[0], kept[...], NT, preferred_element_type=jnp.float32)
+    total += lax.dot_general(gated[1], given[...], NT, preferred_element_type=jnp.float32)
     residual = events[:, pl.ds(pl.multiple_of(c * share, share), share)].astype(jnp.float32)
     out_ref[...] = (residual + total).astype(jnp.bfloat16)
 
@@ -307,7 +305,8 @@
 
     kvs = [[kv]] + [[x] for x in direct]
     result = attend(0, None)
-    *direct, far, near, result[0] = lax.optimization_barrier((*direct, far, near, result[0]))
+    far, near, _ = lax.optimization_barrier((far, near, result[0]))
+    *direct, result[0] = lax.optimization_barrier((*direct, result[0]))
     kvs = [[kv]] + [[x] for x in direct]
     if lines == 4:
         part = span // 2
@@ -320,19 +319,18 @@
     across = [swap(x) for x in own]
     parcel = shape(2 * lines * chunk, w_out.shape[0])
     kept, given = call(
-        functools.partial(parcel_kernel, lead),
+        functools.partial(parcel_kernel, lead, lines),
         [ids, columns, near, far, relayed],
         [parcel, parcel],
         [],
     )
     given = swap(given)
     return call(
-        functools.partial(output_kernel, lead, lines),
+        functools.partial(output_kernel, lead),
         [ids, events, kept, given, *own, *across],
         [shape(rows, share)],
         [
             pltpu.VMEM((2, rows, lead * size), bf16),
-            pltpu.VMEM((2, share, lead * size), bf16),
         ],
     )[0]
 

time: 82 us -> 81 us (0.988)
  waiting for transfers between devices: 39.6 us -> 37.5 us
  starting transfers between devices: 23.1 us -> 24.1 us
    ppermute x19, waiting for transfers between devices: 37 us -> 35 us  [exchange(): return lax.ppermute(x, 'seq', [(t, t ^ flip) for t in range(devices)])]
    ppermute x19, starting transfers between devices: 22.1 us -> 23.2 us  [exchange(): return lax.ppermute(x, 'seq', [(t, t ^ flip) for t in range(devices)])]
  transfers between devices with their start and end apart: 27 -> 27, of which waited for: 14 -> 14; matrix products, arithmetic and copies ran while one was open for 0% -> 0% of each run, Pallas kernels for 12% -> 13%
where the time goes in v4:
time: 81 us; the launch traced here: 80.8 us
  waiting for transfers between devices  37.5 us (46%)
  starting transfers between devices  24.1 us (30%)
  Pallas kernels  15.6 us (19%)
  local copies, waits for them, and re-layouts  2.42 us (3%)
  other arithmetic  0.84 us (1%)
    ppermute x19, waiting for transfers between devices, exchange(): return lax.ppermute(x, 'seq', [(t, t ^ flip) for t in range(devices)])  35 us
    ppermute x19, starting transfers between devices, exchange(): return lax.ppermute(x, 'seq', [(t, t ^ flip) for t in range(devices)])  23.2 us
    pallas_call x9, Pallas kernels, call(): pl.pallas_call(kernel, out_shape=outs, in_specs=[pl.BlockSpec(memory_spac...  15.6 us
    ppermute x8, waiting for transfers between devices, swap(): return lax.ppermute(x, 'head', [(0, 1), (1, 0)])  2.55 us
  transfers between devices with their start and end apart: 27, of which 14 were waited for; matrix products, arithmetic and copies ran while one was open for 0% of the time, Pallas kernels for 13%

profile of v4, /device:TPU:0, one launch (start us, length us, event | category | flops | bytes accessed | tf_op | source)
XLA Modules:
  0.0 80.8 jit_solution(7781768800759580544)
XLA Ops:
  0.0 0.7 convert_element_type.5
  0.8 1.1 %reshape.6 = bf16[64,4,4,128]{3,2,1,0:T(4,128)(2,1)S(1)} reshape(bf16[64,4,512]{2,1,0:T(4,128)(2,1)} %param.6) | data formatting | bytes 524288 | tf_op jit(solution)/shard_map/reshape | solution.py:252
  1.8 0.1 copy.6
  1.9 0.1 reshape.7
  2.1 5.1 %collective-permute-start.4 = (bf16[80,512]{1,0:T(8,128)(2,1)S(1)}, bf16[80,512]{1,0:T(8,128)(2,1)S(1)}, u32[]{:S(2)}, u32[]{:S(2)}) collective-permute-start(bf16[80,512]{1,0:T(8,128)(2,1)S(1)} %get-tuple-element.72), channel_id=1, source_target_pairs={{0,24},{2,26},{4,28},{6,30},{8,16},{10,18},{12,20},{14,22},{16,8},... | collective-permute-start | bytes 245768 | tf_op jit(solution)/shard_map/ppermute | solution.py:244
  7.3 0.0 collective-permute-start
  7.3 0.6 collective-permute-start.3
  7.9 0.1 pad_add_fusion.ids
  8.0 0.9 %shard_map.55 = (bf16[256,1024]{1,0:T(8,128)(2,1)S(1)}, bf16[128,1024]{1,0:T(8,128)(2,1)S(1)}) custom-call(s32[3]{0:T(128)S(1)} %pad_add_fusion.ids, bf16[256,1024]{1,0:T(8,128)(2,1)S(1)} %copy-done.2), custom_call_target="tpu_custom_call" | custom-call | flops 1 | bytes 1 | tf_op jit(solution)/shard_map/pallas_call | solution.py:218
  8.9 4.6 %collective-permute-done.refs_6_ = bf16[80,512]{1,0:T(8,128)(2,1)S(1)} collective-permute-done((bf16[80,512]{1,0:T(8,128)(2,1)S(1)}, bf16[80,512]{1,0:T(8,128)(2,1)S(1)}, u32[]{:S(2)}, u32[]{:S(2)}) %collective-permute-start) | collective-permute-done | bytes 81952 | tf_op jit(solution)/shard_map/ppermute | solution.py:244
  13.5 0.0 collective-permute-start.2
  13.5 1.3 %collective-permute-start.1 = (bf16[128,1024]{1,0:T(8,128)(2,1)S(1)}, bf16[128,1024]{1,0:T(8,128)(2,1)S(1)}, u32[]{:S(2)}, u32[]{:S(2)}) collective-permute-start(bf16[128,1024]{1,0:T(8,128)(2,1)S(1)} %get-tuple-element.38), channel_id=1, source_target_pairs={{0,8},{2,10},{4,12},{6,14},{8,0},{10,2},{12,4},{14,6},{16,24},{18,... | collective-permute-start | bytes 786440 | tf_op jit(solution)/shard_map/ppermute | solution.py:244
  14.8 0.0 collective-permute-done.3.refs_7_
  14.8 0.0 collective-permute-done.4.refs_8_
  14.9 2.8 %collective-permute-start.7 = (bf16[320,512]{1,0:T(8,128)(2,1)S(1)}, bf16[320,512]{1,0:T(8,128)(2,1)S(1)}, u32[]{:S(2)}, u32[]{:S(2)}) collective-permute-start(bf16[320,512]{1,0:T(8,128)(2,1)S(1)} %bitcast_dynamic-update-slice_fusion.refs_9_.refs_0_), channel_id=1, source_target_pairs={{0,6},{2,4},{4,2},{6,0},{8,14},{10,12},{12,10},{14,8},{16,22},{18,... | collective-permute-start | bytes 983048 | tf_op jit(solution)/shard_map/ppermute | solution.py:244
  17.7 0.5 collective-permute-start.6
  18.2 0.2 collective-permute-start.5
  18.4 7.6 %collective-permute-done.2.refs_1_ = bf16[128,1024]{1,0:T(8,128)(2,1)S(1)} collective-permute-done((bf16[128,1024]{1,0:T(8,128)(2,1)S(1)}, bf16[128,1024]{1,0:T(8,128)(2,1)S(1)}, u32[]{:S(2)}, u32[]{:S(2)}) %collective-permute-start.2) | collective-permute-done | bytes 262176 | tf_op jit(solution)/shard_map/ppermute | solution.py:244
  26.0 0.0 collective-permute-done.1.refs_0_
  26.0 0.2 collective-permute-start.8
  26.2 0.0 collective-permute-start.9
  26.2 0.1 collective-permute-done.7.refs_12_.refs_3_
  26.3 0.4 collective-permute-start.10
  26.7 3.0 %collective-permute-done.6.refs_11_.refs_2_ = bf16[320,512]{1,0:T(8,128)(2,1)S(1)} collective-permute-done((bf16[320,512]{1,0:T(8,128)(2,1)S(1)}, bf16[320,512]{1,0:T(8,128)(2,1)S(1)}, u32[]{:S(2)}, u32[]{:S(2)}) %collective-permute-start.6) | collective-permute-done | bytes 327712 | tf_op jit(solution)/shard_map/ppermute | solution.py:244
  29.7 0.3 collective-permute-done.5.refs_10_.refs_1_
  30.0 4.0 %collective-permute-done.8.refs_2_ = bf16[128,1024]{1,0:T(8,128)(2,1)S(1)} collective-permute-done((bf16[128,1024]{1,0:T(8,128)(2,1)S(1)}, bf16[128,1024]{1,0:T(8,128)(2,1)S(1)}, u32[]{:S(2)}, u32[]{:S(2)}) %collective-permute-start.8) | collective-permute-done | bytes 262176 | tf_op jit(solution)/shard_map/ppermute | solution.py:244
  34.0 0.0 collective-permute-start.11
  34.0 0.0 collective-permute-done.10.refs_4_
  34.0 0.0 collective-permute-done.9.refs_3_
  34.0 1.5 %collective-permute-done.11.refs_5_ = bf16[128,1024]{1,0:T(8,128)(2,1)S(1)} collective-permute-done((bf16[128,1024]{1,0:T(8,128)(2,1)S(1)}, bf16[128,1024]{1,0:T(8,128)(2,1)S(1)}, u32[]{:S(2)}, u32[]{:S(2)}) %collective-permute-start.11) | collective-permute-done | bytes 262176 | tf_op jit(solution)/shard_map/ppermute | solution.py:247
  35.5 2.3 %shard_map.56 = (bf16[1040,256]{1,0:T(8,128)(2,1)}, bf16[1024,1024]{1,0:T(8,128)(2,1)}, bf16[256,512]{1,0:T(8,128)(2,1)S(1)}) custom-call(s32[3]{0:T(128)S(1)} %pad_add_fusion.ids, bf16[256,1024]{1,0:T(8,128)(2,1)S(1)} %get-tuple-element.36.normed, bf16[80,512]{1,0:T(8,128)(2,1)S(1)} %get-tuple-element.73.own_msg, ...), custom_call_target="tpu_custom_call" | custom-call | flops 1 | bytes 1 | tf_op jit(solution)/shard_map/pallas_call | solution.py:218
  37.9 1.4 %collective-permute-start.16 = (bf16[1040,256]{1,0:T(8,128)(2,1)}, bf16[1040,256]{1,0:T(8,128)(2,1)S(1)}, u32[]{:S(2)}, u32[]{:S(2)}) collective-permute-start(bf16[1040,256]{1,0:T(8,128)(2,1)} %get-tuple-element.48.kv_ref.refs_0_), channel_id=1, source_target_pairs={{0,4},{2,6},{4,0},{6,2},{8,12},{10,14},{12,8},{14,10},{16,20},{18,... | collective-permute-start | bytes 1597448 | tf_op jit(solution)/shard_map/ppermute | solution.py:244
  39.2 1.5 %collective-permute-start.15 = (bf16[1040,256]{1,0:T(8,128)(2,1)}, bf16[1040,256]{1,0:T(8,128)(2,1)S(1)}, u32[]{:S(2)}, u32[]{:S(2)}) collective-permute-start(bf16[1040,256]{1,0:T(8,128)(2,1)} %get-tuple-element.48.kv_ref.refs_0_), channel_id=1, source_target_pairs={{0,2},{2,0},{4,6},{6,4},{8,10},{10,8},{12,14},{14,12},{16,18},{18,... | collective-permute-start | bytes 1597448 | tf_op jit(solution)/shard_map/ppermute | solution.py:244
  40.7 0.3 collective-permute-start.13
  41.0 2.4 %collective-permute-start.12 = (bf16[256,512]{1,0:T(8,128)(2,1)S(1)}, bf16[256,512]{1,0:T(8,128)(2,1)S(1)}, u32[]{:S(2)}, u32[]{:S(2)}) collective-permute-start(bf16[256,512]{1,0:T(8,128)(2,1)S(1)} %get-tuple-element.46.refs_0_), channel_id=1, source_target_pairs={{0,16},{2,18},{4,20},{6,22},{8,24},{10,26},{12,28},{14,30},{16,0},... | collective-permute-start | bytes 786440 | tf_op jit(solution)/shard_map/ppermute | solution.py:244
  43.4 1.0 %copy-done = bf16[1040,256]{1,0:T(8,128)(2,1)S(1)} copy-done((bf16[1040,256]{1,0:T(8,128)(2,1)S(1)}, bf16[1040,256]{1,0:T(8,128)(2,1)}, u32[]{:S(2)}) %copy-start) | copy-done | bytes 532504
  44.5 2.6 %shard_map.57 = (bf16[1024,256]{1,0:T(8,128)(2,1)S(1)}, bf16[256,128]{1,0:T(8,128)(2,1)S(1)}, bf16[256,128]{1,0:T(8,128)(2,1)S(1)}, bf16[256,128]{1,0:T(8,128)(2,1)S(1)}, bf16[256,128]{1,0:T(8,128)(2,1)S(1)}) custom-call(s32[3]{0:T(128)S(1)} %pad_add_fusion.ids, bf16[1024,1024]{1,0:T(8,128)(2,1)} %get-tuple-element.47.normed_all, ...), custom_call_target="tpu_custom_call" | custom-call | flops 1 | bytes 1 | tf_op jit(solution)/shard_map/pallas_call | solution.py:218
  47.1 1.8 %shard_map.58.refs_1_ = f32[1024,128]{1,0:T(8,128)S(1)} custom-call(s32[3]{0:T(128)S(1)} %pad_add_fusion.ids, bf16[1024,256]{1,0:T(8,128)(2,1)S(1)} %get-tuple-element.49.q_ref, bf16[1040,256]{1,0:T(8,128)(2,1)S(1)} %copy-done.1), custom_call_target="tpu_custom_call" | custom-call | flops 1 | bytes 1 | tf_op jit(solution)/shard_map/pallas_call | solution.py:218
  48.9 3.4 %collective-permute-done.16.refs_0_ = bf16[1040,256]{1,0:T(8,128)(2,1)S(1)} collective-permute-done((bf16[1040,256]{1,0:T(8,128)(2,1)}, bf16[1040,256]{1,0:T(8,128)(2,1)S(1)}, u32[]{:S(2)}, u32[]{:S(2)}) %collective-permute-start.16) | collective-permute-done | bytes 532512 | tf_op jit(solution)/shard_map/ppermute | solution.py:244
  52.2 1.1 %collective-permute-done.15.refs_0_ = bf16[1040,256]{1,0:T(8,128)(2,1)S(1)} collective-permute-done((bf16[1040,256]{1,0:T(8,128)(2,1)}, bf16[1040,256]{1,0:T(8,128)(2,1)S(1)}, u32[]{:S(2)}, u32[]{:S(2)}) %collective-permute-start.15) | collective-permute-done | bytes 532512 | tf_op jit(solution)/shard_map/ppermute | solution.py:244
  53.3 0.7 collective-permute-start.18
  54.1 1.4 %collective-permute-start.17 = (bf16[512,256]{1,0:T(8,128)(2,1)S(1)}, bf16[512,256]{1,0:T(8,128)(2,1)S(1)}, u32[]{:S(2)}, u32[]{:S(2)}) collective-permute-start(bf16[512,256]{1,0:T(8,128)(2,1)S(1)} %slice.18), channel_id=1, source_target_pairs={{0,2},{2,0},{4,6},{6,4},{8,10},{10,8},{12,14},{14,12},{16,18},{18,... | collective-permute-start | bytes 786440 | tf_op jit(solution)/shard_map/ppermute | solution.py:244
  55.5 0.0 collective-permute-done.13.refs_1_
  55.5 0.0 collective-permute-done.12.refs_2_
  55.5 0.3 collective-permute-start.14
  55.8 1.6 %shard_map.59.refs_1_ = f32[1024,128]{1,0:T(8,128)S(1)} custom-call(s32[3]{0:T(128)S(1)} %pad_add_fusion.ids, bf16[1024,256]{1,0:T(8,128)(2,1)S(1)} %get-tuple-element.49.q_ref, bf16[1040,256]{1,0:T(8,128)(2,1)S(1)} %collective-permute-done.15.refs_0_, f32[1024,128]{1,0:T(8,128)S(1)} %shard_map.58.refs_1_), custom_call_target="tpu_custom_call" | custom-call | flops 1 | bytes 1 | tf_op jit(solution)/shard_map/pallas_call | solution.py:218
  57.4 1.6 %shard_map.60.refs_2_ = f32[1024,128]{1,0:T(8,128)S(1)} custom-call(s32[3]{0:T(128)S(1)} %pad_add_fusion.ids, bf16[1024,256]{1,0:T(8,128)(2,1)S(1)} %get-tuple-element.49.q_ref, bf16[1040,256]{1,0:T(8,128)(2,1)S(1)} %collective-permute-done.16.refs_0_, f32[1024,128]{1,0:T(8,128)S(1)} %shard_map.59.refs_1_), custom_call_target="tpu_custom_call" | custom-call | flops 1 | bytes 1 | tf_op jit(solution)/shard_map/pallas_call | solution.py:218
  59.0 2.1 %collective-permute-done.17.refs_0_ = bf16[512,256]{1,0:T(8,128)(2,1)S(1)} collective-permute-done((bf16[512,256]{1,0:T(8,128)(2,1)S(1)}, bf16[512,256]{1,0:T(8,128)(2,1)S(1)}, u32[]{:S(2)}, u32[]{:S(2)}) %collective-permute-start.17) | collective-permute-done | bytes 262176 | tf_op jit(solution)/shard_map/ppermute | solution.py:244
  61.1 0.0 collective-permute-done.18.refs_1_
  61.1 1.7 %shard_map.61 = (bf16[256,256]{1,0:T(8,128)(2,1)S(1)}, bf16[256,256]{1,0:T(8,128)(2,1)S(1)}, bf16[256,256]{1,0:T(8,128)(2,1)S(1)}, bf16[256,256]{1,0:T(8,128)(2,1)S(1)}) custom-call(s32[3]{0:T(128)S(1)} %pad_add_fusion.ids, bf16[1024,256]{1,0:T(8,128)(2,1)S(1)} %get-tuple-element.49.q_ref, bf16[512,256]{1,0:T(8,128)(2,1)S(1)} %collective-permute-done.17.refs_0_, ...), custom_call_target="tpu_custom_call" | custom-call | flops 1 | bytes 1 | tf_op jit(solution)/shard_map/pallas_call | solution.py:218
  62.7 0.0 collective-permute-done.14.refs_3_
  62.8 0.6 shard_map.62
  63.4 0.1 collective-permute-start.19
  63.5 0.3 collective-permute-start.20
  63.8 2.4 %collective-permute-start.21 = (bf16[256,256]{1,0:T(8,128)(2,1)S(1)}, bf16[256,256]{1,0:T(8,128)(2,1)S(1)}, u32[]{:S(2)}, u32[]{:S(2)}) collective-permute-start(bf16[256,256]{1,0:T(8,128)(2,1)S(1)} %get-tuple-element.65), channel_id=1, source_target_pairs={{0,16},{2,18},{4,20},{6,22},{8,24},{10,26},{12,28},{14,30},{16,0},... | collective-permute-start | bytes 393224 | tf_op jit(solution)/shard_map/ppermute | solution.py:244
  66.2 1.8 %collective-permute-start.22 = (bf16[256,256]{1,0:T(8,128)(2,1)S(1)}, bf16[256,256]{1,0:T(8,128)(2,1)S(1)}, u32[]{:S(2)}, u32[]{:S(2)}) collective-permute-start(bf16[256,256]{1,0:T(8,128)(2,1)S(1)} %get-tuple-element.66), channel_id=1, source_target_pairs={{0,24},{2,26},{4,28},{6,30},{8,16},{10,18},{12,20},{14,22},{16,8},... | collective-permute-start | bytes 393224 | tf_op jit(solution)/shard_map/ppermute | solution.py:244
  67.9 0.0 collective-permute-start.23
  67.9 3.6 %collective-permute-done.20.refs_1_ = bf16[256,256]{1,0:T(8,128)(2,1)S(1)} collective-permute-done((bf16[256,256]{1,0:T(8,128)(2,1)S(1)}, bf16[256,256]{1,0:T(8,128)(2,1)S(1)}, u32[]{:S(2)}, u32[]{:S(2)}) %collective-permute-start.20) | collective-permute-done | bytes 131104 | tf_op jit(solution)/shard_map/ppermute | solution.py:244
  71.6 5.1 %collective-permute-done.21.refs_2_ = bf16[256,256]{1,0:T(8,128)(2,1)S(1)} collective-permute-done((bf16[256,256]{1,0:T(8,128)(2,1)S(1)}, bf16[256,256]{1,0:T(8,128)(2,1)S(1)}, u32[]{:S(2)}, u32[]{:S(2)}) %collective-permute-start.21) | collective-permute-done | bytes 131104 | tf_op jit(solution)/shard_map/ppermute | solution.py:244
  76.7 0.0 collective-permute-start.25
  76.7 0.5 collective-permute-start.26
  77.2 0.8 %collective-permute-done.25.refs_6_ = bf16[256,256]{1,0:T(8,128)(2,1)S(1)} collective-permute-done((bf16[256,256]{1,0:T(8,128)(2,1)S(1)}, bf16[256,256]{1,0:T(8,128)(2,1)S(1)}, u32[]{:S(2)}, u32[]{:S(2)}) %collective-permute-start.25) | collective-permute-done | bytes 131104 | tf_op jit(solution)/shard_map/ppermute | solution.py:247
  78.1 0.2 collective-permute-done.26.refs_7_
  78.2 2.5 %shard_map.63 = bf16[256,512]{1,0:T(8,128)(2,1)} custom-call(s32[3]{0:T(128)S(1)} %pad_add_fusion.ids, bf16[256,1024]{1,0:T(8,128)(2,1)S(1)} %copy-done.2, bf16[512,512]{1,0:T(8,128)(2,1)S(1)} %get-tuple-element.61.kept, bf16[512,512]{1,0:T(8,128)(2,1)S(1)} %collective-permute-done.19.given, bf16[256,256]{1,0:T(8,128)(2,1)S(1)} %get-tuple-element.63.refs_0_, ...), custom_call_target="tpu_custom_call" | custom-call | flops 1 | bytes 1 | tf_op jit(solution)/shard_map/pallas_call | solution.py:218
  (24 shorter events, 0.2 us)
Async XLA Ops:
  0.0 8.0 %copy-start.2 = (bf16[256,1024]{1,0:T(8,128)(2,1)S(1)}, bf16[256,1024]{1,0:T(8,128)(2,1)}, u32[]{:S(2)}) copy-start(bf16[256,1024]{1,0:T(8,128)(2,1)} %events.3) | copy-start | bytes 1572868
  0.0 14.8 %copy-start.4 = (bf16[512,64]{0,1:T(8,128)(2,1)S(1)}, bf16[512,64]{0,1:T(8,128)(2,1)}, u32[]{:S(2)}) copy-start(bf16[512,64]{0,1:T(8,128)(2,1)} %param.7) | copy-start | bytes 196612
  2.1 12.7 %collective-permute-start.4 = (bf16[80,512]{1,0:T(8,128)(2,1)S(1)}, bf16[80,512]{1,0:T(8,128)(2,1)S(1)}, u32[]{:S(2)}, u32[]{:S(2)}) collective-permute-start(bf16[80,512]{1,0:T(8,128)(2,1)S(1)} %get-tuple-element.72), channel_id=1, source_target_pairs={{0,24},{2,26},{4,28},{6,30},{8,16},{10,18},{12,20},{14,22},{16,8},... | collective-permute-start | bytes 245768 | tf_op jit(solution)/shard_map/ppermute | solution.py:244
  7.3 6.2 %collective-permute-start = (bf16[80,512]{1,0:T(8,128)(2,1)S(1)}, bf16[80,512]{1,0:T(8,128)(2,1)S(1)}, u32[]{:S(2)}, u32[]{:S(2)}) collective-permute-start(bf16[80,512]{1,0:T(8,128)(2,1)S(1)} %get-tuple-element.74), channel_id=1, source_target_pairs={{0,8},{2,10},{4,12},{6,14},{8,0},{10,2},{12,4},{14,6},{16,24},{18,... | collective-permute-start | bytes 245768 | tf_op jit(solution)/shard_map/ppermute | solution.py:244
  7.3 7.5 %collective-permute-start.3 = (bf16[80,512]{1,0:T(8,128)(2,1)S(1)}, bf16[80,512]{1,0:T(8,128)(2,1)S(1)}, u32[]{:S(2)}, u32[]{:S(2)}) collective-permute-start(bf16[80,512]{1,0:T(8,128)(2,1)S(1)} %get-tuple-element.75), channel_id=1, source_target_pairs={{0,16},{2,18},{4,20},{6,22},{8,24},{10,26},{12,28},{14,30},{16,0},... | collective-permute-start | bytes 245768 | tf_op jit(solution)/shard_map/ppermute | solution.py:244
  13.5 12.5 %collective-permute-start.2 = (bf16[128,1024]{1,0:T(8,128)(2,1)S(1)}, bf16[128,1024]{1,0:T(8,128)(2,1)S(1)}, u32[]{:S(2)}, u32[]{:S(2)}) collective-permute-start(bf16[128,1024]{1,0:T(8,128)(2,1)S(1)} %get-tuple-element.38), channel_id=1, source_target_pairs={{0,16},{2,18},{4,20},{6,22},{8,24},{10,26},{12,28},{14,30},{16,0},... | collective-permute-start | bytes 786440 | tf_op jit(solution)/shard_map/ppermute | solution.py:244
  13.5 12.5 %collective-permute-start.1 = (bf16[128,1024]{1,0:T(8,128)(2,1)S(1)}, bf16[128,1024]{1,0:T(8,128)(2,1)S(1)}, u32[]{:S(2)}, u32[]{:S(2)}) collective-permute-start(bf16[128,1024]{1,0:T(8,128)(2,1)S(1)} %get-tuple-element.38), channel_id=1, source_target_pairs={{0,8},{2,10},{4,12},{6,14},{8,0},{10,2},{12,4},{14,6},{16,24},{18,... | collective-permute-start | bytes 786440 | tf_op jit(solution)/shard_map/ppermute | solution.py:244
  14.8 28.6 %copy-start.3 = (bf16[4,128]{1,0:T(4,128)(2,1)S(1)}, bf16[4,128]{1,0:T(4,128)(2,1)}, u32[]{:S(2)}) copy-start(bf16[4,128]{1,0:T(4,128)(2,1)} %time_bias.1) | copy-start | bytes 3076
  14.9 11.4 %collective-permute-start.7 = (bf16[320,512]{1,0:T(8,128)(2,1)S(1)}, bf16[320,512]{1,0:T(8,128)(2,1)S(1)}, u32[]{:S(2)}, u32[]{:S(2)}) collective-permute-start(bf16[320,512]{1,0:T(8,128)(2,1)S(1)} %bitcast_dynamic-update-slice_fusion.refs_9_.refs_0_), channel_id=1, source_target_pairs={{0,6},{2,4},{4,2},{6,0},{8,14},{10,12},{12,10},{14,8},{16,22},{18,... | collective-permute-start | bytes 983048 | tf_op jit(solution)/shard_map/ppermute | solution.py:244
  17.7 12.1 %collective-permute-start.6 = (bf16[320,512]{1,0:T(8,128)(2,1)S(1)}, bf16[320,512]{1,0:T(8,128)(2,1)S(1)}, u32[]{:S(2)}, u32[]{:S(2)}) collective-permute-start(bf16[320,512]{1,0:T(8,128)(2,1)S(1)} %bitcast_dynamic-update-slice_fusion.refs_9_.refs_0_), channel_id=1, source_target_pairs={{0,4},{2,6},{4,0},{6,2},{8,12},{10,14},{12,8},{14,10},{16,20},{18,... | collective-permute-start | bytes 983048 | tf_op jit(solution)/shard_map/ppermute | solution.py:244
  18.2 11.9 %collective-permute-start.5 = (bf16[320,512]{1,0:T(8,128)(2,1)S(1)}, bf16[320,512]{1,0:T(8,128)(2,1)S(1)}, u32[]{:S(2)}, u32[]{:S(2)}) collective-permute-start(bf16[320,512]{1,0:T(8,128)(2,1)S(1)} %bitcast_dynamic-update-slice_fusion.refs_9_.refs_0_), channel_id=1, source_target_pairs={{0,2},{2,0},{4,6},{6,4},{8,10},{10,8},{12,14},{14,12},{16,18},{18,... | collective-permute-start | bytes 983048 | tf_op jit(solution)/shard_map/ppermute | solution.py:244
  26.0 8.0 %collective-permute-start.8 = (bf16[128,1024]{1,0:T(8,128)(2,1)S(1)}, bf16[128,1024]{1,0:T(8,128)(2,1)S(1)}, u32[]{:S(2)}, u32[]{:S(2)}) collective-permute-start(bf16[128,1024]{1,0:T(8,128)(2,1)S(1)} %collective-permute-done.2.refs_1_), channel_id=1, source_target_pairs={{0,8},{2,10},{4,12},{6,14},{8,0},{10,2},{12,4},{14,6},{16,24},{18,... | collective-permute-start | bytes 786440 | tf_op jit(solution)/shard_map/ppermute | solution.py:244
  26.2 7.8 %collective-permute-start.9 = (bf16[128,1024]{1,0:T(8,128)(2,1)S(1)}, bf16[128,1024]{1,0:T(8,128)(2,1)S(1)}, u32[]{:S(2)}, u32[]{:S(2)}) collective-permute-start(bf16[128,1024]{1,0:T(8,128)(2,1)S(1)} %collective-permute-done.1.refs_0_), channel_id=1, source_target_pairs={{0,1},{1,0},{2,3},{3,2},{4,5},{5,4},{6,7},{7,6},{8,9},{9,8},{10,11... | collective-permute-start | bytes 786440 | tf_op jit(solution)/shard_map/ppermute | solution.py:247
  26.3 7.7 %collective-permute-start.10 = (bf16[128,1024]{1,0:T(8,128)(2,1)S(1)}, bf16[128,1024]{1,0:T(8,128)(2,1)S(1)}, u32[]{:S(2)}, u32[]{:S(2)}) collective-permute-start(bf16[128,1024]{1,0:T(8,128)(2,1)S(1)} %collective-permute-done.2.refs_1_), channel_id=1, source_target_pairs={{0,1},{1,0},{2,3},{3,2},{4,5},{5,4},{6,7},{7,6},{8,9},{9,8},{10,11... | collective-permute-start | bytes 786440 | tf_op jit(solution)/shard_map/ppermute | solution.py:247
  34.0 1.5 %collective-permute-start.11 = (bf16[128,1024]{1,0:T(8,128)(2,1)S(1)}, bf16[128,1024]{1,0:T(8,128)(2,1)S(1)}, u32[]{:S(2)}, u32[]{:S(2)}) collective-permute-start(bf16[128,1024]{1,0:T(8,128)(2,1)S(1)} %collective-permute-done.8.refs_2_), channel_id=1, source_target_pairs={{0,1},{1,0},{2,3},{3,2},{4,5},{5,4},{6,7},{7,6},{8,9},{9,8},{10,11... | collective-permute-start | bytes 786440 | tf_op jit(solution)/shard_map/ppermute | solution.py:247
  37.9 14.4 %collective-permute-start.16 = (bf16[1040,256]{1,0:T(8,128)(2,1)}, bf16[1040,256]{1,0:T(8,128)(2,1)S(1)}, u32[]{:S(2)}, u32[]{:S(2)}) collective-permute-start(bf16[1040,256]{1,0:T(8,128)(2,1)} %get-tuple-element.48.kv_ref.refs_0_), channel_id=1, source_target_pairs={{0,4},{2,6},{4,0},{6,2},{8,12},{10,14},{12,8},{14,10},{16,20},{18,... | collective-permute-start | bytes 1597448 | tf_op jit(solution)/shard_map/ppermute | solution.py:244
  39.2 14.1 %collective-permute-start.15 = (bf16[1040,256]{1,0:T(8,128)(2,1)}, bf16[1040,256]{1,0:T(8,128)(2,1)S(1)}, u32[]{:S(2)}, u32[]{:S(2)}) collective-permute-start(bf16[1040,256]{1,0:T(8,128)(2,1)} %get-tuple-element.48.kv_ref.refs_0_), channel_id=1, source_target_pairs={{0,2},{2,0},{4,6},{6,4},{8,10},{10,8},{12,14},{14,12},{16,18},{18,... | collective-permute-start | bytes 1597448 | tf_op jit(solution)/shard_map/ppermute | solution.py:244
  40.7 14.8 %collective-permute-start.13 = (bf16[256,512]{1,0:T(8,128)(2,1)S(1)}, bf16[256,512]{1,0:T(8,128)(2,1)S(1)}, u32[]{:S(2)}, u32[]{:S(2)}) collective-permute-start(bf16[256,512]{1,0:T(8,128)(2,1)S(1)} %get-tuple-element.46.refs_0_), channel_id=1, source_target_pairs={{0,8},{2,10},{4,12},{6,14},{8,0},{10,2},{12,4},{14,6},{16,24},{18,... | collective-permute-start | bytes 786440 | tf_op jit(solution)/shard_map/ppermute | solution.py:244
  41.0 14.5 %collective-permute-start.12 = (bf16[256,512]{1,0:T(8,128)(2,1)S(1)}, bf16[256,512]{1,0:T(8,128)(2,1)S(1)}, u32[]{:S(2)}, u32[]{:S(2)}) collective-permute-start(bf16[256,512]{1,0:T(8,128)(2,1)S(1)} %get-tuple-element.46.refs_0_), channel_id=1, source_target_pairs={{0,16},{2,18},{4,20},{6,22},{8,24},{10,26},{12,28},{14,30},{16,0},... | collective-permute-start | bytes 786440 | tf_op jit(solution)/shard_map/ppermute | solution.py:244
  43.4 1.0 %copy-start = (bf16[1040,256]{1,0:T(8,128)(2,1)S(1)}, bf16[1040,256]{1,0:T(8,128)(2,1)}, u32[]{:S(2)}) copy-start(bf16[1040,256]{1,0:T(8,128)(2,1)} %get-tuple-element.48.kv_ref.refs_0_) | copy-start | bytes 1597444
  44.5 2.6 %copy-start.1 = (bf16[1040,256]{1,0:T(8,128)(2,1)S(1)}, bf16[1040,256]{1,0:T(8,128)(2,1)}, u32[]{:S(2)}) copy-start(bf16[1040,256]{1,0:T(8,128)(2,1)} %get-tuple-element.48.kv_ref.refs_0_) | copy-start | bytes 1597444
  53.3 7.7 %collective-permute-start.18 = (bf16[528,256]{1,0:T(8,128)(2,1)S(1)}, bf16[528,256]{1,0:T(8,128)(2,1)S(1)}, u32[]{:S(2)}, u32[]{:S(2)}) collective-permute-start(bf16[528,256]{1,0:T(8,128)(2,1)S(1)} %slice.19), channel_id=1, source_target_pairs={{0,4},{2,6},{4,0},{6,2},{8,12},{10,14},{12,8},{14,10},{16,20},{18,... | collective-permute-start | bytes 811016 | tf_op jit(solution)/shard_map/ppermute | solution.py:244
  54.1 7.0 %collective-permute-start.17 = (bf16[512,256]{1,0:T(8,128)(2,1)S(1)}, bf16[512,256]{1,0:T(8,128)(2,1)S(1)}, u32[]{:S(2)}, u32[]{:S(2)}) collective-permute-start(bf16[512,256]{1,0:T(8,128)(2,1)S(1)} %slice.18), channel_id=1, source_target_pairs={{0,2},{2,0},{4,6},{6,4},{8,10},{10,8},{12,14},{14,12},{16,18},{18,... | collective-permute-start | bytes 786440 | tf_op jit(solution)/shard_map/ppermute | solution.py:244
  55.5 7.3 %collective-permute-start.14 = (bf16[256,512]{1,0:T(8,128)(2,1)S(1)}, bf16[256,512]{1,0:T(8,128)(2,1)S(1)}, u32[]{:S(2)}, u32[]{:S(2)}) collective-permute-start(bf16[256,512]{1,0:T(8,128)(2,1)S(1)} %collective-permute-done.12.refs_2_), channel_id=1, source_target_pairs={{0,8},{2,10},{4,12},{6,14},{8,0},{10,2},{12,4},{14,6},{16,24},{18,... | collective-permute-start | bytes 786440 | tf_op jit(solution)/shard_map/ppermute | solution.py:244
  63.4 14.8 %collective-permute-start.19 = (bf16[512,512]{1,0:T(8,128)(2,1)S(1)}, bf16[512,512]{1,0:T(8,128)(2,1)S(1)}, u32[]{:S(2)}, u32[]{:S(2)}) collective-permute-start(bf16[512,512]{1,0:T(8,128)(2,1)S(1)} %get-tuple-element.62), channel_id=1, source_target_pairs={{0,1},{1,0},{2,3},{3,2},{4,5},{5,4},{6,7},{7,6},{8,9},{9,8},{10,11... | collective-permute-start | bytes 1572872 | tf_op jit(solution)/shard_map/ppermute | solution.py:247
  63.5 8.1 %collective-permute-start.20 = (bf16[256,256]{1,0:T(8,128)(2,1)S(1)}, bf16[256,256]{1,0:T(8,128)(2,1)S(1)}, u32[]{:S(2)}, u32[]{:S(2)}) collective-permute-start(bf16[256,256]{1,0:T(8,128)(2,1)S(1)} %get-tuple-element.64), channel_id=1, source_target_pairs={{0,8},{2,10},{4,12},{6,14},{8,0},{10,2},{12,4},{14,6},{16,24},{18,... | collective-permute-start | bytes 393224 | tf_op jit(solution)/shard_map/ppermute | solution.py:244
  63.8 12.9 %collective-permute-start.21 = (bf16[256,256]{1,0:T(8,128)(2,1)S(1)}, bf16[256,256]{1,0:T(8,128)(2,1)S(1)}, u32[]{:S(2)}, u32[]{:S(2)}) collective-permute-start(bf16[256,256]{1,0:T(8,128)(2,1)S(1)} %get-tuple-element.65), channel_id=1, source_target_pairs={{0,16},{2,18},{4,20},{6,22},{8,24},{10,26},{12,28},{14,30},{16,0},... | collective-permute-start | bytes 393224 | tf_op jit(solution)/shard_map/ppermute | solution.py:244
  66.2 10.5 %collective-permute-start.22 = (bf16[256,256]{1,0:T(8,128)(2,1)S(1)}, bf16[256,256]{1,0:T(8,128)(2,1)S(1)}, u32[]{:S(2)}, u32[]{:S(2)}) collective-permute-start(bf16[256,256]{1,0:T(8,128)(2,1)S(1)} %get-tuple-element.66), channel_id=1, source_target_pairs={{0,24},{2,26},{4,28},{6,30},{8,16},{10,18},{12,20},{14,22},{16,8},... | collective-permute-start | bytes 393224 | tf_op jit(solution)/shard_map/ppermute | solution.py:244
  67.9 9.3 %collective-permute-start.23 = (bf16[256,256]{1,0:T(8,128)(2,1)S(1)}, bf16[256,256]{1,0:T(8,128)(2,1)S(1)}, u32[]{:S(2)}, u32[]{:S(2)}) collective-permute-start(bf16[256,256]{1,0:T(8,128)(2,1)S(1)} %get-tuple-element.63.refs_0_), channel_id=1, source_target_pairs={{0,1},{1,0},{2,3},{3,2},{4,5},{5,4},{6,7},{7,6},{8,9},{9,8},{10,11... | collective-permute-start | bytes 393224 | tf_op jit(solution)/shard_map/ppermute | solution.py:247
  71.6 5.7 %collective-permute-start.24 = (bf16[256,256]{1,0:T(8,128)(2,1)S(1)}, bf16[256,256]{1,0:T(8,128)(2,1)S(1)}, u32[]{:S(2)}, u32[]{:S(2)}) collective-permute-start(bf16[256,256]{1,0:T(8,128)(2,1)S(1)} %collective-permute-done.20.refs_1_), channel_id=1, source_target_pairs={{0,1},{1,0},{2,3},{3,2},{4,5},{5,4},{6,7},{7,6},{8,9},{9,8},{10,11... | collective-permute-start | bytes 393224 | tf_op jit(solution)/shard_map/ppermute | solution.py:247
  76.7 1.3 %collective-permute-start.25 = (bf16[256,256]{1,0:T(8,128)(2,1)S(1)}, bf16[256,256]{1,0:T(8,128)(2,1)S(1)}, u32[]{:S(2)}, u32[]{:S(2)}) collective-permute-start(bf16[256,256]{1,0:T(8,128)(2,1)S(1)} %collective-permute-done.21.refs_2_), channel_id=1, source_target_pairs={{0,1},{1,0},{2,3},{3,2},{4,5},{5,4},{6,7},{7,6},{8,9},{9,8},{10,11... | collective-permute-start | bytes 393224 | tf_op jit(solution)/shard_map/ppermute | solution.py:247
  76.7 1.5 %collective-permute-start.26 = (bf16[256,256]{1,0:T(8,128)(2,1)S(1)}, bf16[256,256]{1,0:T(8,128)(2,1)S(1)}, u32[]{:S(2)}, u32[]{:S(2)}) collective-permute-start(bf16[256,256]{1,0:T(8,128)(2,1)S(1)} %collective-permute-done.22.refs_3_), channel_id=1, source_target_pairs={{0,1},{1,0},{2,3},{3,2},{4,5},{5,4},{6,7},{7,6},{8,9},{9,8},{10,11... | collective-permute-start | bytes 393224 | tf_op jit(solution)/shard_map/ppermute | solution.py:247

commit v5 on v4

--- a/solution.py
+++ b/solution.py
@@ -57,7 +57,7 @@
     arrived, refs = refs[: lead - 1], refs[lead - 1 :]
     others, refs = refs[: lead - 1], refs[lead - 1 :]
     marks, refs = refs[: lead - 1], refs[lead - 1 :]
-    weights, (kv_ref, all_ref, columns_ref, wbuf) = refs[:lines], refs[lines:]
+    weights, (kv_ref, columns_ref, wbuf, all_ref) = refs[:lines], refs[lines:]
     a, i, c = ids[0], ids[1], ids[2]
     rows = normed.shape[0]
     half = rows // 2
@@ -83,13 +83,21 @@
     kv_ref[lead * rows :, :] = stamp_tile.astype(jnp.bfloat16)
 
 
-def queries_kernel(lead, lines, ids, normed_all, time_bias, kv_ref, *refs):
-    weights, (q_ref, *gate_refs, wbuf, ubuf) = refs[:lines], refs[lines:]
-    a, i = ids[0], ids[1]
+def queries_kernel(lead, lines, ids, normed, time_bias, kv_ref, *refs):
+    arrived, refs = refs[: lead - 1], refs[lead - 1 :]
+    others, refs = refs[: lead - 1], refs[lead - 1 :]
+    weights, (q_ref, *gate_refs, wbuf, ubuf, xbuf) = refs[:lines], refs[lines:]
+    a, i, c = ids[0], ids[1], ids[2]
     size = wbuf.shape[1] // 2
     buckets = time_bias.shape[1]
     chunk = wbuf.shape[0] // (lead * lines)
-    rows = normed_all.shape[0] // lead
+    rows = normed.shape[0]
+    half = rows // 2
+    xbuf[pl.ds(pl.multiple_of(a * rows, rows), rows), :] = normed[...]
+    for k in range(1, lead):
+        for side, block in ((c, arrived[k - 1]), (1 - c, others[k - 1])):
+            place = (a ^ k) * rows + side * half
+            xbuf[pl.ds(pl.multiple_of(place, half), half), :] = block[...]
     gather_weights(lead, lines, a, i, weights, wbuf, (2, 0))
     bias = time_bias[...].astype(jnp.float32) * 0.5
     picked = lax.broadcasted_iota(jnp.int32, bias.shape, 0) == a
@@ -100,7 +108,7 @@
     scale = 0.5 / math.sqrt(size)
     for p in range(lead):
         block = slice(p * rows, (p + 1) * rows)
-        product = jnp.dot(normed_all[block, :], wbuf[...], preferred_element_type=jnp.float32)
+        product = jnp.dot(xbuf[block, :], wbuf[...], preferred_element_type=jnp.float32)
         active = half_silu(0.5 * product)
         q_ref[block, :size] = (active[:, :size] * scale).astype(jnp.bfloat16)
         ubuf[block, :] = active[:, size:].astype(jnp.bfloat16)
@@ -250,7 +258,8 @@
         return jax.ShapeDtypeStruct(dims, dtype)
 
     by_head = w_uvqk.reshape(chunk, 4, lead, size).transpose(2, 0, 1, 3).reshape(lead, chunk, -1)
-    stamp_rows = jnp.pad(stamps.astype(bf16)[None, :], ((0, PAD - 1), (0, 4 * size - rows)))
+    stamp_rows = jnp.broadcast_to(stamps[None, :], (PAD, rows)).astype(bf16)
+    stamp_rows = jnp.tile(stamp_rows, (1, -(-4 * size // rows)))[:, : 4 * size]
     sent = [
         jnp.concatenate([lax.dynamic_index_in_dim(by_head, a ^ k, 0, False), stamp_rows])
         for k in range(lead)
@@ -274,19 +283,23 @@
     others.append(swap(last_half))
 
     span = lead * rows
-    kv, normed_all, columns = call(
+    kv, columns = call(
         functools.partial(keys_kernel, lead, lines),
         [ids, normed, sent[0], *arrived, *others, *got, *stacks],
-        [shape(span + PAD, 2 * size), shape(span, width), shape(lines * chunk, w_out.shape[0])],
-        [pltpu.VMEM((width, 2 * size), bf16)],
+        [shape(span + PAD, 2 * size), shape(lines * chunk, w_out.shape[0])],
+        [pltpu.VMEM((width, 2 * size), bf16), pltpu.VMEM((span, width), bf16)],
     )
     direct = [exchange(kv, j) for j in ((1, 2) if lines == 4 else range(1, lines))]
     near, far = exchange(columns, lines), exchange(columns, 2 * lines)
     queries, *gates = call(
         functools.partial(queries_kernel, lead, lines),
-        [ids, normed_all, time_bias, kv, *stacks],
+        [ids, normed, time_bias, kv, *arrived, *others, *stacks],
         [shape(span, size + time_bias.shape[1])] + [shape(rows, size)] * lead,
-        [pltpu.VMEM((width, 2 * size), bf16), pltpu.VMEM((span, size), bf16)],
+        [
+            pltpu.VMEM((width, 2 * size), bf16),
+            pltpu.VMEM((span, size), bf16),
+            pltpu.VMEM((span, width), bf16),
+        ],
     )
 
     def attend(j, total):

time: 81 us -> 81 us (level)
  waiting for transfers between devices: 37.5 us -> 38.6 us
    ppermute x19, waiting for transfers between devices: 35 us -> 36 us  [exchange(): return lax.ppermute(x, 'seq', [(t, t ^ flip) for t in range(devices)])]
  transfers between devices with their start and end apart: 27 -> 27, of which waited for: 14 -> 14; matrix products, arithmetic and copies ran while one was open for 0% -> 0% of each run, Pallas kernels for 13% -> 12%
where the time goes in v5:
time: 81 us; the launch traced here: 80.8 us
  waiting for transfers between devices  38.6 us (48%)
  starting transfers between devices  23.7 us (29%)
  Pallas kernels  15.3 us (19%)
  local copies, waits for them, and re-layouts  2.88 us (4%)
    ppermute x19, waiting for transfers between devices, exchange(): return lax.ppermute(x, 'seq', [(t, t ^ flip) for t in range(devices)])  36 us
    ppermute x19, starting transfers between devices, exchange(): return lax.ppermute(x, 'seq', [(t, t ^ flip) for t in range(devices)])  23.1 us
    pallas_call x9, Pallas kernels, call(): pl.pallas_call(kernel, out_shape=outs, in_specs=[pl.BlockSpec(memory_spac...  15.3 us
    ppermute x8, waiting for transfers between devices, swap(): return lax.ppermute(x, 'head', [(0, 1), (1, 0)])  2.55 us
  transfers between devices with their start and end apart: 27, of which 14 were waited for; matrix products, arithmetic and copies ran while one was open for 0% of the time, Pallas kernels for 12%

profile of v5, /device:TPU:0, one launch (start us, length us, event | category | flops | bytes accessed | tf_op | source)
XLA Modules:
  0.0 80.8 jit_solution(2821373727868632947)
XLA Ops:
  0.0 0.7 copy-done.5
  0.7 1.1 %reshape.10 = bf16[64,4,4,128]{3,2,1,0:T(4,128)(2,1)S(1)} reshape(bf16[64,4,512]{2,1,0:T(4,128)(2,1)} %param.6) | data formatting | bytes 524288 | tf_op jit(solution)/shard_map/reshape | solution.py:260
  1.8 0.1 copy.6
  1.9 0.1 reshape.11
  2.0 0.0 copy-start.2
  2.1 5.1 %collective-permute-start.4 = (bf16[80,512]{1,0:T(8,128)(2,1)S(1)}, bf16[80,512]{1,0:T(8,128)(2,1)S(1)}, u32[]{:S(2)}, u32[]{:S(2)}) collective-permute-start(bf16[80,512]{1,0:T(8,128)(2,1)S(1)} %get-tuple-element.70), channel_id=1, source_target_pairs={{0,24},{2,26},{4,28},{6,30},{8,16},{10,18},{12,20},{14,22},{16,8},... | collective-permute-start | bytes 245768 | tf_op jit(solution)/shard_map/ppermute | solution.py:252
  7.2 0.6 collective-permute-start.3
  7.9 0.1 pad_add_fusion.ids
  7.9 0.9 %shard_map.55 = (bf16[256,1024]{1,0:T(8,128)(2,1)S(1)}, bf16[128,1024]{1,0:T(8,128)(2,1)S(1)}) custom-call(s32[3]{0:T(128)S(1)} %pad_add_fusion.ids, bf16[256,1024]{1,0:T(8,128)(2,1)S(1)} %copy-done.2), custom_call_target="tpu_custom_call" | custom-call | flops 1 | bytes 1 | tf_op jit(solution)/shard_map/pallas_call | solution.py:226
  8.9 4.6 %collective-permute-done.refs_6_ = bf16[80,512]{1,0:T(8,128)(2,1)S(1)} collective-permute-done((bf16[80,512]{1,0:T(8,128)(2,1)S(1)}, bf16[80,512]{1,0:T(8,128)(2,1)S(1)}, u32[]{:S(2)}, u32[]{:S(2)}) %collective-permute-start) | collective-permute-done | bytes 81952 | tf_op jit(solution)/shard_map/ppermute | solution.py:252
  13.5 1.3 %collective-permute-start.1 = (bf16[128,1024]{1,0:T(8,128)(2,1)S(1)}, bf16[128,1024]{1,0:T(8,128)(2,1)S(1)}, u32[]{:S(2)}, u32[]{:S(2)}) collective-permute-start(bf16[128,1024]{1,0:T(8,128)(2,1)S(1)} %get-tuple-element.37), channel_id=1, source_target_pairs={{0,8},{2,10},{4,12},{6,14},{8,0},{10,2},{12,4},{14,6},{16,24},{18,... | collective-permute-start | bytes 786440 | tf_op jit(solution)/shard_map/ppermute | solution.py:252
  14.8 0.0 copy-start.4
  14.8 0.0 collective-permute-done.4.refs_8_
  14.8 0.8 copy-done.4
  15.6 2.7 %collective-permute-start.7 = (bf16[320,512]{1,0:T(8,128)(2,1)S(1)}, bf16[320,512]{1,0:T(8,128)(2,1)S(1)}, u32[]{:S(2)}, u32[]{:S(2)}) collective-permute-start(bf16[320,512]{1,0:T(8,128)(2,1)S(1)} %bitcast_dynamic-update-slice_fusion.refs_9_.refs_6_), channel_id=1, source_target_pairs={{0,6},{2,4},{4,2},{6,0},{8,14},{10,12},{12,10},{14,8},{16,22},{18,... | collective-permute-start | bytes 983048 | tf_op jit(solution)/shard_map/ppermute | solution.py:252
  18.4 0.5 collective-permute-start.6
  18.9 0.2 collective-permute-start.5
  19.1 6.9 %collective-permute-done.2.refs_1_ = bf16[128,1024]{1,0:T(8,128)(2,1)S(1)} collective-permute-done((bf16[128,1024]{1,0:T(8,128)(2,1)S(1)}, bf16[128,1024]{1,0:T(8,128)(2,1)S(1)}, u32[]{:S(2)}, u32[]{:S(2)}) %collective-permute-start.2) | collective-permute-done | bytes 262176 | tf_op jit(solution)/shard_map/ppermute | solution.py:252
  26.0 0.0 collective-permute-done.1.refs_0_
  26.0 0.2 collective-permute-start.8
  26.2 0.0 collective-permute-start.9
  26.2 0.8 %collective-permute-done.7.refs_12_.refs_9_ = bf16[320,512]{1,0:T(8,128)(2,1)S(1)} collective-permute-done((bf16[320,512]{1,0:T(8,128)(2,1)S(1)}, bf16[320,512]{1,0:T(8,128)(2,1)S(1)}, u32[]{:S(2)}, u32[]{:S(2)}) %collective-permute-start.7) | collective-permute-done | bytes 327712 | tf_op jit(solution)/shard_map/ppermute | solution.py:252
  27.0 0.0 collective-permute-start.10
  27.0 3.4 %collective-permute-done.6.refs_11_.refs_8_ = bf16[320,512]{1,0:T(8,128)(2,1)S(1)} collective-permute-done((bf16[320,512]{1,0:T(8,128)(2,1)S(1)}, bf16[320,512]{1,0:T(8,128)(2,1)S(1)}, u32[]{:S(2)}, u32[]{:S(2)}) %collective-permute-start.6) | collective-permute-done | bytes 327712 | tf_op jit(solution)/shard_map/ppermute | solution.py:252
  30.4 0.3 collective-permute-done.5.refs_10_.refs_7_
  30.7 3.3 %collective-permute-done.8.refs_2_ = bf16[128,1024]{1,0:T(8,128)(2,1)S(1)} collective-permute-done((bf16[128,1024]{1,0:T(8,128)(2,1)S(1)}, bf16[128,1024]{1,0:T(8,128)(2,1)S(1)}, u32[]{:S(2)}, u32[]{:S(2)}) %collective-permute-start.8) | collective-permute-done | bytes 262176 | tf_op jit(solution)/shard_map/ppermute | solution.py:252
  34.0 0.0 collective-permute-start.11
  34.0 0.0 collective-permute-done.10.refs_4_
  34.0 0.0 collective-permute-done.9.refs_3_
  34.0 1.5 %collective-permute-done.11.refs_5_ = bf16[128,1024]{1,0:T(8,128)(2,1)S(1)} collective-permute-done((bf16[128,1024]{1,0:T(8,128)(2,1)S(1)}, bf16[128,1024]{1,0:T(8,128)(2,1)S(1)}, u32[]{:S(2)}, u32[]{:S(2)}) %collective-permute-start.11) | collective-permute-done | bytes 262176 | tf_op jit(solution)/shard_map/ppermute | solution.py:255
  35.5 2.3 %shard_map.56 = (bf16[1040,256]{1,0:T(8,128)(2,1)}, bf16[256,512]{1,0:T(8,128)(2,1)S(1)}) custom-call(s32[3]{0:T(128)S(1)} %pad_add_fusion.ids, bf16[256,1024]{1,0:T(8,128)(2,1)S(1)} %get-tuple-element.35.normed, bf16[80,512]{1,0:T(8,128)(2,1)S(1)} %get-tuple-element.73.own_msg, bf16[128,1024]{1,0:T(8,128)(2,1)S(1)} %collective-permute-done.1.refs_0_, ...), custom_call_target="tpu_custom_call" | custom-call | flops 1 | bytes 1 | tf_op jit(solution)/shard_map/pallas_call | solution.py:226
  37.8 1.3 %collective-permute-start.16 = (bf16[1040,256]{1,0:T(8,128)(2,1)}, bf16[1040,256]{1,0:T(8,128)(2,1)S(1)}, u32[]{:S(2)}, u32[]{:S(2)}) collective-permute-start(bf16[1040,256]{1,0:T(8,128)(2,1)} %get-tuple-element.46.kv_ref.refs_0_), channel_id=1, source_target_pairs={{0,4},{2,6},{4,0},{6,2},{8,12},{10,14},{12,8},{14,10},{16,20},{18,... | collective-permute-start | bytes 1597448 | tf_op jit(solution)/shard_map/ppermute | solution.py:252
  39.2 1.5 %collective-permute-start.15 = (bf16[1040,256]{1,0:T(8,128)(2,1)}, bf16[1040,256]{1,0:T(8,128)(2,1)S(1)}, u32[]{:S(2)}, u32[]{:S(2)}) collective-permute-start(bf16[1040,256]{1,0:T(8,128)(2,1)} %get-tuple-element.46.kv_ref.refs_0_), channel_id=1, source_target_pairs={{0,2},{2,0},{4,6},{6,4},{8,10},{10,8},{12,14},{14,12},{16,18},{18,... | collective-permute-start | bytes 1597448 | tf_op jit(solution)/shard_map/ppermute | solution.py:252
  40.7 0.3 collective-permute-start.13
  41.0 2.4 %collective-permute-start.12 = (bf16[256,512]{1,0:T(8,128)(2,1)S(1)}, bf16[256,512]{1,0:T(8,128)(2,1)S(1)}, u32[]{:S(2)}, u32[]{:S(2)}) collective-permute-start(bf16[256,512]{1,0:T(8,128)(2,1)S(1)} %get-tuple-element.45.refs_0_), channel_id=1, source_target_pairs={{0,16},{2,18},{4,20},{6,22},{8,24},{10,26},{12,28},{14,30},{16,0},... | collective-permute-start | bytes 786440 | tf_op jit(solution)/shard_map/ppermute | solution.py:252
  43.4 2.2 %shard_map.57 = (bf16[1024,256]{1,0:T(8,128)(2,1)S(1)}, bf16[256,128]{1,0:T(8,128)(2,1)S(1)}, bf16[256,128]{1,0:T(8,128)(2,1)S(1)}, bf16[256,128]{1,0:T(8,128)(2,1)S(1)}, bf16[256,128]{1,0:T(8,128)(2,1)S(1)}) custom-call(s32[3]{0:T(128)S(1)} %pad_add_fusion.ids, bf16[256,1024]{1,0:T(8,128)(2,1)} %copy-done.1, bf16[4,128]{1,0:T(4,128)(2,1)S(1)} %copy-done.3, ...), custom_call_target="tpu_custom_call" | custom-call | flops 1 | bytes 1 | tf_op jit(solution)/shard_map/pallas_call | solution.py:226
  45.6 1.8 %shard_map.58.refs_1_ = f32[1024,128]{1,0:T(8,128)S(1)} custom-call(s32[3]{0:T(128)S(1)} %pad_add_fusion.ids, bf16[1024,256]{1,0:T(8,128)(2,1)S(1)} %get-tuple-element.47.q_ref, bf16[1040,256]{1,0:T(8,128)(2,1)S(1)} %copy-done), custom_call_target="tpu_custom_call" | custom-call | flops 1 | bytes 1 | tf_op jit(solution)/shard_map/pallas_call | solution.py:226
  47.4 4.8 %collective-permute-done.16.refs_0_ = bf16[1040,256]{1,0:T(8,128)(2,1)S(1)} collective-permute-done((bf16[1040,256]{1,0:T(8,128)(2,1)}, bf16[1040,256]{1,0:T(8,128)(2,1)S(1)}, u32[]{:S(2)}, u32[]{:S(2)}) %collective-permute-start.16) | collective-permute-done | bytes 532512 | tf_op jit(solution)/shard_map/ppermute | solution.py:252
  52.2 1.1 %collective-permute-done.15.refs_0_ = bf16[1040,256]{1,0:T(8,128)(2,1)S(1)} collective-permute-done((bf16[1040,256]{1,0:T(8,128)(2,1)}, bf16[1040,256]{1,0:T(8,128)(2,1)S(1)}, u32[]{:S(2)}, u32[]{:S(2)}) %collective-permute-start.15) | collective-permute-done | bytes 532512 | tf_op jit(solution)/shard_map/ppermute | solution.py:252
  53.3 0.7 collective-permute-start.18
  54.0 1.4 %collective-permute-start.17 = (bf16[512,256]{1,0:T(8,128)(2,1)S(1)}, bf16[512,256]{1,0:T(8,128)(2,1)S(1)}, u32[]{:S(2)}, u32[]{:S(2)}) collective-permute-start(bf16[512,256]{1,0:T(8,128)(2,1)S(1)} %slice.18), channel_id=1, source_target_pairs={{0,2},{2,0},{4,6},{6,4},{8,10},{10,8},{12,14},{14,12},{16,18},{18,... | collective-permute-start | bytes 786440 | tf_op jit(solution)/shard_map/ppermute | solution.py:252
  55.4 0.0 collective-permute-done.13.refs_1_
  55.4 0.0 collective-permute-done.12.refs_2_
  55.4 0.3 collective-permute-start.14
  55.7 1.6 %shard_map.59.refs_1_ = f32[1024,128]{1,0:T(8,128)S(1)} custom-call(s32[3]{0:T(128)S(1)} %pad_add_fusion.ids, bf16[1024,256]{1,0:T(8,128)(2,1)S(1)} %get-tuple-element.47.q_ref, bf16[1040,256]{1,0:T(8,128)(2,1)S(1)} %collective-permute-done.15.refs_0_, f32[1024,128]{1,0:T(8,128)S(1)} %shard_map.58.refs_1_), custom_call_target="tpu_custom_call" | custom-call | flops 1 | bytes 1 | tf_op jit(solution)/shard_map/pallas_call | solution.py:226
  57.3 1.6 %shard_map.60.refs_2_ = f32[1024,128]{1,0:T(8,128)S(1)} custom-call(s32[3]{0:T(128)S(1)} %pad_add_fusion.ids, bf16[1024,256]{1,0:T(8,128)(2,1)S(1)} %get-tuple-element.47.q_ref, bf16[1040,256]{1,0:T(8,128)(2,1)S(1)} %collective-permute-done.16.refs_0_, f32[1024,128]{1,0:T(8,128)S(1)} %shard_map.59.refs_1_), custom_call_target="tpu_custom_call" | custom-call | flops 1 | bytes 1 | tf_op jit(solution)/shard_map/pallas_call | solution.py:226
  59.0 2.1 %collective-permute-done.17.refs_0_ = bf16[512,256]{1,0:T(8,128)(2,1)S(1)} collective-permute-done((bf16[512,256]{1,0:T(8,128)(2,1)S(1)}, bf16[512,256]{1,0:T(8,128)(2,1)S(1)}, u32[]{:S(2)}, u32[]{:S(2)}) %collective-permute-start.17) | collective-permute-done | bytes 262176 | tf_op jit(solution)/shard_map/ppermute | solution.py:252
  61.0 1.7 %shard_map.61 = (bf16[256,256]{1,0:T(8,128)(2,1)S(1)}, bf16[256,256]{1,0:T(8,128)(2,1)S(1)}, bf16[256,256]{1,0:T(8,128)(2,1)S(1)}, bf16[256,256]{1,0:T(8,128)(2,1)S(1)}) custom-call(s32[3]{0:T(128)S(1)} %pad_add_fusion.ids, bf16[1024,256]{1,0:T(8,128)(2,1)S(1)} %get-tuple-element.47.q_ref, bf16[512,256]{1,0:T(8,128)(2,1)S(1)} %collective-permute-done.17.refs_0_, ...), custom_call_target="tpu_custom_call" | custom-call | flops 1 | bytes 1 | tf_op jit(solution)/shard_map/pallas_call | solution.py:226
  62.7 0.0 collective-permute-done.14.refs_3_
  62.7 0.6 shard_map.62
  63.4 0.1 collective-permute-start.19
  63.4 0.4 collective-permute-start.20
  63.8 2.3 %collective-permute-start.21 = (bf16[256,256]{1,0:T(8,128)(2,1)S(1)}, bf16[256,256]{1,0:T(8,128)(2,1)S(1)}, u32[]{:S(2)}, u32[]{:S(2)}) collective-permute-start(bf16[256,256]{1,0:T(8,128)(2,1)S(1)} %get-tuple-element.63), channel_id=1, source_target_pairs={{0,16},{2,18},{4,20},{6,22},{8,24},{10,26},{12,28},{14,30},{16,0},... | collective-permute-start | bytes 393224 | tf_op jit(solution)/shard_map/ppermute | solution.py:252
  66.1 1.8 %collective-permute-start.22 = (bf16[256,256]{1,0:T(8,128)(2,1)S(1)}, bf16[256,256]{1,0:T(8,128)(2,1)S(1)}, u32[]{:S(2)}, u32[]{:S(2)}) collective-permute-start(bf16[256,256]{1,0:T(8,128)(2,1)S(1)} %get-tuple-element.64), channel_id=1, source_target_pairs={{0,24},{2,26},{4,28},{6,30},{8,16},{10,18},{12,20},{14,22},{16,8},... | collective-permute-start | bytes 393224 | tf_op jit(solution)/shard_map/ppermute | solution.py:252
  67.9 0.0 collective-permute-start.23
  67.9 3.6 %collective-permute-done.20.refs_1_ = bf16[256,256]{1,0:T(8,128)(2,1)S(1)} collective-permute-done((bf16[256,256]{1,0:T(8,128)(2,1)S(1)}, bf16[256,256]{1,0:T(8,128)(2,1)S(1)}, u32[]{:S(2)}, u32[]{:S(2)}) %collective-permute-start.20) | collective-permute-done | bytes 131104 | tf_op jit(solution)/shard_map/ppermute | solution.py:252
  71.5 0.0 collective-permute-start.24
  71.5 5.2 %collective-permute-done.21.refs_2_ = bf16[256,256]{1,0:T(8,128)(2,1)S(1)} collective-permute-done((bf16[256,256]{1,0:T(8,128)(2,1)S(1)}, bf16[256,256]{1,0:T(8,128)(2,1)S(1)}, u32[]{:S(2)}, u32[]{:S(2)}) %collective-permute-start.21) | collective-permute-done | bytes 131104 | tf_op jit(solution)/shard_map/ppermute | solution.py:252
  76.7 0.0 collective-permute-start.25
  76.7 0.0 collective-permute-done.22.refs_3_
  76.7 0.5 collective-permute-start.26
  77.2 0.8 %collective-permute-done.25.refs_6_ = bf16[256,256]{1,0:T(8,128)(2,1)S(1)} collective-permute-done((bf16[256,256]{1,0:T(8,128)(2,1)S(1)}, bf16[256,256]{1,0:T(8,128)(2,1)S(1)}, u32[]{:S(2)}, u32[]{:S(2)}) %collective-permute-start.25) | collective-permute-done | bytes 131104 | tf_op jit(solution)/shard_map/ppermute | solution.py:255
  78.1 0.2 collective-permute-done.26.refs_7_
  78.2 2.5 %shard_map.63 = bf16[256,512]{1,0:T(8,128)(2,1)} custom-call(s32[3]{0:T(128)S(1)} %pad_add_fusion.ids, bf16[256,1024]{1,0:T(8,128)(2,1)S(1)} %copy-done.2, bf16[512,512]{1,0:T(8,128)(2,1)S(1)} %get-tuple-element.59.kept, bf16[512,512]{1,0:T(8,128)(2,1)S(1)} %collective-permute-done.19.given, bf16[256,256]{1,0:T(8,128)(2,1)S(1)} %get-tuple-element.61.refs_0_, ...), custom_call_target="tpu_custom_call" | custom-call | flops 1 | bytes 1 | tf_op jit(solution)/shard_map/pallas_call | solution.py:226
  (28 shorter events, 0.2 us)
Async XLA Ops:
  0.0 0.7 copy-start.5
  2.0 5.9 %copy-start.2 = (bf16[256,1024]{1,0:T(8,128)(2,1)S(1)}, bf16[256,1024]{1,0:T(8,128)(2,1)}, u32[]{:S(2)}) copy-start(bf16[256,1024]{1,0:T(8,128)(2,1)} %events.3) | copy-start | bytes 1572868
  2.1 12.7 %collective-permute-start.4 = (bf16[80,512]{1,0:T(8,128)(2,1)S(1)}, bf16[80,512]{1,0:T(8,128)(2,1)S(1)}, u32[]{:S(2)}, u32[]{:S(2)}) collective-permute-start(bf16[80,512]{1,0:T(8,128)(2,1)S(1)} %get-tuple-element.70), channel_id=1, source_target_pairs={{0,24},{2,26},{4,28},{6,30},{8,16},{10,18},{12,20},{14,22},{16,8},... | collective-permute-start | bytes 245768 | tf_op jit(solution)/shard_map/ppermute | solution.py:252
  7.2 6.2 %collective-permute-start = (bf16[80,512]{1,0:T(8,128)(2,1)S(1)}, bf16[80,512]{1,0:T(8,128)(2,1)S(1)}, u32[]{:S(2)}, u32[]{:S(2)}) collective-permute-start(bf16[80,512]{1,0:T(8,128)(2,1)S(1)} %get-tuple-element.71), channel_id=1, source_target_pairs={{0,8},{2,10},{4,12},{6,14},{8,0},{10,2},{12,4},{14,6},{16,24},{18,... | collective-permute-start | bytes 245768 | tf_op jit(solution)/shard_map/ppermute | solution.py:252
  7.2 7.5 %collective-permute-start.3 = (bf16[80,512]{1,0:T(8,128)(2,1)S(1)}, bf16[80,512]{1,0:T(8,128)(2,1)S(1)}, u32[]{:S(2)}, u32[]{:S(2)}) collective-permute-start(bf16[80,512]{1,0:T(8,128)(2,1)S(1)} %get-tuple-element.72), channel_id=1, source_target_pairs={{0,16},{2,18},{4,20},{6,22},{8,24},{10,26},{12,28},{14,30},{16,0},... | collective-permute-start | bytes 245768 | tf_op jit(solution)/shard_map/ppermute | solution.py:252
  8.8 29.0 %copy-start.1 = (bf16[256,1024]{1,0:T(8,128)(2,1)}, bf16[256,1024]{1,0:T(8,128)(2,1)S(1)}, u32[]{:S(2)}) copy-start(bf16[256,1024]{1,0:T(8,128)(2,1)S(1)} %get-tuple-element.35.normed) | copy-start | bytes 1572868
  13.4 12.5 %collective-permute-start.2 = (bf16[128,1024]{1,0:T(8,128)(2,1)S(1)}, bf16[128,1024]{1,0:T(8,128)(2,1)S(1)}, u32[]{:S(2)}, u32[]{:S(2)}) collective-permute-start(bf16[128,1024]{1,0:T(8,128)(2,1)S(1)} %get-tuple-element.37), channel_id=1, source_target_pairs={{0,16},{2,18},{4,20},{6,22},{8,24},{10,26},{12,28},{14,30},{16,0},... | collective-permute-start | bytes 786440 | tf_op jit(solution)/shard_map/ppermute | solution.py:252
  13.5 12.5 %collective-permute-start.1 = (bf16[128,1024]{1,0:T(8,128)(2,1)S(1)}, bf16[128,1024]{1,0:T(8,128)(2,1)S(1)}, u32[]{:S(2)}, u32[]{:S(2)}) collective-permute-start(bf16[128,1024]{1,0:T(8,128)(2,1)S(1)} %get-tuple-element.37), channel_id=1, source_target_pairs={{0,8},{2,10},{4,12},{6,14},{8,0},{10,2},{12,4},{14,6},{16,24},{18,... | collective-permute-start | bytes 786440 | tf_op jit(solution)/shard_map/ppermute | solution.py:252
  14.8 0.8 %copy-start.4 = (bf16[512,64]{0,1:T(8,128)(2,1)S(1)}, bf16[512,64]{0,1:T(8,128)(2,1)}, u32[]{:S(2)}) copy-start(bf16[512,64]{0,1:T(8,128)(2,1)} %param.7) | copy-start | bytes 196612
  15.6 11.4 %collective-permute-start.7 = (bf16[320,512]{1,0:T(8,128)(2,1)S(1)}, bf16[320,512]{1,0:T(8,128)(2,1)S(1)}, u32[]{:S(2)}, u32[]{:S(2)}) collective-permute-start(bf16[320,512]{1,0:T(8,128)(2,1)S(1)} %bitcast_dynamic-update-slice_fusion.refs_9_.refs_6_), channel_id=1, source_target_pairs={{0,6},{2,4},{4,2},{6,0},{8,14},{10,12},{12,10},{14,8},{16,22},{18,... | collective-permute-start | bytes 983048 | tf_op jit(solution)/shard_map/ppermute | solution.py:252
  18.4 12.1 %collective-permute-start.6 = (bf16[320,512]{1,0:T(8,128)(2,1)S(1)}, bf16[320,512]{1,0:T(8,128)(2,1)S(1)}, u32[]{:S(2)}, u32[]{:S(2)}) collective-permute-start(bf16[320,512]{1,0:T(8,128)(2,1)S(1)} %bitcast_dynamic-update-slice_fusion.refs_9_.refs_6_), channel_id=1, source_target_pairs={{0,4},{2,6},{4,0},{6,2},{8,12},{10,14},{12,8},{14,10},{16,20},{18,... | collective-permute-start | bytes 983048 | tf_op jit(solution)/shard_map/ppermute | solution.py:252
  18.9 11.9 %collective-permute-start.5 = (bf16[320,512]{1,0:T(8,128)(2,1)S(1)}, bf16[320,512]{1,0:T(8,128)(2,1)S(1)}, u32[]{:S(2)}, u32[]{:S(2)}) collective-permute-start(bf16[320,512]{1,0:T(8,128)(2,1)S(1)} %bitcast_dynamic-update-slice_fusion.refs_9_.refs_6_), channel_id=1, source_target_pairs={{0,2},{2,0},{4,6},{6,4},{8,10},{10,8},{12,14},{14,12},{16,18},{18,... | collective-permute-start | bytes 983048 | tf_op jit(solution)/shard_map/ppermute | solution.py:252
  26.0 8.0 %collective-permute-start.8 = (bf16[128,1024]{1,0:T(8,128)(2,1)S(1)}, bf16[128,1024]{1,0:T(8,128)(2,1)S(1)}, u32[]{:S(2)}, u32[]{:S(2)}) collective-permute-start(bf16[128,1024]{1,0:T(8,128)(2,1)S(1)} %collective-permute-done.2.refs_1_), channel_id=1, source_target_pairs={{0,8},{2,10},{4,12},{6,14},{8,0},{10,2},{12,4},{14,6},{16,24},{18,... | collective-permute-start | bytes 786440 | tf_op jit(solution)/shard_map/ppermute | solution.py:252
  26.2 7.8 %collective-permute-start.9 = (bf16[128,1024]{1,0:T(8,128)(2,1)S(1)}, bf16[128,1024]{1,0:T(8,128)(2,1)S(1)}, u32[]{:S(2)}, u32[]{:S(2)}) collective-permute-start(bf16[128,1024]{1,0:T(8,128)(2,1)S(1)} %collective-permute-done.1.refs_0_), channel_id=1, source_target_pairs={{0,1},{1,0},{2,3},{3,2},{4,5},{5,4},{6,7},{7,6},{8,9},{9,8},{10,11... | collective-permute-start | bytes 786440 | tf_op jit(solution)/shard_map/ppermute | solution.py:255
  27.0 7.0 %collective-permute-start.10 = (bf16[128,1024]{1,0:T(8,128)(2,1)S(1)}, bf16[128,1024]{1,0:T(8,128)(2,1)S(1)}, u32[]{:S(2)}, u32[]{:S(2)}) collective-permute-start(bf16[128,1024]{1,0:T(8,128)(2,1)S(1)} %collective-permute-done.2.refs_1_), channel_id=1, source_target_pairs={{0,1},{1,0},{2,3},{3,2},{4,5},{5,4},{6,7},{7,6},{8,9},{9,8},{10,11... | collective-permute-start | bytes 786440 | tf_op jit(solution)/shard_map/ppermute | solution.py:255
  34.0 1.5 %collective-permute-start.11 = (bf16[128,1024]{1,0:T(8,128)(2,1)S(1)}, bf16[128,1024]{1,0:T(8,128)(2,1)S(1)}, u32[]{:S(2)}, u32[]{:S(2)}) collective-permute-start(bf16[128,1024]{1,0:T(8,128)(2,1)S(1)} %collective-permute-done.8.refs_2_), channel_id=1, source_target_pairs={{0,1},{1,0},{2,3},{3,2},{4,5},{5,4},{6,7},{7,6},{8,9},{9,8},{10,11... | collective-permute-start | bytes 786440 | tf_op jit(solution)/shard_map/ppermute | solution.py:255
  37.8 5.5 %copy-start.3 = (bf16[4,128]{1,0:T(4,128)(2,1)S(1)}, bf16[4,128]{1,0:T(4,128)(2,1)}, u32[]{:S(2)}) copy-start(bf16[4,128]{1,0:T(4,128)(2,1)} %time_bias.1) | copy-start | bytes 3076
  37.8 14.3 %collective-permute-start.16 = (bf16[1040,256]{1,0:T(8,128)(2,1)}, bf16[1040,256]{1,0:T(8,128)(2,1)S(1)}, u32[]{:S(2)}, u32[]{:S(2)}) collective-permute-start(bf16[1040,256]{1,0:T(8,128)(2,1)} %get-tuple-element.46.kv_ref.refs_0_), channel_id=1, source_target_pairs={{0,4},{2,6},{4,0},{6,2},{8,12},{10,14},{12,8},{14,10},{16,20},{18,... | collective-permute-start | bytes 1597448 | tf_op jit(solution)/shard_map/ppermute | solution.py:252
  39.2 14.1 %collective-permute-start.15 = (bf16[1040,256]{1,0:T(8,128)(2,1)}, bf16[1040,256]{1,0:T(8,128)(2,1)S(1)}, u32[]{:S(2)}, u32[]{:S(2)}) collective-permute-start(bf16[1040,256]{1,0:T(8,128)(2,1)} %get-tuple-element.46.kv_ref.refs_0_), channel_id=1, source_target_pairs={{0,2},{2,0},{4,6},{6,4},{8,10},{10,8},{12,14},{14,12},{16,18},{18,... | collective-permute-start | bytes 1597448 | tf_op jit(solution)/shard_map/ppermute | solution.py:252
  40.7 4.9 %copy-start = (bf16[1040,256]{1,0:T(8,128)(2,1)S(1)}, bf16[1040,256]{1,0:T(8,128)(2,1)}, u32[]{:S(2)}) copy-start(bf16[1040,256]{1,0:T(8,128)(2,1)} %get-tuple-element.46.kv_ref.refs_0_) | copy-start | bytes 1597444
  40.7 14.8 %collective-permute-start.13 = (bf16[256,512]{1,0:T(8,128)(2,1)S(1)}, bf16[256,512]{1,0:T(8,128)(2,1)S(1)}, u32[]{:S(2)}, u32[]{:S(2)}) collective-permute-start(bf16[256,512]{1,0:T(8,128)(2,1)S(1)} %get-tuple-element.45.refs_0_), channel_id=1, source_target_pairs={{0,8},{2,10},{4,12},{6,14},{8,0},{10,2},{12,4},{14,6},{16,24},{18,... | collective-permute-start | bytes 786440 | tf_op jit(solution)/shard_map/ppermute | solution.py:252
  41.0 14.5 %collective-permute-start.12 = (bf16[256,512]{1,0:T(8,128)(2,1)S(1)}, bf16[256,512]{1,0:T(8,128)(2,1)S(1)}, u32[]{:S(2)}, u32[]{:S(2)}) collective-permute-start(bf16[256,512]{1,0:T(8,128)(2,1)S(1)} %get-tuple-element.45.refs_0_), channel_id=1, source_target_pairs={{0,16},{2,18},{4,20},{6,22},{8,24},{10,26},{12,28},{14,30},{16,0},... | collective-permute-start | bytes 786440 | tf_op jit(solution)/shard_map/ppermute | solution.py:252
  53.3 7.7 %collective-permute-start.18 = (bf16[528,256]{1,0:T(8,128)(2,1)S(1)}, bf16[528,256]{1,0:T(8,128)(2,1)S(1)}, u32[]{:S(2)}, u32[]{:S(2)}) collective-permute-start(bf16[528,256]{1,0:T(8,128)(2,1)S(1)} %slice.19), channel_id=1, source_target_pairs={{0,4},{2,6},{4,0},{6,2},{8,12},{10,14},{12,8},{14,10},{16,20},{18,... | collective-permute-start | bytes 811016 | tf_op jit(solution)/shard_map/ppermute | solution.py:252
  54.0 7.0 %collective-permute-start.17 = (bf16[512,256]{1,0:T(8,128)(2,1)S(1)}, bf16[512,256]{1,0:T(8,128)(2,1)S(1)}, u32[]{:S(2)}, u32[]{:S(2)}) collective-permute-start(bf16[512,256]{1,0:T(8,128)(2,1)S(1)} %slice.18), channel_id=1, source_target_pairs={{0,2},{2,0},{4,6},{6,4},{8,10},{10,8},{12,14},{14,12},{16,18},{18,... | collective-permute-start | bytes 786440 | tf_op jit(solution)/shard_map/ppermute | solution.py:252
  55.4 7.3 %collective-permute-start.14 = (bf16[256,512]{1,0:T(8,128)(2,1)S(1)}, bf16[256,512]{1,0:T(8,128)(2,1)S(1)}, u32[]{:S(2)}, u32[]{:S(2)}) collective-permute-start(bf16[256,512]{1,0:T(8,128)(2,1)S(1)} %collective-permute-done.12.refs_2_), channel_id=1, source_target_pairs={{0,8},{2,10},{4,12},{6,14},{8,0},{10,2},{12,4},{14,6},{16,24},{18,... | collective-permute-start | bytes 786440 | tf_op jit(solution)/shard_map/ppermute | solution.py:252
  63.4 14.9 %collective-permute-start.19 = (bf16[512,512]{1,0:T(8,128)(2,1)S(1)}, bf16[512,512]{1,0:T(8,128)(2,1)S(1)}, u32[]{:S(2)}, u32[]{:S(2)}) collective-permute-start(bf16[512,512]{1,0:T(8,128)(2,1)S(1)} %get-tuple-element.60), channel_id=1, source_target_pairs={{0,1},{1,0},{2,3},{3,2},{4,5},{5,4},{6,7},{7,6},{8,9},{9,8},{10,11... | collective-permute-start | bytes 1572872 | tf_op jit(solution)/shard_map/ppermute | solution.py:255
  63.4 8.1 %collective-permute-start.20 = (bf16[256,256]{1,0:T(8,128)(2,1)S(1)}, bf16[256,256]{1,0:T(8,128)(2,1)S(1)}, u32[]{:S(2)}, u32[]{:S(2)}) collective-permute-start(bf16[256,256]{1,0:T(8,128)(2,1)S(1)} %get-tuple-element.62), channel_id=1, source_target_pairs={{0,8},{2,10},{4,12},{6,14},{8,0},{10,2},{12,4},{14,6},{16,24},{18,... | collective-permute-start | bytes 393224 | tf_op jit(solution)/shard_map/ppermute | solution.py:252
  63.8 12.9 %collective-permute-start.21 = (bf16[256,256]{1,0:T(8,128)(2,1)S(1)}, bf16[256,256]{1,0:T(8,128)(2,1)S(1)}, u32[]{:S(2)}, u32[]{:S(2)}) collective-permute-start(bf16[256,256]{1,0:T(8,128)(2,1)S(1)} %get-tuple-element.63), channel_id=1, source_target_pairs={{0,16},{2,18},{4,20},{6,22},{8,24},{10,26},{12,28},{14,30},{16,0},... | collective-permute-start | bytes 393224 | tf_op jit(solution)/shard_map/ppermute | solution.py:252
  66.1 10.6 %collective-permute-start.22 = (bf16[256,256]{1,0:T(8,128)(2,1)S(1)}, bf16[256,256]{1,0:T(8,128)(2,1)S(1)}, u32[]{:S(2)}, u32[]{:S(2)}) collective-permute-start(bf16[256,256]{1,0:T(8,128)(2,1)S(1)} %get-tuple-element.64), channel_id=1, source_target_pairs={{0,24},{2,26},{4,28},{6,30},{8,16},{10,18},{12,20},{14,22},{16,8},... | collective-permute-start | bytes 393224 | tf_op jit(solution)/shard_map/ppermute | solution.py:252
  67.9 9.3 %collective-permute-start.23 = (bf16[256,256]{1,0:T(8,128)(2,1)S(1)}, bf16[256,256]{1,0:T(8,128)(2,1)S(1)}, u32[]{:S(2)}, u32[]{:S(2)}) collective-permute-start(bf16[256,256]{1,0:T(8,128)(2,1)S(1)} %get-tuple-element.61.refs_0_), channel_id=1, source_target_pairs={{0,1},{1,0},{2,3},{3,2},{4,5},{5,4},{6,7},{7,6},{8,9},{9,8},{10,11... | collective-permute-start | bytes 393224 | tf_op jit(solution)/shard_map/ppermute | solution.py:255
  71.5 5.7 %collective-permute-start.24 = (bf16[256,256]{1,0:T(8,128)(2,1)S(1)}, bf16[256,256]{1,0:T(8,128)(2,1)S(1)}, u32[]{:S(2)}, u32[]{:S(2)}) collective-permute-start(bf16[256,256]{1,0:T(8,128)(2,1)S(1)} %collective-permute-done.20.refs_1_), channel_id=1, source_target_pairs={{0,1},{1,0},{2,3},{3,2},{4,5},{5,4},{6,7},{7,6},{8,9},{9,8},{10,11... | collective-permute-start | bytes 393224 | tf_op jit(solution)/shard_map/ppermute | solution.py:255
  76.7 1.3 %collective-permute-start.25 = (bf16[256,256]{1,0:T(8,128)(2,1)S(1)}, bf16[256,256]{1,0:T(8,128)(2,1)S(1)}, u32[]{:S(2)}, u32[]{:S(2)}) collective-permute-start(bf16[256,256]{1,0:T(8,128)(2,1)S(1)} %collective-permute-done.21.refs_2_), channel_id=1, source_target_pairs={{0,1},{1,0},{2,3},{3,2},{4,5},{5,4},{6,7},{7,6},{8,9},{9,8},{10,11... | collective-permute-start | bytes 393224 | tf_op jit(solution)/shard_map/ppermute | solution.py:255
  76.7 1.5 %collective-permute-start.26 = (bf16[256,256]{1,0:T(8,128)(2,1)S(1)}, bf16[256,256]{1,0:T(8,128)(2,1)S(1)}, u32[]{:S(2)}, u32[]{:S(2)}) collective-permute-start(bf16[256,256]{1,0:T(8,128)(2,1)S(1)} %collective-permute-done.22.refs_3_), channel_id=1, source_target_pairs={{0,1},{1,0},{2,3},{3,2},{4,5},{5,4},{6,7},{7,6},{8,9},{9,8},{10,11... | collective-permute-start | bytes 393224 | tf_op jit(solution)/shard_map/ppermute | solution.py:255
